TPU v7x, 512 devices: a whole 4x8x8 slice. The times are simulated.
512 devices in a mesh: server: 32 (over x, z), worker: 16 (over y, core).
Axes of the slice: x: 4, y: 8, z: 8, core: 2. Of those that a mesh axis runs over, the one named last changes fastest.
Arguments:
- factors: float32 [16384, 256], P('server'), may hold values from -0.3 to 0.3
- linear: float32 [16384], P('server'), may hold values from -0.6 to 0.6
- acc_factors: float32 [16384, 256], P(('server', 'worker')), may hold values from 0.5 to 20
- acc_linear: float32 [16384], P(('server', 'worker')), may hold values from 10 to 300
- feature_slot: int32 [131072, 39], P(('server', 'worker')), may hold values from 0 to 511, as said below
- requests: int32 [16384, 16], P(('server', 'worker')), may hold values from 0 to 511, as said below
- clicks: int32 [131072], P(('server', 'worker')), may hold values from 0 to 1
Outputs:
- new_factors: float32 [16384, 256], P('server')
- new_linear: float32 [16384], P('server')
- new_acc_factors: float32 [16384, 256], P(('server', 'worker'))
- new_acc_linear: float32 [16384], P(('server', 'worker'))
Inputs may be any that keep to these rules, and one draw needn't show every extreme that they name: Within each device's list for one owner, the first entries (its live requests, at most 16) are distinct and increasing, the rest are 0. The owner that is fullest gets 16 live requests from every device, and owners' loads differ. `feature_slot`: every feature of a sample names a live slot of its device's request list: o * 16 + j with j below the number of live requests of that device to owner o.
All inputs are finite; a program needn't handle non-finite values.
Results may differ from a plain program's by a relative error of at most 0.006.
Values may be sent and summed in bfloat16 or wider, within the bound.
No kernel may reach another device: no remote copies, remote signals or barrier semaphores. Data moves between devices by JAX's collectives and lax.ppermute only.
A program may use at most 64 MiB of HBM per device.

v0:
```python
import jax
import jax.numpy as jnp
from jax import lax
from jax.sharding import PartitionSpec as P

step_size = 0.5


def body(factors, linear, acc_factors, acc_linear, feature_slot, requests, clicks):
    servers = lax.axis_size("server")
    slot_cap = requests.shape[1]
    row_width = factors.shape[1]
    buffer_rows = servers * slot_cap
    owner_rows = factors.shape[0]
    asked_rows = lax.all_to_all(requests, "server", split_axis=0, concat_axis=0, tiled=True)
    found_rows = factors[asked_rows].astype(jnp.bfloat16)
    found_linear = linear[asked_rows].astype(jnp.bfloat16)
    got_rows = lax.all_to_all(found_rows, "server", split_axis=0, concat_axis=0, tiled=True)
    got_linear = lax.all_to_all(found_linear, "server", split_axis=0, concat_axis=0, tiled=True)
    vectors = got_rows.reshape(buffer_rows, row_width)
    linear_weights = got_linear.reshape(buffer_rows).astype(jnp.float32)
    slot_numbers = jnp.arange(buffer_rows, dtype=jnp.int32)
    counts = jnp.sum(
        (feature_slot[:, :, None] == slot_numbers[None, None, :]).astype(jnp.bfloat16),
        axis=1,
        dtype=jnp.bfloat16,
    )
    count_values = counts.astype(jnp.float32)
    factor_sums = jnp.dot(counts, vectors, preferred_element_type=jnp.float32)
    row_norms = jnp.sum(jnp.square(vectors.astype(jnp.float32)), axis=1)
    slot_table = jnp.stack([row_norms, linear_weights], axis=1)
    sample_terms = jnp.dot(count_values, slot_table, precision=lax.Precision.HIGHEST)
    squares = sample_terms[:, 0]
    linear_part = sample_terms[:, 1]
    logits = linear_part + 0.5 * (jnp.sum(factor_sums * factor_sums, axis=1) - squares)
    errors = jax.nn.sigmoid(logits) - clicks.astype(jnp.float32)
    weighted = (errors[:, None] * factor_sums).astype(jnp.bfloat16)
    gathered_terms = lax.dot_general(
        counts, weighted, (((0,), (0,)), ((), ())), preferred_element_type=jnp.float32
    )
    error_sums = jnp.dot(errors, count_values, precision=lax.Precision.HIGHEST)
    row_grads = gathered_terms - error_sums[:, None] * vectors.astype(jnp.float32)
    pushed_rows, pushed_linear = (
        lax.all_to_all(
            row_grads.reshape(servers, slot_cap, row_width),
            "server",
            split_axis=0,
            concat_axis=0,
            tiled=True,
        ),
        lax.all_to_all(
            error_sums.reshape(servers, slot_cap), "server", split_axis=0, concat_axis=0, tiled=True
        ),
    )
    flat_index = asked_rows.reshape(-1)
    dense_rows = (
        jnp.zeros((owner_rows, row_width), jnp.float32)
        .at[flat_index]
        .add(pushed_rows.reshape(-1, row_width))
    )
    dense_linear = (
        jnp.zeros((owner_rows,), jnp.float32).at[flat_index].add(pushed_linear.reshape(-1))
    )
    share_rows = acc_factors.shape[0]
    start_row = lax.axis_index("worker") * share_rows
    total_rows, total_linear = lax.psum((dense_rows, dense_linear), "worker")
    state_rows, state_linear = (
        lax.all_gather(acc_factors.astype(jnp.bfloat16), "worker", axis=0, tiled=True).astype(
            acc_factors.dtype
        ),
        lax.all_gather(acc_linear.astype(jnp.bfloat16), "worker", axis=0, tiled=True).astype(
            acc_linear.dtype
        ),
    )
    state_rows = state_rows + total_rows * total_rows
    state_linear = state_linear + total_linear * total_linear
    new_factors = factors - step_size * total_rows / jnp.sqrt(state_rows)
    new_linear = linear - step_size * total_linear / jnp.sqrt(state_linear)
    new_acc_rows = lax.dynamic_slice_in_dim(state_rows, start_row, share_rows, 0)
    new_acc_linear = lax.dynamic_slice_in_dim(state_linear, start_row, share_rows, 0)
    return (new_factors, new_linear, new_acc_rows, new_acc_linear)


def solution(mesh):
    in_specs = (
        P("server", None),
        P("server"),
        P(("server", "worker"), None),
        P(("server", "worker")),
        P(("server", "worker"), None),
        P(("server", "worker"), None),
        P(("server", "worker")),
    )
    out_specs = (
        P("server", None),
        P("server"),
        P(("server", "worker"), None),
        P(("server", "worker")),
    )
    return jax.shard_map(body, mesh=mesh, in_specs=in_specs, out_specs=out_specs, check_vma=False)
```

profile of v0, /device:TPU:1, one launch (start us, length us, event | category | flops | bytes accessed | tf_op | source)
XLA Modules:
  0.0 220.3 jit_solution(6730099871547125526)
XLA Ops:
  7.2 0.8 copy.19
  8.0 22.1 %all_to_all.37 = s32[32,1,16]{2,1,0:T(1,128)S(1)} all-to-all(s32[32,1,16]{2,1,0:T(1,128)S(1)} %bitcast.25), channel_id=1, replica_groups=mesh['server'=32,'worker'=16] {'server'}, dimensions={0} | all-to-all | bytes 4096 | tf_op jit(solution)/shard_map/all_to_all | solution.py:15
  30.2 3.5 %gather_fusion.1 = bf16[512]{0:T(512)(128)(2,1)S(1)} fusion(f32[512]{0:T(512)S(1)} %copy-done, s32[1024]{0:T(1024)S(1)} %pad_clamp_fusion), kind=kCustom, calls=%fused_computation.1 | custom fusion | bytes 4096 | tf_op jit(solution)/shard_map/gather | solution.py:17
  33.7 0.7 convert_element_type.75
  34.4 3.8 %all-to-all-start.2 = ((bf16[32,1,16]{2,1,0:T(2,128)(2,1)}), bf16[32,1,16]{2,1,0:T(2,128)(2,1)S(1)}, u32[]{:S(2)}, u32[]{:S(2)}) async-start(bf16[32,1,16]{2,1,0:T(2,128)(2,1)} %convert_element_type.75), calls=%async_computation.2 | async-start | bytes 32768 | tf_op jit(solution)/shard_map/all_to_all | solution.py:19
  38.3 2.2 gather_fusion
  40.5 6.4 %all-to-all-done.2 = bf16[32,1,16]{2,1,0:T(2,128)(2,1)S(1)} async-done(((bf16[32,1,16]{2,1,0:T(2,128)(2,1)}), bf16[32,1,16]{2,1,0:T(2,128)(2,1)S(1)}, u32[]{:S(2)}, u32[]{:S(2)}) %all-to-all-start.2) | async-done | bytes 1056 | tf_op jit(solution)/shard_map/all_to_all | solution.py:19
  46.8 3.9 %all-to-all-start.1 = ((bf16[32,16,256]{2,1,0:T(8,128)(2,1)}), bf16[32,16,256]{2,1,0:T(8,128)(2,1)S(1)}, u32[]{:S(2)}, u32[]{:S(2)}) async-start(bf16[32,16,256]{2,1,0:T(8,128)(2,1)} %bitcast.3), calls=%async_computation.1 | async-start | bytes 524288 | tf_op jit(solution)/shard_map/all_to_all | solution.py:18
  50.7 2.6 %fusion.1 = bf16[256,512]{1,0:T(8,128)(2,1)S(1)} fusion(s32[256,39]{0,1:T(8,128)S(1)} %copy-done.2), kind=kLoop, calls=%fused_computation.6 | loop fusion | flops 15204352 | bytes 302080 | tf_op jit(solution)/shard_map/reduce_sum | solution.py:23
  53.5 7.1 %all-to-all-done.1 = bf16[32,16,256]{2,1,0:T(8,128)(2,1)S(1)} async-done(((bf16[32,16,256]{2,1,0:T(8,128)(2,1)}), bf16[32,16,256]{2,1,0:T(8,128)(2,1)S(1)}, u32[]{:S(2)}, u32[]{:S(2)}) %all-to-all-start.1) | async-done | bytes 262176 | tf_op jit(solution)/shard_map/all_to_all | solution.py:18
  60.8 0.3 fusion.5
  61.1 0.3 multiply_reduce_fusion.1
  61.7 1.1 convolution_subtract_fusion
  62.8 4.5 %all-to-all-start.3 = ((f32[32,16,256]{2,1,0:T(8,128)}), f32[32,16,256]{2,1,0:T(8,128)S(1)}, u32[]{:S(2)}, u32[]{:S(2)}) async-start(f32[32,16,256]{2,1,0:T(8,128)} %bitcast.9), calls=%async_computation.3 | async-start | bytes 1048576 | tf_op jit(solution)/shard_map/all_to_all | solution.py:44
  67.3 0.5 broadcast.72
  67.8 0.7 reduce.11
  68.6 0.7 all_to_all.30
  69.3 9.5 %all-to-all-done.3 = f32[32,16,256]{2,1,0:T(8,128)S(1)} async-done(((f32[32,16,256]{2,1,0:T(8,128)}), f32[32,16,256]{2,1,0:T(8,128)S(1)}, u32[]{:S(2)}, u32[]{:S(2)}) %all-to-all-start.3) | async-done | bytes 524320 | tf_op jit(solution)/shard_map/all_to_all | solution.py:44
  78.8 7.0 %all-to-all-start.4 = ((f32[32,1,16]{2,1,0:T(1,128)}), f32[32,1,16]{2,1,0:T(1,128)S(1)}, u32[]{:S(2)}, u32[]{:S(2)}) async-start(f32[32,1,16]{2,1,0:T(1,128)} %bitcast.11), calls=%async_computation.4 | async-start | bytes 32768 | tf_op jit(solution)/shard_map/all_to_all | solution.py:51
  85.8 4.1 %scatter_custom_fusion = f32[512,256]{1,0:T(8,128)} fusion(s32[512]{0:T(512)S(1)} %bitcast.31, f32[512,256]{1,0:T(8,128)S(1)} %bitcast.23, f32[]{:T(128)} %constant.8.clone.1), kind=kCustom, calls=%fused_computation.13 | custom fusion | flops 131072 | bytes 524292 | tf_op jit(solution)/shard_map/scatter-add | solution.py:59
  89.9 23.3 %all_gather.6 = bf16[512,256]{1,0:T(8,128)(2,1)S(1)} all-gather(bf16[32,256]{1,0:T(8,128)(2,1)S(1)} %convert_element_type.68), channel_id=1, replica_groups=mesh['server'=32,'worker'=16] {'worker'}, dimensions={0}, use_global_device_ids=true | all-gather | bytes 278528 | tf_op jit(solution)/shard_map/all_gather | solution.py:68
  113.2 1.3 dynamic-slice
  115.4 23.1 %all-reduce = bf16[512]{0:T(512)(128)(2,1)S(1)} all-reduce(bf16[512]{0:T(512)(128)(2,1)S(1)} %dynamic-update-slice), channel_id=1, replica_groups=mesh['server'=32,'worker'=16] {'worker'}, use_global_device_ids=true, to_apply=%add | all-reduce | flops 512 | bytes 2048
  138.4 0.5 broadcast.73
  138.9 0.7 reduce.12
  139.7 4.1 %scatter_custom_fusion.1 = f32[512]{0:T(512)S(1)} fusion(s32[512]{0:T(512)S(1)} %bitcast.32, f32[512]{0:T(512)S(1)} %reshape.150, f32[]{:T(128)} %constant.8.clone.1), kind=kCustom, calls=%fused_computation.27 | custom fusion | flops 512 | bytes 2052 | tf_op jit(solution)/shard_map/scatter-add | solution.py:62
  143.8 24.3 %psum.15 = f32[512]{0:T(512)S(1)} all-reduce(f32[512]{0:T(512)S(1)} %scatter_custom_fusion.1), channel_id=1, replica_groups=mesh['server'=32,'worker'=16] {'worker'}, use_global_device_ids=true, to_apply=%region_6.0 | all-reduce | flops 512 | bytes 4096 | tf_op jit(solution)/shard_map/psum | solution.py:66
  168.1 0.6 multiply_subtract_fusion.1
  168.7 0.6 dynamic_slice.7
  169.3 41.6 %all-reduce.3.cloned.1.call-done = f32[512,256]{1,0:T(8,128)} async-done(((f32[512,256]{1,0:T(8,128)}), f32[512,256]{1,0:T(8,128)}) %all-reduce.3.cloned.1.call-update) | async-done | bytes 524304 | tf_op jit(solution)/shard_map/psum | solution.py:66
  210.9 2.0 multiply_subtract_fusion
  212.9 0.6 constant_dynamic-slice_fusion
  (32 shorter events, 1.2 us)
Async XLA Ops:
  7.2 23.0 %copy-start = (f32[512]{0:T(512)S(1)}, f32[512]{0:T(512)}, u32[]{:S(2)}) copy-start(f32[512]{0:T(512)} %param.8) | copy-start | bytes 6148
  30.2 8.1 %copy-start.1 = (f32[512,256]{1,0:T(8,128)S(1)}, f32[512,256]{1,0:T(8,128)}, u32[]{:S(2)}) copy-start(f32[512,256]{1,0:T(8,128)} %param.7) | copy-start | bytes 1572868
  34.4 12.4 %all-to-all-start.2 = ((bf16[32,1,16]{2,1,0:T(2,128)(2,1)}), bf16[32,1,16]{2,1,0:T(2,128)(2,1)S(1)}, u32[]{:S(2)}, u32[]{:S(2)}) async-start(bf16[32,1,16]{2,1,0:T(2,128)(2,1)} %convert_element_type.75), calls=%async_computation.2 | async-start | bytes 32768 | tf_op jit(solution)/shard_map/all_to_all | solution.py:19
  40.5 10.2 %copy-start.2 = (s32[256,39]{0,1:T(8,128)S(1)}, s32[256,39]{0,1:T(8,128)}, u32[]{:S(2)}) copy-start(s32[256,39]{0,1:T(8,128)} %param.11) | copy-start | bytes 119812
  46.8 13.7 %all-to-all-start.1 = ((bf16[32,16,256]{2,1,0:T(8,128)(2,1)}), bf16[32,16,256]{2,1,0:T(8,128)(2,1)S(1)}, u32[]{:S(2)}, u32[]{:S(2)}) async-start(bf16[32,16,256]{2,1,0:T(8,128)(2,1)} %bitcast.3), calls=%async_computation.1 | async-start | bytes 524288 | tf_op jit(solution)/shard_map/all_to_all | solution.py:18
  60.8 0.7 copy-start.4
  62.8 4.5 %copy-start.3 = (f32[32,256]{1,0:T(8,128)S(1)}, f32[32,256]{1,0:T(8,128)}, u32[]{:S(2)}) copy-start(f32[32,256]{1,0:T(8,128)} %param.9) | copy-start | bytes 98308
  62.8 16.0 %all-to-all-start.3 = ((f32[32,16,256]{2,1,0:T(8,128)}), f32[32,16,256]{2,1,0:T(8,128)S(1)}, u32[]{:S(2)}, u32[]{:S(2)}) async-start(f32[32,16,256]{2,1,0:T(8,128)} %bitcast.9), calls=%async_computation.3 | async-start | bytes 1048576 | tf_op jit(solution)/shard_map/all_to_all | solution.py:44
  78.8 59.7 %all-to-all-start.4 = ((f32[32,1,16]{2,1,0:T(1,128)}), f32[32,1,16]{2,1,0:T(1,128)S(1)}, u32[]{:S(2)}, u32[]{:S(2)}) async-start(f32[32,1,16]{2,1,0:T(1,128)} %bitcast.11), calls=%async_computation.4 | async-start | bytes 32768 | tf_op jit(solution)/shard_map/all_to_all | solution.py:51
  85.7 125.1 %all-reduce.3.cloned.1.call-start = ((), (), s32[]{:S(2)}) async-start(), calls=%async_computation.5 | async-start | bytes 1048576 | tf_op jit(solution)/shard_map/psum | solution.py:66
  89.9 23.3 %copy-start.5 = (f32[32]{0:T(128)S(1)}, f32[32]{0:T(128)}, u32[]{:S(2)}) copy-start(f32[32]{0:T(128)} %param.10) | copy-start | bytes 388
Sparse Core Ops, SparseCore 0:
  90.0 120.7 all-reduce.2
where the time goes:
time: 221 us; the launch traced here: 220 us
  blocking collectives  92.8 us (42%)
  waiting for transfers between devices  64.5 us (29%)
  starting transfers between devices  19.2 us (9%)
  other arithmetic  15 us (7%)
  between operations  14.8 us (7%)
  local copies, waits for them, and re-layouts  12.1 us (5%)
    psum x1, waiting for transfers between devices, body(): total_rows, total_linear = lax.psum((dense_rows, dense_linear), 'worker')  41.6 us
    psum x1, blocking collectives, body(): total_rows, total_linear = lax.psum((dense_rows, dense_linear), 'worker')  24.3 us
    all_gather x1, blocking collectives, body(): lax.all_gather(acc_factors.astype(jnp.bfloat16), 'worker', axis=0, tiled=...  23.3 us
    unnamed x1, blocking collectives  23.1 us
    all_to_all x1, blocking collectives, body(): lax.all_to_all(requests, 'server', split_axis=0, concat_axis=0, tiled=True)  22.1 us
    all_to_all x1, waiting for transfers between devices, body(): lax.all_to_all(row_grads.reshape(servers, slot_cap, row_width), 'server',...  9.47 us
    all_to_all x1, waiting for transfers between devices, body(): lax.all_to_all(found_rows, 'server', split_axis=0, concat_axis=0, tiled=T...  7.07 us
    all_to_all x1, starting transfers between devices, body(): lax.all_to_all(error_sums.reshape(servers, slot_cap), 'server', split_axi...  6.96 us
  transfers between devices with their start and end apart: 5, of which 4 were waited for; matrix products, arithmetic and copies ran while one was open for 8% of the time, Pallas kernels for 0%

commit v1 on v0

v1 whole, which is shorter than its diff:
```python
import jax
import jax.numpy as jnp
from jax import lax
from jax.experimental import pallas as pl
from jax.experimental.pallas import tpu as pltpu
from jax.sharding import Mesh, PartitionSpec as P

step_size = 0.5
bf16 = jnp.bfloat16
f32 = jnp.float32

OWNERS = 32
CAP = 16
SLOTS = OWNERS * CAP
ROWS = 512
K = 256
WIDE = K + 128
SAMPLES = 256
FIELDS = 39
N_Y = 8
N_CORE = 2
N_WORKER = N_Y * N_CORE
SHARE = ROWS // N_WORKER


def iota(shape, axis):
    return lax.broadcasted_iota(jnp.int32, shape, axis)


def dot(a, b, ca=1, cb=0):
    return lax.dot_general(a, b, (((ca,), (cb,)), ((), ())), preferred_element_type=f32)


def parts(x, lanes):
    first = x.astype(bf16).astype(f32)
    rest = x - first
    second = rest.astype(bf16).astype(f32)
    third = rest - second
    out = jnp.where(lanes == 0, first, jnp.where(lanes == 1, second, jnp.where(lanes == 2, third, 0.0)))
    return out.astype(bf16)


def split_requests(req_t):
    high = jnp.bitwise_and(req_t, -16)
    low = jnp.bitwise_and(req_t, 15)
    pad = jnp.zeros((96, OWNERS), jnp.int32)
    return jnp.concatenate([high, low, pad], axis=0).astype(f32).astype(bf16)


def pick_slot(a, slot_axis):
    place_axis = 1 - slot_axis
    place = iota(a.shape, place_axis)
    position = jnp.bitwise_and(iota(a.shape, slot_axis), CAP - 1)
    keep = (place < 2 * CAP) & (jnp.bitwise_and(place, CAP - 1) == position)
    return jnp.sum(jnp.where(keep, a, 0.0), axis=place_axis, keepdims=True)


def ask_kernel(req_t_ref, lin_ref, out_ref):
    lists = split_requests(req_t_ref[...])
    block = jnp.right_shift(iota((8 * OWNERS, OWNERS), 0), 3)
    sub = jnp.bitwise_and(iota((8 * OWNERS, OWNERS), 0), 7)
    to_owner = (block == iota((8 * OWNERS, OWNERS), 1)) & (sub == 4)
    lin = lin_ref[...].astype(bf16)
    sub4 = jnp.bitwise_and(iota((8 * OWNERS, 4), 0), 7)
    spread = sub4 == iota((8 * OWNERS, 4), 1)
    out = dot(to_owner.astype(f32).astype(bf16), lists, 1, 1) + dot(spread.astype(f32).astype(bf16), lin)
    out_ref[...] = out.reshape(OWNERS, 8, 128)


def count_kernel(fs_t_ref, clicks_ref, counts_t_ref, counts_ref, clicks_col_ref):
    chunk = 64

    def one(i, carry):
        base = pl.multiple_of(i * chunk, chunk)
        slots = iota((chunk, SAMPLES), 0) + base
        total = jnp.zeros((chunk, SAMPLES), f32)
        for f in range(FIELDS):
            total = total + jnp.where(fs_t_ref[pl.ds(f, 1), :] == slots, 1.0, 0.0)
        counts_t_ref[pl.ds(base, chunk), :] = total.astype(bf16)
        return carry

    lax.fori_loop(0, SLOTS // chunk, one, 0)
    counts_ref[...] = jnp.transpose(counts_t_ref[...].astype(f32)).astype(bf16)
    same = iota((SAMPLES, SAMPLES), 0) == iota((SAMPLES, SAMPLES), 1)
    clicks = clicks_ref[...].astype(f32)
    clicks_col_ref[...] = jnp.sum(jnp.where(same, clicks, 0.0), axis=1, keepdims=True)


def asked_rows_matrix(got):
    owner = jnp.right_shift(iota((SLOTS, 8 * OWNERS), 0), 4)
    pick = (owner * 8 + 4 == iota((SLOTS, 8 * OWNERS), 1)).astype(f32).astype(bf16)
    return pick_slot(dot(pick, got), 0)


def gather_kernel(got_ref, factors_ref, out_ref):
    got = got_ref[...].reshape(8 * OWNERS, 128).astype(bf16)
    asked = asked_rows_matrix(got)
    hot = (asked == iota((SLOTS, ROWS), 1).astype(f32)).astype(f32).astype(bf16)
    found = dot(hot, factors_ref[...].astype(bf16))
    out_ref[...] = found.astype(bf16).reshape(OWNERS, CAP, K)


def side_kernel(got_ref, req_t_ref, lin_ref, hot_t_ref):
    got = got_ref[...].reshape(8 * OWNERS, 128).astype(bf16)
    lists = split_requests(req_t_ref[...])
    owner = jnp.right_shift(iota((SLOTS, OWNERS), 0), 4)
    mine = (owner == iota((SLOTS, OWNERS), 1)).astype(f32).astype(bf16)
    wanted = pick_slot(dot(mine, lists, 1, 1), 0)
    block = jnp.right_shift(iota((SLOTS, 8 * OWNERS), 0), 4) * 8
    column = iota((SLOTS, 8 * OWNERS), 1)
    lanes = iota((SLOTS, 128), 1).astype(f32)
    total = jnp.zeros((SLOTS, 128), f32)
    for k in range(4):
        pick = (block + k == column).astype(f32).astype(bf16)
        values = dot(pick, got)
        total = total + jnp.where(wanted == lanes + 128.0 * k, values, 0.0)
    lin_ref[...] = jnp.sum(total, axis=1, keepdims=True)
    owner_t = jnp.right_shift(iota((8 * OWNERS, SLOTS), 1), 4)
    pick_t = (owner_t * 8 + 4 == iota((8 * OWNERS, SLOTS), 0)).astype(f32).astype(bf16)
    asked_t = pick_slot(dot(got, pick_t, 0, 0), 1)
    hot_t_ref[...] = (asked_t == iota((ROWS, SLOTS), 0).astype(f32)).astype(f32).astype(bf16)


def learn_kernel(rows_ref, counts_ref, counts_t_ref, clicks_ref, lin_ref, out_ref):
    rows = rows_ref[...].reshape(SLOTS, K)
    wide_rows = rows.astype(f32)
    counts = counts_ref[...]
    sums = dot(counts, rows)
    norms = jnp.sum(wide_rows * wide_rows, axis=1, keepdims=True)
    lanes = iota((SLOTS, 128), 1)
    terms = parts(lin_ref[...] - 0.5 * norms, lanes)
    base = jnp.sum(dot(counts, terms), axis=1, keepdims=True)
    logits = base + 0.5 * jnp.sum(sums * sums, axis=1, keepdims=True)
    errors = jax.nn.sigmoid(logits) - clicks_ref[...]
    weighted = (errors * sums).astype(bf16)
    error_parts = parts(errors, iota((SAMPLES, 128), 1))
    counts_t = counts_t_ref[...]
    gathered = dot(counts_t, weighted)
    error_sums = jnp.sum(dot(counts_t, error_parts), axis=1, keepdims=True)
    grads = gathered - error_sums * wide_rows
    out_ref[:, :, :K] = grads.astype(bf16).reshape(OWNERS, CAP, K)
    out_ref[:, :, K:] = parts(error_sums, lanes).reshape(OWNERS, CAP, 128)


def scatter_kernel(push_ref, hot_t_ref, out_ref):
    pushed = push_ref[...].reshape(SLOTS, WIDE)
    total = dot(hot_t_ref[...], pushed)
    linear = jnp.sum(total[:, K:], axis=1, keepdims=True)
    out_ref[:, :, :K] = total[:, :K].astype(bf16).reshape(N_WORKER, SHARE, K)
    out_ref[:, :, K:] = parts(linear, iota((ROWS, 128), 1)).reshape(N_WORKER, SHARE, 128)


def update_kernel(part_ref, acc_ref, acc_lin_ref, delta_ref, new_acc_ref, new_acc_lin_ref):
    total = part_ref[0].astype(f32)
    for w in range(1, N_WORKER):
        total = total + part_ref[w].astype(f32)
    grad = total[:, :K]
    grad_lin = jnp.sum(total[:, K:], axis=1, keepdims=True)
    state = acc_ref[...] + grad * grad
    new_acc_ref[...] = state
    delta = (step_size * grad / jnp.sqrt(state)).astype(bf16)
    same = iota((SHARE, SHARE), 0) == iota((SHARE, SHARE), 1)
    acc_lin = jnp.sum(jnp.where(same, acc_lin_ref[...], 0.0), axis=1, keepdims=True)
    state_lin = acc_lin + grad_lin * grad_lin
    new_acc_lin_ref[...] = jnp.sum(jnp.where(same, state_lin, 0.0), axis=0, keepdims=True)
    delta_lin = parts(step_size * grad_lin / jnp.sqrt(state_lin), iota((SHARE, 128), 1))
    for y in range(N_Y):
        delta_ref[y, :, :K] = delta
        delta_ref[y, :, K:] = delta_lin


def apply_kernel(delta_ref, factors_ref, linear_ref, new_factors_ref, new_linear_ref):
    lin = jnp.zeros((1, ROWS), f32)
    place = iota((SHARE, ROWS), 1) - iota((SHARE, ROWS), 0)
    for y in range(N_Y):
        for c in range(N_CORE):
            first = (y * N_CORE + c) * SHARE
            block = delta_ref[c * N_Y + y]
            here = pl.ds(first, SHARE)
            new_factors_ref[here, :] = factors_ref[here, :] - block[:, :K].astype(f32)
            step = jnp.sum(block[:, K:].astype(f32), axis=1, keepdims=True)
            lin = lin + jnp.sum(jnp.where(place == first, step, 0.0), axis=0, keepdims=True)
    new_linear_ref[...] = linear_ref[...] - lin


def call(kernel, out, flops, *args):
    size = sum(a.size * a.dtype.itemsize for a in args)
    return pl.pallas_call(
        kernel,
        out_shape=out,
        in_specs=[pl.BlockSpec(memory_space=pltpu.VMEM)] * len(args),
        out_specs=jax.tree.map(lambda _: pl.BlockSpec(memory_space=pltpu.VMEM), out),
        compiler_params=pltpu.CompilerParams(vmem_limit_bytes=24 * 1024 * 1024),
        cost_estimate=pl.CostEstimate(flops=flops, bytes_accessed=size, transcendentals=0),
    )(*args)


def shape(dims, dtype):
    return jax.ShapeDtypeStruct(dims, dtype)


def exchange(x, axis):
    return lax.all_to_all(x, axis, split_axis=0, concat_axis=0, tiled=True)


def body(factors, linear, acc_factors, acc_linear, feature_slot, requests, clicks):
    req_t = requests.T
    ask = call(ask_kernel, shape((OWNERS, 8, 128), f32), 1 << 20, req_t, linear.reshape(4, 128))
    got = exchange(ask, "server")
    counts_t, counts, clicks_col = call(
        count_kernel,
        [shape((SLOTS, SAMPLES), bf16), shape((SAMPLES, SLOTS), bf16), shape((SAMPLES, 1), f32)],
        1 << 30,
        feature_slot.T,
        clicks.reshape(1, SAMPLES),
    )
    found = call(gather_kernel, shape((OWNERS, CAP, K), bf16), 1 << 28, got, factors)
    rows = exchange(found, "server")
    lin_col, hot_t = call(
        side_kernel, [shape((SLOTS, 1), f32), shape((ROWS, SLOTS), bf16)], 1 << 28, got, req_t
    )
    push = call(
        learn_kernel,
        shape((OWNERS, CAP, WIDE), bf16),
        1 << 28,
        rows,
        counts,
        counts_t,
        clicks_col,
        lin_col,
    )
    pushed = exchange(push, "server")
    dense = call(scatter_kernel, shape((N_WORKER, SHARE, WIDE), bf16), 1 << 28, pushed, hot_t)
    shared = exchange(dense, ("y", "core"))
    delta, new_acc, new_acc_lin = call(
        update_kernel,
        [shape((N_Y, SHARE, WIDE), bf16), shape((SHARE, K), f32), shape((1, SHARE), f32)],
        1 << 20,
        shared,
        acc_factors,
        acc_linear.reshape(1, SHARE),
    )
    deltas = exchange(delta, "y")
    deltas = lax.all_gather(deltas, "core", axis=0, tiled=True)
    new_factors, new_linear = call(
        apply_kernel,
        [shape((ROWS, K), f32), shape((1, ROWS), f32)],
        1 << 20,
        deltas,
        factors,
        linear.reshape(1, ROWS),
    )
    return new_factors, new_linear.reshape(ROWS), new_acc, new_acc_lin.reshape(SHARE)


def solution(mesh):
    mesh = Mesh(mesh.devices.reshape(OWNERS, N_Y, N_CORE), ("server", "y", "core"))
    every = ("server", "y", "core")
    in_specs = (
        P("server", None),
        P("server"),
        P(every, None),
        P(every),
        P(every, None),
        P(every, None),
        P(every),
    )
    out_specs = (P("server", None), P("server"), P(every, None), P(every))
    return jax.shard_map(body, mesh=mesh, in_specs=in_specs, out_specs=out_specs, check_vma=False)
```

time: 221 us -> 103 us (0.47)
  waiting for transfers between devices: 64.5 us -> 6.01 us
  starting transfers between devices: 19.2 us -> 4 us
  other arithmetic: 15 us -> 0 us
  between operations: 14.8 us -> 0.72 us
  blocking collectives: 92.8 us -> 80.6 us
  local copies, waits for them, and re-layouts: 12.1 us -> 3.75 us
  Pallas kernels: 0 us -> 7.64 us
    all_to_all x1 -> x4, blocking collectives: 22.1 us -> 78.3 us  [exchange(): return lax.all_to_all(x, axis, split_axis=0, concat_axis=0, tiled=True)]
    psum x1 -> x0, waiting for transfers between devices: 41.6 us -> none  [body(): total_rows, total_linear = lax.psum((dense_rows, dense_linear), 'worker')]
    psum x1 -> x0, blocking collectives: 24.3 us -> none  [body(): total_rows, total_linear = lax.psum((dense_rows, dense_linear), 'worker')]
    unnamed x1 -> x0, blocking collectives: 23.1 us -> none
    all_gather x1, blocking collectives: 23.3 us -> 2.27 us  [body(): deltas = lax.all_gather(deltas, 'core', axis=0, tiled=True)]
    all_to_all x4 -> x1, waiting for transfers between devices: 22.9 us -> 6.01 us  [exchange(): return lax.all_to_all(x, axis, split_axis=0, concat_axis=0, tiled=True)]
    all_to_all x4 -> x1, starting transfers between devices: 19.2 us -> 4 us  [exchange(): return lax.all_to_all(x, axis, split_axis=0, concat_axis=0, tiled=True)]
    scatter-add x2 -> x0, other arithmetic: 8.19 us -> none  [the longest x1 4.11 us: body(): dense_rows = jnp.zeros((owner_rows, row_width), jnp.float32).at[flat_inde...]
  transfers between devices with their start and end apart: 5 -> 1, of which waited for: 4 -> 1; matrix products, arithmetic and copies ran while one was open for 8% -> 0% of each run, Pallas kernels for 0% -> 3%
where the time goes in v1:
time: 103 us
  blocking collectives  80.6 us (78%)
  Pallas kernels  7.64 us (7%)
  waiting for transfers between devices  6.01 us (6%)
  starting transfers between devices  4 us (4%)
  local copies, waits for them, and re-layouts  3.75 us (4%)
    all_to_all x4, blocking collectives, exchange(): return lax.all_to_all(x, axis, split_axis=0, concat_axis=0, tiled=True)  78.3 us
    pallas_call x8, Pallas kernels, call(): pl.pallas_call(kernel, out_shape=out, in_specs=[pl.BlockSpec(memory_space...  7.64 us
    all_to_all x1, waiting for transfers between devices, exchange(): return lax.all_to_all(x, axis, split_axis=0, concat_axis=0, tiled=True)  6.01 us
    all_to_all x1, starting transfers between devices, exchange(): return lax.all_to_all(x, axis, split_axis=0, concat_axis=0, tiled=True)  4 us
    unnamed x18, local copies, waits for them, and re-layouts  3.75 us
    all_gather x1, blocking collectives, body(): deltas = lax.all_gather(deltas, 'core', axis=0, tiled=True)  2.27 us
  transfers between devices with their start and end apart: 1, of which 1 were waited for; matrix products, arithmetic and copies ran while one was open for 0% of the time, Pallas kernels for 3%

profile of v1, /device:TPU:1, one launch (start us, length us, event | category | flops | bytes accessed | tf_op | source)
XLA Modules:
  0.0 102.7 jit_solution(11164594196633860150)
XLA Ops:
  0.6 0.0 copy-start.3
  0.6 0.7 copy-done.3
  1.3 0.0 copy-start.4
  1.3 0.7 copy-done.4
  2.0 0.2 shard_map.102
  2.2 22.7 %all_to_all.25.got_ref = f32[32,8,128]{2,1,0:T(8,128)S(1)} all-to-all(f32[32,8,128]{2,1,0:T(8,128)S(1)} %shard_map.102), channel_id=1, replica_groups=mesh['server'=32,'y'=8,'core'=2] {'server'}, dimensions={0} | all-to-all | bytes 262144 | tf_op jit(solution)/shard_map/all_to_all | solution.py:203
  24.9 0.0 copy-start
  24.9 1.0 %copy-done = f32[512,256]{1,0:T(8,128)S(1)} copy-done((f32[512,256]{1,0:T(8,128)S(1)}, f32[512,256]{1,0:T(8,128)}, u32[]{:S(2)}) %copy-start) | copy-done | bytes 524312
  25.9 1.3 %shard_map.103 = bf16[32,16,256]{2,1,0:T(8,128)(2,1)} custom-call(f32[32,8,128]{2,1,0:T(8,128)S(1)} %all_to_all.25.got_ref, f32[512,256]{1,0:T(8,128)S(1)} %copy-done), custom_call_target="tpu_custom_call" | custom-call | flops 268435456 | bytes 655360 | tf_op jit(solution)/shard_map/pallas_call | solution.py:188
  27.2 0.0 copy-start.7
  27.2 4.0 %all-to-all-start.1 = ((bf16[32,16,256]{2,1,0:T(8,128)(2,1)}), bf16[32,16,256]{2,1,0:T(8,128)(2,1)S(1)}, u32[]{:S(2)}, u32[]{:S(2)}) async-start(bf16[32,16,256]{2,1,0:T(8,128)(2,1)} %shard_map.103), calls=%async_computation.1 | async-start | bytes 524288 | tf_op jit(solution)/shard_map/all_to_all | solution.py:203
  31.2 0.0 copy-start.8
  31.2 0.0 copy-done.7
  31.3 0.7 copy-done.8
  31.9 0.0 copy-start.5
  31.9 2.3 %shard_map.104 = (bf16[512,256]{1,0:T(8,128)(2,1)S(1)}, bf16[256,512]{1,0:T(8,128)(2,1)S(1)}, f32[256,1]{1,0:T(8,128)S(1)}) custom-call(s32[39,256]{1,0:T(8,128)S(1)} %bitcast.13, s32[1,256]{1,0:T(1,128)S(1)} %bitcast.14), custom_call_target="tpu_custom_call" | custom-call | flops 1073741824 | bytes 40960 | tf_op jit(solution)/shard_map/pallas_call | solution.py:188
  34.2 0.0 copy-done.5
  34.2 0.7 shard_map.105
  34.9 6.0 %all-to-all-done.1.rows_ref = bf16[32,16,256]{2,1,0:T(8,128)(2,1)S(1)} async-done(((bf16[32,16,256]{2,1,0:T(8,128)(2,1)}), bf16[32,16,256]{2,1,0:T(8,128)(2,1)S(1)}, u32[]{:S(2)}, u32[]{:S(2)}) %all-to-all-start.1) | async-done | bytes 262176 | tf_op jit(solution)/shard_map/all_to_all | solution.py:203
  40.9 1.1 %shard_map.106 = bf16[32,16,384]{2,1,0:T(8,128)(2,1)S(1)} custom-call(bf16[32,16,256]{2,1,0:T(8,128)(2,1)S(1)} %all-to-all-done.1.rows_ref, bf16[256,512]{1,0:T(8,128)(2,1)S(1)} %get-tuple-element.14.counts_ref, bf16[512,256]{1,0:T(8,128)(2,1)S(1)} %get-tuple-element.15.counts_t_ref, f32[256,1]{1,0:T(8,128)S(1)} %get-tuple-element.16.clicks_ref, ...), custom_call_target="tpu_custom_call" | custom-call | flops 268435456 | bytes 789504 | tf_op jit(solution)/shard_map/pallas_call | solution.py:188
  42.0 15.2 %all_to_all.26.push_ref = bf16[32,16,384]{2,1,0:T(8,128)(2,1)S(1)} all-to-all(bf16[32,16,384]{2,1,0:T(8,128)(2,1)S(1)} %shard_map.106), channel_id=1, replica_groups=mesh['server'=32,'y'=8,'core'=2] {'server'}, dimensions={0} | all-to-all | bytes 786432 | tf_op jit(solution)/shard_map/all_to_all | solution.py:203
  57.2 0.5 shard_map.107
  57.7 0.0 copy-start.2
  57.7 27.0 %all_to_all.27.part_ref = bf16[16,32,384]{2,1,0:T(8,128)(2,1)S(1)} all-to-all(bf16[16,32,384]{2,1,0:T(8,128)(2,1)S(1)} %shard_map.107), channel_id=1, replica_groups=mesh['server'=32,'y'=8,'core'=2] {'y','core'}, dimensions={0} | all-to-all | bytes 786432 | tf_op jit(solution)/shard_map/all_to_all | solution.py:203
  84.7 0.0 copy-start.6
  84.7 0.0 copy-done.2
  84.7 0.7 copy-done.6
  85.4 0.7 shard_map.108
  86.1 13.4 %all_to_all.28 = bf16[8,32,384]{2,1,0:T(8,128)(2,1)S(1)} all-to-all(bf16[8,32,384]{2,1,0:T(8,128)(2,1)S(1)} %get-tuple-element.19), channel_id=1, replica_groups=mesh['server'=32,'y'=8,'core'=2] {'y'}, dimensions={0} | all-to-all | bytes 393216 | tf_op jit(solution)/shard_map/all_to_all | solution.py:203
  99.5 2.3 %all_gather.3.delta_ref = bf16[16,32,384]{2,1,0:T(8,128)(2,1)S(1)} all-gather(bf16[8,32,384]{2,1,0:T(8,128)(2,1)S(1)} %all_to_all.28), channel_id=1, replica_groups=mesh['server'=32,'y'=8,'core'=2] {'core'}, dimensions={0}, use_global_device_ids=true | all-gather | bytes 589824 | tf_op jit(solution)/shard_map/all_gather | solution.py:244
  101.7 0.0 copy-done.1
  101.7 0.9 shard_map.109
  (1 shorter events, 0.0 us)
Async XLA Ops:
  0.6 0.7 copy-start.3
  1.3 0.7 copy-start.4
  24.9 1.0 %copy-start = (f32[512,256]{1,0:T(8,128)S(1)}, f32[512,256]{1,0:T(8,128)}, u32[]{:S(2)}) copy-start(f32[512,256]{1,0:T(8,128)} %factors_ref.3) | copy-start | bytes 1572868
  27.2 4.0 %copy-start.7 = (s32[256,39]{0,1:T(8,128)S(1)}, s32[256,39]{0,1:T(8,128)}, u32[]{:S(2)}) copy-start(s32[256,39]{0,1:T(8,128)} %param.11) | copy-start | bytes 119812
  27.2 13.7 %all-to-all-start.1 = ((bf16[32,16,256]{2,1,0:T(8,128)(2,1)}), bf16[32,16,256]{2,1,0:T(8,128)(2,1)S(1)}, u32[]{:S(2)}, u32[]{:S(2)}) async-start(bf16[32,16,256]{2,1,0:T(8,128)(2,1)} %shard_map.103), calls=%async_computation.1 | async-start | bytes 524288 | tf_op jit(solution)/shard_map/all_to_all | solution.py:203
  31.2 0.7 copy-start.8
  31.9 2.3 %copy-start.5 = (s32[32,16]{0,1:T(8,128)S(1)}, s32[32,16]{0,1:T(8,128)}, u32[]{:S(2)}) copy-start(s32[32,16]{0,1:T(8,128)} %param.12) | copy-start | bytes 6148
  57.7 27.0 %copy-start.2 = (f32[32,256]{1,0:T(8,128)S(1)}, f32[32,256]{1,0:T(8,128)}, u32[]{:S(2)}) copy-start(f32[32,256]{1,0:T(8,128)} %acc_ref.1) | copy-start | bytes 98308
  84.7 0.7 copy-start.6
  86.1 15.7 %copy-start.1 = (f32[512,256]{1,0:T(8,128)S(1)}, f32[512,256]{1,0:T(8,128)}, u32[]{:S(2)}) copy-start(f32[512,256]{1,0:T(8,128)} %factors_ref.3) | copy-start | bytes 1572868

commit v2 on v1

--- a/solution.py
+++ b/solution.py
@@ -55,19 +55,55 @@
     return jnp.sum(jnp.where(keep, a, 0.0), axis=place_axis, keepdims=True)
 
 
-def ask_kernel(req_t_ref, lin_ref, out_ref):
-    lists = split_requests(req_t_ref[...])
+def ask_kernel(req_t_hbm, lin_hbm, out_ref, req_t_ref, lin_ref, sems):
+    copies = [
+        pltpu.make_async_copy(req_t_hbm, req_t_ref, sems.at[0]),
+        pltpu.make_async_copy(lin_hbm, lin_ref, sems.at[1]),
+    ]
+    for copy in copies:
+        copy.start()
     block = jnp.right_shift(iota((8 * OWNERS, OWNERS), 0), 3)
     sub = jnp.bitwise_and(iota((8 * OWNERS, OWNERS), 0), 7)
     to_owner = (block == iota((8 * OWNERS, OWNERS), 1)) & (sub == 4)
-    lin = lin_ref[...].astype(bf16)
     sub4 = jnp.bitwise_and(iota((8 * OWNERS, 4), 0), 7)
     spread = sub4 == iota((8 * OWNERS, 4), 1)
+    for copy in copies:
+        copy.wait()
+    lists = split_requests(req_t_ref[...])
+    lin = lin_ref[...].astype(bf16)
     out = dot(to_owner.astype(f32).astype(bf16), lists, 1, 1) + dot(spread.astype(f32).astype(bf16), lin)
     out_ref[...] = out.reshape(OWNERS, 8, 128)
 
 
-def count_kernel(fs_t_ref, clicks_ref, counts_t_ref, counts_ref, clicks_col_ref):
+def prep_kernel(
+    fs_t_ref,
+    clicks_ref,
+    req_t_in,
+    factors_in,
+    acc_in,
+    acc_lin_row_ref,
+    linear_in,
+    counts_t_ref,
+    counts_ref,
+    clicks_col_ref,
+    req_t_ref,
+    factors_ref,
+    narrow_ref,
+    acc_ref,
+    acc_lin_ref,
+    linear_ref,
+):
+    for here, there in (
+        (req_t_in, req_t_ref),
+        (factors_in, factors_ref),
+        (acc_in, acc_ref),
+        (linear_in, linear_ref),
+    ):
+        there[...] = here[...]
+    narrow_ref[...] = factors_in[...].astype(bf16)
+    same_share = iota((SHARE, SHARE), 0) == iota((SHARE, SHARE), 1)
+    acc_lin = jnp.sum(jnp.where(same_share, acc_lin_row_ref[...], 0.0), axis=1, keepdims=True)
+    acc_lin_ref[...] = jnp.sum(jnp.where(of_share(), acc_lin, 0.0), axis=0, keepdims=True)
     chunk = 64
 
     def one(i, carry):
@@ -86,17 +122,21 @@
     clicks_col_ref[...] = jnp.sum(jnp.where(same, clicks, 0.0), axis=1, keepdims=True)
 
 
+def of_share():
+    return jnp.bitwise_and(iota((SHARE, 128), 1), SHARE - 1) == iota((SHARE, 128), 0)
+
+
 def asked_rows_matrix(got):
     owner = jnp.right_shift(iota((SLOTS, 8 * OWNERS), 0), 4)
     pick = (owner * 8 + 4 == iota((SLOTS, 8 * OWNERS), 1)).astype(f32).astype(bf16)
     return pick_slot(dot(pick, got), 0)
 
 
-def gather_kernel(got_ref, factors_ref, out_ref):
+def gather_kernel(got_ref, narrow_ref, out_ref):
     got = got_ref[...].reshape(8 * OWNERS, 128).astype(bf16)
     asked = asked_rows_matrix(got)
     hot = (asked == iota((SLOTS, ROWS), 1).astype(f32)).astype(f32).astype(bf16)
-    found = dot(hot, factors_ref[...].astype(bf16))
+    found = dot(hot, narrow_ref[...])
     out_ref[...] = found.astype(bf16).reshape(OWNERS, CAP, K)
 
 
@@ -142,55 +182,89 @@
     out_ref[:, :, K:] = parts(error_sums, lanes).reshape(OWNERS, CAP, 128)
 
 
+def part_rows(x):
+    rows = iota((8, x.shape[1]), 0)
+    first = x.astype(bf16).astype(f32)
+    rest = x - first
+    second = rest.astype(bf16).astype(f32)
+    third = rest - second
+    out = jnp.where(rows == 0, first, jnp.where(rows == 1, second, jnp.where(rows == 2, third, 0.0)))
+    return out.astype(bf16)
+
+
 def scatter_kernel(push_ref, hot_t_ref, out_ref):
     pushed = push_ref[...].reshape(SLOTS, WIDE)
-    total = dot(hot_t_ref[...], pushed)
-    linear = jnp.sum(total[:, K:], axis=1, keepdims=True)
-    out_ref[:, :, :K] = total[:, :K].astype(bf16).reshape(N_WORKER, SHARE, K)
-    out_ref[:, :, K:] = parts(linear, iota((ROWS, 128), 1)).reshape(N_WORKER, SHARE, 128)
-
-
-def update_kernel(part_ref, acc_ref, acc_lin_ref, delta_ref, new_acc_ref, new_acc_lin_ref):
+    hot_t = hot_t_ref[...]
+    total = dot(hot_t, pushed[:, :K]).astype(bf16)
+    out_ref[:, :SHARE, :] = total[:, :128].reshape(N_WORKER, SHARE, 128)
+    out_ref[:, SHARE : 2 * SHARE, :] = total[:, 128:].reshape(N_WORKER, SHARE, 128)
+    linear = part_rows(jnp.sum(dot(pushed[:, K:], hot_t, 0, 1), axis=0, keepdims=True))
+    for w in range(N_WORKER):
+        lanes = w // 4 * 128
+        out_ref[w, 2 * SHARE :, :] = linear[:, lanes : lanes + 128]
+
+
+def add_parts(part_ref):
     total = part_ref[0].astype(f32)
     for w in range(1, N_WORKER):
         total = total + part_ref[w].astype(f32)
-    grad = total[:, :K]
-    grad_lin = jnp.sum(total[:, K:], axis=1, keepdims=True)
-    state = acc_ref[...] + grad * grad
-    new_acc_ref[...] = state
-    delta = (step_size * grad / jnp.sqrt(state)).astype(bf16)
+    left, right = total[:SHARE], total[SHARE : 2 * SHARE]
+    return left, right, jnp.sum(total[2 * SHARE :], axis=0, keepdims=True)
+
+
+def my_lanes():
+    me = lax.axis_index("y") * N_CORE + lax.axis_index("core")
+    return jnp.right_shift(iota((1, 128), 1), 5) == lax.rem(me, 4)
+
+
+def update_kernel(part_ref, acc_ref, acc_lin_ref, delta_ref):
+    left, right, linear = add_parts(part_ref)
+    acc = acc_ref[...]
+
+    def step(grad, state):
+        return step_size * grad / jnp.sqrt(state + grad * grad)
+
+    left = step(left, acc[:, :128]).astype(bf16)
+    right = step(right, acc[:, 128:]).astype(bf16)
+    linear = part_rows(jnp.where(my_lanes(), step(linear, acc_lin_ref[...]), 0.0))
+    for y in range(N_Y):
+        delta_ref[y, :SHARE, :] = left
+        delta_ref[y, SHARE : 2 * SHARE, :] = right
+        delta_ref[y, 2 * SHARE :, :] = linear
+
+
+def state_kernel(part_ref, acc_ref, acc_lin_ref, new_acc_ref, new_acc_lin_ref):
+    left, right, linear = add_parts(part_ref)
+    new_acc_ref[:, :128] = acc_ref[:, :128] + left * left
+    new_acc_ref[:, 128:] = acc_ref[:, 128:] + right * right
+    state = jnp.where(my_lanes(), acc_lin_ref[...] + linear * linear, 0.0)
+    column = jnp.sum(jnp.where(of_share(), state, 0.0), axis=1, keepdims=True)
     same = iota((SHARE, SHARE), 0) == iota((SHARE, SHARE), 1)
-    acc_lin = jnp.sum(jnp.where(same, acc_lin_ref[...], 0.0), axis=1, keepdims=True)
-    state_lin = acc_lin + grad_lin * grad_lin
-    new_acc_lin_ref[...] = jnp.sum(jnp.where(same, state_lin, 0.0), axis=0, keepdims=True)
-    delta_lin = parts(step_size * grad_lin / jnp.sqrt(state_lin), iota((SHARE, 128), 1))
-    for y in range(N_Y):
-        delta_ref[y, :, :K] = delta
-        delta_ref[y, :, K:] = delta_lin
+    new_acc_lin_ref[...] = jnp.sum(jnp.where(same, column, 0.0), axis=0, keepdims=True)
 
 
 def apply_kernel(delta_ref, factors_ref, linear_ref, new_factors_ref, new_linear_ref):
-    lin = jnp.zeros((1, ROWS), f32)
-    place = iota((SHARE, ROWS), 1) - iota((SHARE, ROWS), 0)
-    for y in range(N_Y):
-        for c in range(N_CORE):
-            first = (y * N_CORE + c) * SHARE
-            block = delta_ref[c * N_Y + y]
-            here = pl.ds(first, SHARE)
-            new_factors_ref[here, :] = factors_ref[here, :] - block[:, :K].astype(f32)
-            step = jnp.sum(block[:, K:].astype(f32), axis=1, keepdims=True)
-            lin = lin + jnp.sum(jnp.where(place == first, step, 0.0), axis=0, keepdims=True)
-    new_linear_ref[...] = linear_ref[...] - lin
-
-
-def call(kernel, out, flops, *args):
+    for q in range(4):
+        lin = jnp.zeros((8, 128), f32)
+        for w in range(4 * q, 4 * q + 4):
+            block = delta_ref[w % N_CORE * N_Y + w // N_CORE].astype(f32)
+            here = pl.ds(w * SHARE, SHARE)
+            new_factors_ref[here, :128] = factors_ref[here, :128] - block[:SHARE]
+            new_factors_ref[here, 128:] = factors_ref[here, 128:] - block[SHARE : 2 * SHARE]
+            lin = lin + block[2 * SHARE :]
+        lanes = pl.ds(q * 128, 128)
+        new_linear_ref[:, lanes] = linear_ref[:, lanes] - jnp.sum(lin, axis=0, keepdims=True)
+
+
+def call(kernel, out, flops, *args, scratch=(), far=False):
     size = sum(a.size * a.dtype.itemsize for a in args)
     return pl.pallas_call(
         kernel,
         out_shape=out,
-        in_specs=[pl.BlockSpec(memory_space=pltpu.VMEM)] * len(args),
+        in_specs=[pl.BlockSpec(memory_space=pltpu.HBM if far else pltpu.VMEM)] * len(args),
         out_specs=jax.tree.map(lambda _: pl.BlockSpec(memory_space=pltpu.VMEM), out),
-        compiler_params=pltpu.CompilerParams(vmem_limit_bytes=24 * 1024 * 1024),
+        scratch_shapes=scratch,
+        compiler_params=pltpu.CompilerParams(vmem_limit_bytes=None if far else 24 * 1024 * 1024),
         cost_estimate=pl.CostEstimate(flops=flops, bytes_accessed=size, transcendentals=0),
     )(*args)
 
@@ -203,18 +277,44 @@
     return lax.all_to_all(x, axis, split_axis=0, concat_axis=0, tiled=True)
 
 
+TALL = 2 * SHARE + 8
+
+
 def body(factors, linear, acc_factors, acc_linear, feature_slot, requests, clicks):
-    req_t = requests.T
-    ask = call(ask_kernel, shape((OWNERS, 8, 128), f32), 1 << 20, req_t, linear.reshape(4, 128))
+    dma = pltpu.SemaphoreType.DMA
+    ask = call(
+        ask_kernel,
+        shape((OWNERS, 8, 128), f32),
+        1 << 20,
+        requests.T,
+        linear.reshape(4, 128),
+        scratch=[pltpu.VMEM((CAP, OWNERS), jnp.int32), pltpu.VMEM((4, 128), f32), dma((2,))],
+        far=True,
+    )
     got = exchange(ask, "server")
-    counts_t, counts, clicks_col = call(
-        count_kernel,
-        [shape((SLOTS, SAMPLES), bf16), shape((SAMPLES, SLOTS), bf16), shape((SAMPLES, 1), f32)],
+    counts_t, counts, clicks_col, req_t, wide, narrow, acc, acc_lin, lin_row = call(
+        prep_kernel,
+        [
+            shape((SLOTS, SAMPLES), bf16),
+            shape((SAMPLES, SLOTS), bf16),
+            shape((SAMPLES, 1), f32),
+            shape((CAP, OWNERS), jnp.int32),
+            shape((ROWS, K), f32),
+            shape((ROWS, K), bf16),
+            shape((SHARE, K), f32),
+            shape((1, 128), f32),
+            shape((1, ROWS), f32),
+        ],
         1 << 30,
         feature_slot.T,
         clicks.reshape(1, SAMPLES),
-    )
-    found = call(gather_kernel, shape((OWNERS, CAP, K), bf16), 1 << 28, got, factors)
+        requests.T,
+        factors,
+        acc_factors,
+        acc_linear.reshape(1, SHARE),
+        linear.reshape(1, ROWS),
+    )
+    found = call(gather_kernel, shape((OWNERS, CAP, K), bf16), 1 << 28, got, narrow)
     rows = exchange(found, "server")
     lin_col, hot_t = call(
         side_kernel, [shape((SLOTS, 1), f32), shape((ROWS, SLOTS), bf16)], 1 << 28, got, req_t
@@ -230,25 +330,16 @@
         lin_col,
     )
     pushed = exchange(push, "server")
-    dense = call(scatter_kernel, shape((N_WORKER, SHARE, WIDE), bf16), 1 << 28, pushed, hot_t)
+    dense = call(scatter_kernel, shape((N_WORKER, TALL, 128), bf16), 1 << 28, pushed, hot_t)
     shared = exchange(dense, ("y", "core"))
-    delta, new_acc, new_acc_lin = call(
-        update_kernel,
-        [shape((N_Y, SHARE, WIDE), bf16), shape((SHARE, K), f32), shape((1, SHARE), f32)],
-        1 << 20,
-        shared,
-        acc_factors,
-        acc_linear.reshape(1, SHARE),
-    )
+    delta = call(update_kernel, shape((N_Y, TALL, 128), bf16), 1 << 20, shared, acc, acc_lin)
     deltas = exchange(delta, "y")
+    new_acc, new_acc_lin = call(
+        state_kernel, [shape((SHARE, K), f32), shape((1, SHARE), f32)], 1 << 20, shared, acc, acc_lin
+    )
     deltas = lax.all_gather(deltas, "core", axis=0, tiled=True)
     new_factors, new_linear = call(
-        apply_kernel,
-        [shape((ROWS, K), f32), shape((1, ROWS), f32)],
-        1 << 20,
-        deltas,
-        factors,
-        linear.reshape(1, ROWS),
+        apply_kernel, [shape((ROWS, K), f32), shape((1, ROWS), f32)], 1 << 20, deltas, wide, lin_row
     )
     return new_factors, new_linear.reshape(ROWS), new_acc, new_acc_lin.reshape(SHARE)
 

time: 103 us -> 99.9 us (0.970)
  blocking collectives: 80.6 us -> 42.5 us
  starting transfers between devices: 4 us -> 21.4 us
  waiting for transfers between devices: 6.01 us -> 23.2 us
  Pallas kernels: 7.64 us -> 9.68 us
  local copies, waits for them, and re-layouts: 3.75 us -> 1.71 us
    all_to_all x4 -> x2, blocking collectives: 78.3 us -> 40.4 us  [exchange(): return lax.all_to_all(x, axis, split_axis=0, concat_axis=0, tiled=True)]
    all_to_all x1 -> x3, starting transfers between devices: 4 us -> 21.4 us  [exchange(): return lax.all_to_all(x, axis, split_axis=0, concat_axis=0, tiled=True)]
    all_to_all x1 -> x3, waiting for transfers between devices: 6.01 us -> 23.2 us  [exchange(): return lax.all_to_all(x, axis, split_axis=0, concat_axis=0, tiled=True)]
    unnamed x18 -> x14, local copies, waits for them, and re-layouts: 3.75 us -> 1.71 us
    pallas_call x8 -> x9, Pallas kernels: 7.64 us -> 9.68 us  [call(): pl.pallas_call(kernel, out_shape=out, in_specs=[pl.BlockSpec(memory_space...]
  transfers between devices with their start and end apart: 1 -> 3, of which waited for: 1 -> 3; matrix products, arithmetic and copies ran while one was open for 0% -> 0% of each run, Pallas kernels for 3% -> 4%
where the time goes in v2:
time: 99.9 us; the launch traced here: 99.3 us
  blocking collectives  42.5 us (43%)
  waiting for transfers between devices  23.2 us (23%)
  starting transfers between devices  21.4 us (21%)
  Pallas kernels  9.68 us (10%)
  local copies, waits for them, and re-layouts  1.71 us (2%)
    all_to_all x2, blocking collectives, exchange(): return lax.all_to_all(x, axis, split_axis=0, concat_axis=0, tiled=True)  40.4 us
    all_to_all x3, waiting for transfers between devices, exchange(): return lax.all_to_all(x, axis, split_axis=0, concat_axis=0, tiled=True)  23.2 us
    all_to_all x3, starting transfers between devices, exchange(): return lax.all_to_all(x, axis, split_axis=0, concat_axis=0, tiled=True)  21.4 us
    pallas_call x9, Pallas kernels, call(): pl.pallas_call(kernel, out_shape=out, in_specs=[pl.BlockSpec(memory_space...  9.68 us
    all_gather x1, blocking collectives, body(): deltas = lax.all_gather(deltas, 'core', axis=0, tiled=True)  2.04 us
  transfers between devices with their start and end apart: 3, of which 3 were waited for; matrix products, arithmetic and copies ran while one was open for 0% of the time, Pallas kernels for 4%

profile of v2, /device:TPU:1, one launch (start us, length us, event | category | flops | bytes accessed | tf_op | source)
XLA Modules:
  0.0 99.3 jit_solution(11040754746457280631)
XLA Ops:
  0.6 1.5 %shard_map.102 = f32[32,8,128]{2,1,0:T(8,128)} custom-call(s32[16,32]{1,0:T(8,128)} %bitcast.8, f32[4,128]{1,0:T(4,128)} %bitcast.10), custom_call_target="tpu_custom_call" | custom-call | flops 1048576 | bytes 4096 | tf_op jit(solution)/shard_map/pallas_call | solution.py:261
  2.2 0.0 copy-start
  2.2 0.0 copy-start.3
  2.2 0.0 copy-start.4
  2.2 13.9 %all-to-all-start = ((f32[32,8,128]{2,1,0:T(8,128)}), f32[32,8,128]{2,1,0:T(8,128)S(1)}, u32[]{:S(2)}, u32[]{:S(2)}) async-start(f32[32,8,128]{2,1,0:T(8,128)} %shard_map.102), calls=%async_computation | async-start | bytes 262144 | tf_op jit(solution)/shard_map/all_to_all | solution.py:277
  16.1 0.0 copy-start.1
  16.1 0.0 copy-start.5
  16.1 0.0 copy-start.6
  16.1 0.0 copy-done
  16.1 0.0 copy-done.3
  16.1 0.0 copy-done.4
  16.1 0.6 copy-done.1
  16.8 0.0 copy-done.5
  16.8 0.0 copy-done.6
  16.8 0.0 copy-start.2
  16.8 1.0 %copy-done.2 = f32[512,256]{1,0:T(8,128)S(1)} copy-done((f32[512,256]{1,0:T(8,128)S(1)}, f32[512,256]{1,0:T(8,128)}, u32[]{:S(2)}) %copy-start.2) | copy-done | bytes 524312
  17.8 2.4 %shard_map.103 = (bf16[512,256]{1,0:T(8,128)(2,1)S(1)}, bf16[256,512]{1,0:T(8,128)(2,1)S(1)}, f32[256,1]{1,0:T(8,128)S(1)}, s32[16,32]{1,0:T(8,128)S(1)}, f32[51...) custom-call(s32[39,256]{1,0:T(8,128)S(1)} %bitcast.12, ...), custom_call_target="tpu_custom_call" | custom-call | flops 1073741824 | bytes 602240 | tf_op jit(solution)/shard_map/pallas_call | solution.py:261
  20.2 5.0 %all-to-all-done.got_ref = f32[32,8,128]{2,1,0:T(8,128)S(1)} async-done(((f32[32,8,128]{2,1,0:T(8,128)}), f32[32,8,128]{2,1,0:T(8,128)S(1)}, u32[]{:S(2)}, u32[]{:S(2)}) %all-to-all-start) | async-done | bytes 131104 | tf_op jit(solution)/shard_map/all_to_all | solution.py:277
  25.2 1.3 %shard_map.104 = bf16[32,16,256]{2,1,0:T(8,128)(2,1)} custom-call(f32[32,8,128]{2,1,0:T(8,128)S(1)} %all-to-all-done.got_ref, bf16[512,256]{1,0:T(8,128)(2,1)S(1)} %get-tuple-element.19.narrow_ref), custom_call_target="tpu_custom_call" | custom-call | flops 268435456 | bytes 393216 | tf_op jit(solution)/shard_map/pallas_call | solution.py:261
  26.6 4.2 %all-to-all-start.1 = ((bf16[32,16,256]{2,1,0:T(8,128)(2,1)}), bf16[32,16,256]{2,1,0:T(8,128)(2,1)S(1)}, u32[]{:S(2)}, u32[]{:S(2)}) async-start(bf16[32,16,256]{2,1,0:T(8,128)(2,1)} %shard_map.104), calls=%async_computation.1 | async-start | bytes 524288 | tf_op jit(solution)/shard_map/all_to_all | solution.py:277
  30.8 0.7 shard_map.105
  31.4 9.0 %all-to-all-done.1.rows_ref = bf16[32,16,256]{2,1,0:T(8,128)(2,1)S(1)} async-done(((bf16[32,16,256]{2,1,0:T(8,128)(2,1)}), bf16[32,16,256]{2,1,0:T(8,128)(2,1)S(1)}, u32[]{:S(2)}, u32[]{:S(2)}) %all-to-all-start.1) | async-done | bytes 262176 | tf_op jit(solution)/shard_map/all_to_all | solution.py:277
  40.4 1.1 %shard_map.106 = bf16[32,16,384]{2,1,0:T(8,128)(2,1)S(1)} custom-call(bf16[32,16,256]{2,1,0:T(8,128)(2,1)S(1)} %all-to-all-done.1.rows_ref, bf16[256,512]{1,0:T(8,128)(2,1)S(1)} %get-tuple-element.20.counts_ref, bf16[512,256]{1,0:T(8,128)(2,1)S(1)} %get-tuple-element.21.counts_t_ref, f32[256,1]{1,0:T(8,128)S(1)} %get-tuple-element.22.clicks_ref, ...), custom_call_target="tpu_custom_call" | custom-call | flops 268435456 | bytes 789504 | tf_op jit(solution)/shard_map/pallas_call | solution.py:261
  41.5 15.9 %all_to_all.25.push_ref = bf16[32,16,384]{2,1,0:T(8,128)(2,1)S(1)} all-to-all(bf16[32,16,384]{2,1,0:T(8,128)(2,1)S(1)} %shard_map.106), channel_id=1, replica_groups=mesh['server'=32,'y'=8,'core'=2] {'server'}, dimensions={0} | all-to-all | bytes 786432 | tf_op jit(solution)/shard_map/all_to_all | solution.py:277
  57.4 0.5 shard_map.107
  57.9 24.5 %all_to_all.26.part_ref = bf16[16,72,128]{2,1,0:T(8,128)(2,1)S(1)} all-to-all(bf16[16,72,128]{2,1,0:T(8,128)(2,1)S(1)} %shard_map.107), channel_id=1, replica_groups=mesh['server'=32,'y'=8,'core'=2] {'y','core'}, dimensions={0} | all-to-all | bytes 589824 | tf_op jit(solution)/shard_map/all_to_all | solution.py:277
  82.4 0.7 shard_map.108
  83.1 3.4 %all-to-all-start.4 = ((bf16[8,72,128]{2,1,0:T(8,128)(2,1)}), bf16[8,72,128]{2,1,0:T(8,128)(2,1)S(1)}, u32[]{:S(2)}, u32[]{:S(2)}) async-start(bf16[8,72,128]{2,1,0:T(8,128)(2,1)} %shard_map.108), calls=%async_computation.4 | async-start | bytes 294912 | tf_op jit(solution)/shard_map/all_to_all | solution.py:277
  86.5 0.7 shard_map.110
  87.2 9.2 %all-to-all-done.4 = bf16[8,72,128]{2,1,0:T(8,128)(2,1)S(1)} async-done(((bf16[8,72,128]{2,1,0:T(8,128)(2,1)}), bf16[8,72,128]{2,1,0:T(8,128)(2,1)S(1)}, u32[]{:S(2)}, u32[]{:S(2)}) %all-to-all-start.4) | async-done | bytes 147488 | tf_op jit(solution)/shard_map/all_to_all | solution.py:277
  96.4 2.0 %all_gather.3.delta_ref = bf16[16,72,128]{2,1,0:T(8,128)(2,1)S(1)} all-gather(bf16[8,72,128]{2,1,0:T(8,128)(2,1)S(1)} %all-to-all-done.4), channel_id=1, replica_groups=mesh['server'=32,'y'=8,'core'=2] {'core'}, dimensions={0}, use_global_device_ids=true | all-gather | bytes 442368 | tf_op jit(solution)/shard_map/all_gather | solution.py:340
  98.4 0.9 shard_map.109
Async XLA Ops:
  2.2 13.9 %copy-start = (s32[32,16]{0,1:T(8,128)S(1)}, s32[32,16]{0,1:T(8,128)}, u32[]{:S(2)}) copy-start(s32[32,16]{0,1:T(8,128)} %param.12) | copy-start | bytes 6148
  2.2 13.9 %copy-start.3 = (s32[256,39]{0,1:T(8,128)S(1)}, s32[256,39]{0,1:T(8,128)}, u32[]{:S(2)}) copy-start(s32[256,39]{0,1:T(8,128)} %param.11) | copy-start | bytes 119812
  2.2 13.9 %copy-start.4 = (f32[32,256]{1,0:T(8,128)S(1)}, f32[32,256]{1,0:T(8,128)}, u32[]{:S(2)}) copy-start(f32[32,256]{1,0:T(8,128)} %acc_in.1) | copy-start | bytes 98308
  2.2 23.0 %all-to-all-start = ((f32[32,8,128]{2,1,0:T(8,128)}), f32[32,8,128]{2,1,0:T(8,128)S(1)}, u32[]{:S(2)}, u32[]{:S(2)}) async-start(f32[32,8,128]{2,1,0:T(8,128)} %shard_map.102), calls=%async_computation | async-start | bytes 262144 | tf_op jit(solution)/shard_map/all_to_all | solution.py:277
  16.1 0.7 copy-start.1
  16.1 0.7 copy-start.5
  16.1 0.7 copy-start.6
  16.8 1.0 %copy-start.2 = (f32[512,256]{1,0:T(8,128)S(1)}, f32[512,256]{1,0:T(8,128)}, u32[]{:S(2)}) copy-start(f32[512,256]{1,0:T(8,128)} %factors_in.1) | copy-start | bytes 1572868
  26.6 13.9 %all-to-all-start.1 = ((bf16[32,16,256]{2,1,0:T(8,128)(2,1)}), bf16[32,16,256]{2,1,0:T(8,128)(2,1)S(1)}, u32[]{:S(2)}, u32[]{:S(2)}) async-start(bf16[32,16,256]{2,1,0:T(8,128)(2,1)} %shard_map.104), calls=%async_computation.1 | async-start | bytes 524288 | tf_op jit(solution)/shard_map/all_to_all | solution.py:277
  83.1 13.3 %all-to-all-start.4 = ((bf16[8,72,128]{2,1,0:T(8,128)(2,1)}), bf16[8,72,128]{2,1,0:T(8,128)(2,1)S(1)}, u32[]{:S(2)}, u32[]{:S(2)}) async-start(bf16[8,72,128]{2,1,0:T(8,128)(2,1)} %shard_map.108), calls=%async_computation.4 | async-start | bytes 294912 | tf_op jit(solution)/shard_map/all_to_all | solution.py:277

commit v3 on v2

--- a/solution.py
+++ b/solution.py
@@ -31,15 +31,6 @@
     return lax.dot_general(a, b, (((ca,), (cb,)), ((), ())), preferred_element_type=f32)
 
 
-def parts(x, lanes):
-    first = x.astype(bf16).astype(f32)
-    rest = x - first
-    second = rest.astype(bf16).astype(f32)
-    third = rest - second
-    out = jnp.where(lanes == 0, first, jnp.where(lanes == 1, second, jnp.where(lanes == 2, third, 0.0)))
-    return out.astype(bf16)
-
-
 def split_requests(req_t):
     high = jnp.bitwise_and(req_t, -16)
     low = jnp.bitwise_and(req_t, 15)
@@ -47,12 +38,18 @@
     return jnp.concatenate([high, low, pad], axis=0).astype(f32).astype(bf16)
 
 
-def pick_slot(a, slot_axis):
-    place_axis = 1 - slot_axis
-    place = iota(a.shape, place_axis)
-    position = jnp.bitwise_and(iota(a.shape, slot_axis), CAP - 1)
-    keep = (place < 2 * CAP) & (jnp.bitwise_and(place, CAP - 1) == position)
-    return jnp.sum(jnp.where(keep, a, 0.0), axis=place_axis, keepdims=True)
+def own_lists(req_t):
+    owner = jnp.right_shift(iota((SLOTS, OWNERS), 0), 4)
+    mine = (owner == iota((SLOTS, OWNERS), 1)).astype(f32).astype(bf16)
+    lists = dot(mine, split_requests(req_t), 1, 1)
+    lane = iota((SLOTS, 128), 1)
+    position = jnp.bitwise_and(iota((SLOTS, 128), 0), CAP - 1)
+    keep = (lane < 2 * CAP) & (jnp.bitwise_and(lane, CAP - 1) == position)
+    return jnp.where(keep, lists, 0.0)
+
+
+def ones(dims, axis):
+    return (iota(dims, axis) < 2 * CAP).astype(f32).astype(bf16)
 
 
 def ask_kernel(req_t_hbm, lin_hbm, out_ref, req_t_ref, lin_ref, sems):
@@ -62,17 +59,15 @@
     ]
     for copy in copies:
         copy.start()
-    block = jnp.right_shift(iota((8 * OWNERS, OWNERS), 0), 3)
-    sub = jnp.bitwise_and(iota((8 * OWNERS, OWNERS), 0), 7)
-    to_owner = (block == iota((8 * OWNERS, OWNERS), 1)) & (sub == 4)
-    sub4 = jnp.bitwise_and(iota((8 * OWNERS, 4), 0), 7)
-    spread = sub4 == iota((8 * OWNERS, 4), 1)
     for copy in copies:
         copy.wait()
-    lists = split_requests(req_t_ref[...])
-    lin = lin_ref[...].astype(bf16)
-    out = dot(to_owner.astype(f32).astype(bf16), lists, 1, 1) + dot(spread.astype(f32).astype(bf16), lin)
-    out_ref[...] = out.reshape(OWNERS, 8, 128)
+    lists = own_lists(req_t_ref[...])
+    spread = (jnp.right_shift(iota((CAP, 4), 0), 1) == iota((CAP, 4), 1)).astype(f32).astype(bf16)
+    lin = dot(spread, lin_ref[...].astype(bf16))
+    odd = jnp.bitwise_and(iota((CAP, 128), 0), 1) == 1
+    lin = jnp.where(odd, lin, pltpu.roll(lin, 64, 1))
+    lin = jnp.where(iota((CAP, 128), 1) >= 64, lin, 0.0)
+    out_ref[...] = (lists.reshape(OWNERS, CAP, 128) + lin[None]).astype(bf16)
 
 
 def prep_kernel(
@@ -126,38 +121,21 @@
     return jnp.bitwise_and(iota((SHARE, 128), 1), SHARE - 1) == iota((SHARE, 128), 0)
 
 
-def asked_rows_matrix(got):
-    owner = jnp.right_shift(iota((SLOTS, 8 * OWNERS), 0), 4)
-    pick = (owner * 8 + 4 == iota((SLOTS, 8 * OWNERS), 1)).astype(f32).astype(bf16)
-    return pick_slot(dot(pick, got), 0)
-
-
 def gather_kernel(got_ref, narrow_ref, out_ref):
-    got = got_ref[...].reshape(8 * OWNERS, 128).astype(bf16)
-    asked = asked_rows_matrix(got)
+    asked = dot(got_ref[...].reshape(SLOTS, 128), ones((128, ROWS), 0))
     hot = (asked == iota((SLOTS, ROWS), 1).astype(f32)).astype(f32).astype(bf16)
-    found = dot(hot, narrow_ref[...])
-    out_ref[...] = found.astype(bf16).reshape(OWNERS, CAP, K)
+    out_ref[...] = dot(hot, narrow_ref[...]).astype(bf16).reshape(OWNERS, CAP, K)
 
 
 def side_kernel(got_ref, req_t_ref, lin_ref, hot_t_ref):
-    got = got_ref[...].reshape(8 * OWNERS, 128).astype(bf16)
-    lists = split_requests(req_t_ref[...])
-    owner = jnp.right_shift(iota((SLOTS, OWNERS), 0), 4)
-    mine = (owner == iota((SLOTS, OWNERS), 1)).astype(f32).astype(bf16)
-    wanted = pick_slot(dot(mine, lists, 1, 1), 0)
-    block = jnp.right_shift(iota((SLOTS, 8 * OWNERS), 0), 4) * 8
-    column = iota((SLOTS, 8 * OWNERS), 1)
-    lanes = iota((SLOTS, 128), 1).astype(f32)
-    total = jnp.zeros((SLOTS, 128), f32)
-    for k in range(4):
-        pick = (block + k == column).astype(f32).astype(bf16)
-        values = dot(pick, got)
-        total = total + jnp.where(wanted == lanes + 128.0 * k, values, 0.0)
-    lin_ref[...] = jnp.sum(total, axis=1, keepdims=True)
-    owner_t = jnp.right_shift(iota((8 * OWNERS, SLOTS), 1), 4)
-    pick_t = (owner_t * 8 + 4 == iota((8 * OWNERS, SLOTS), 0)).astype(f32).astype(bf16)
-    asked_t = pick_slot(dot(got, pick_t, 0, 0), 1)
+    got = got_ref[...].reshape(SLOTS, 128)
+    wanted = dot(own_lists(req_t_ref[...]).astype(bf16), ones((128, SLOTS), 0)).astype(jnp.int32)
+    first = jnp.bitwise_and(iota((SLOTS, SLOTS), 0), -CAP)
+    pick = iota((SLOTS, SLOTS), 1) == first + jnp.right_shift(wanted, 6)
+    values = dot(pick.astype(f32).astype(bf16), got)
+    here = iota((SLOTS, 128), 1) == jnp.bitwise_and(wanted[:, :128], 63) + 64
+    lin_ref[...] = jnp.where(here, values, 0.0).astype(bf16)
+    asked_t = dot(ones((ROWS, 128), 1), got, 1, 1)
     hot_t_ref[...] = (asked_t == iota((ROWS, SLOTS), 0).astype(f32)).astype(f32).astype(bf16)
 
 
@@ -166,20 +144,25 @@
     wide_rows = rows.astype(f32)
     counts = counts_ref[...]
     sums = dot(counts, rows)
-    norms = jnp.sum(wide_rows * wide_rows, axis=1, keepdims=True)
-    lanes = iota((SLOTS, 128), 1)
-    terms = parts(lin_ref[...] - 0.5 * norms, lanes)
-    base = jnp.sum(dot(counts, terms), axis=1, keepdims=True)
-    logits = base + 0.5 * jnp.sum(sums * sums, axis=1, keepdims=True)
-    errors = jax.nn.sigmoid(logits) - clicks_ref[...]
+    square = wide_rows * wide_rows
+    high = square.astype(bf16)
+    low = (square - high.astype(f32)).astype(bf16)
+    terms = sums * sums - dot(counts, high) - dot(counts, low)
+    terms = 0.5 * (terms[:, :128] + terms[:, 128:]) + dot(counts, lin_ref[...])
+    logits = jnp.sum(terms, axis=1, keepdims=True)
+    errors = jnp.broadcast_to(jax.nn.sigmoid(logits) - clicks_ref[...], (SAMPLES, K))
     weighted = (errors * sums).astype(bf16)
-    error_parts = parts(errors, iota((SAMPLES, 128), 1))
+    first = errors.astype(bf16)
+    second = (errors - first.astype(f32)).astype(bf16)
     counts_t = counts_t_ref[...]
-    gathered = dot(counts_t, weighted)
-    error_sums = jnp.sum(dot(counts_t, error_parts), axis=1, keepdims=True)
-    grads = gathered - error_sums * wide_rows
+    error_sums = dot(counts_t, first) + dot(counts_t, second)
+    grads = dot(counts_t, weighted) - error_sums * wide_rows
     out_ref[:, :, :K] = grads.astype(bf16).reshape(OWNERS, CAP, K)
-    out_ref[:, :, K:] = parts(error_sums, lanes).reshape(OWNERS, CAP, 128)
+    total = error_sums[:, :128]
+    lane = iota((SLOTS, 128), 1)
+    first = total.astype(bf16).astype(f32)
+    linear = jnp.where(lane == 0, first, jnp.where(lane == 1, total - first, 0.0))
+    out_ref[:, :, K:] = linear.astype(bf16).reshape(OWNERS, CAP, 128)
 
 
 def part_rows(x):
@@ -284,7 +267,7 @@
     dma = pltpu.SemaphoreType.DMA
     ask = call(
         ask_kernel,
-        shape((OWNERS, 8, 128), f32),
+        shape((OWNERS, CAP, 128), bf16),
         1 << 20,
         requests.T,
         linear.reshape(4, 128),
@@ -316,8 +299,8 @@
     )
     found = call(gather_kernel, shape((OWNERS, CAP, K), bf16), 1 << 28, got, narrow)
     rows = exchange(found, "server")
-    lin_col, hot_t = call(
-        side_kernel, [shape((SLOTS, 1), f32), shape((ROWS, SLOTS), bf16)], 1 << 28, got, req_t
+    lin_terms, hot_t = call(
+        side_kernel, [shape((SLOTS, 128), bf16), shape((ROWS, SLOTS), bf16)], 1 << 28, got, req_t
     )
     push = call(
         learn_kernel,
@@ -327,7 +310,7 @@
         counts,
         counts_t,
         clicks_col,
-        lin_col,
+        lin_terms,
     )
     pushed = exchange(push, "server")
     dense = call(scatter_kernel, shape((N_WORKER, TALL, 128), bf16), 1 << 28, pushed, hot_t)

time: 99.9 us -> 99.9 us (level)
  no operation moved by 1% of the time
where the time goes in v3:
time: 99.9 us; the launch traced here: 99.3 us
  blocking collectives  42.5 us (43%)
  waiting for transfers between devices  23.2 us (23%)
  starting transfers between devices  21.4 us (21%)
  Pallas kernels  9.72 us (10%)
  local copies, waits for them, and re-layouts  1.71 us (2%)
    all_to_all x2, blocking collectives, exchange(): return lax.all_to_all(x, axis, split_axis=0, concat_axis=0, tiled=True)  40.4 us
    all_to_all x3, waiting for transfers between devices, exchange(): return lax.all_to_all(x, axis, split_axis=0, concat_axis=0, tiled=True)  23.2 us
    all_to_all x3, starting transfers between devices, exchange(): return lax.all_to_all(x, axis, split_axis=0, concat_axis=0, tiled=True)  21.4 us
    pallas_call x9, Pallas kernels, call(): pl.pallas_call(kernel, out_shape=out, in_specs=[pl.BlockSpec(memory_space...  9.72 us
    all_gather x1, blocking collectives, body(): deltas = lax.all_gather(deltas, 'core', axis=0, tiled=True)  2.04 us
  transfers between devices with their start and end apart: 3, of which 3 were waited for; matrix products, arithmetic and copies ran while one was open for 0% of the time, Pallas kernels for 4%

profile of v3, /device:TPU:1, one launch (start us, length us, event | category | flops | bytes accessed | tf_op | source)
XLA Modules:
  0.0 99.3 jit_solution(11755580069296990861)
XLA Ops:
  0.6 1.6 %shard_map.102 = bf16[32,16,128]{2,1,0:T(8,128)(2,1)} custom-call(s32[16,32]{1,0:T(8,128)} %bitcast.8, f32[4,128]{1,0:T(4,128)} %bitcast.10), custom_call_target="tpu_custom_call" | custom-call | flops 1048576 | bytes 4096 | tf_op jit(solution)/shard_map/pallas_call | solution.py:244
  2.3 0.0 copy-start
  2.3 0.0 copy-start.3
  2.3 0.0 copy-start.4
  2.3 13.9 %all-to-all-start = ((bf16[32,16,128]{2,1,0:T(8,128)(2,1)}), bf16[32,16,128]{2,1,0:T(8,128)(2,1)S(1)}, u32[]{:S(2)}, u32[]{:S(2)}) async-start(bf16[32,16,128]{2,1,0:T(8,128)(2,1)} %shard_map.102), calls=%async_computation | async-start | bytes 262144 | tf_op jit(solution)/shard_map/all_to_all | solution.py:260
  16.2 0.0 copy-start.1
  16.2 0.0 copy-start.5
  16.2 0.0 copy-start.6
  16.2 0.0 copy-done
  16.2 0.0 copy-done.3
  16.2 0.0 copy-done.4
  16.2 0.6 copy-done.1
  16.9 0.0 copy-done.5
  16.9 0.0 copy-done.6
  16.9 0.0 copy-start.2
  16.9 1.0 %copy-done.2 = f32[512,256]{1,0:T(8,128)S(1)} copy-done((f32[512,256]{1,0:T(8,128)S(1)}, f32[512,256]{1,0:T(8,128)}, u32[]{:S(2)}) %copy-start.2) | copy-done | bytes 524312
  17.9 2.4 %shard_map.103 = (bf16[512,256]{1,0:T(8,128)(2,1)S(1)}, bf16[256,512]{1,0:T(8,128)(2,1)S(1)}, f32[256,1]{1,0:T(8,128)S(1)}, s32[16,32]{1,0:T(8,128)S(1)}, f32[51...) custom-call(s32[39,256]{1,0:T(8,128)S(1)} %bitcast.12, ...), custom_call_target="tpu_custom_call" | custom-call | flops 1073741824 | bytes 602240 | tf_op jit(solution)/shard_map/pallas_call | solution.py:244
  20.3 5.0 %all-to-all-done.got_ref = bf16[32,16,128]{2,1,0:T(8,128)(2,1)S(1)} async-done(((bf16[32,16,128]{2,1,0:T(8,128)(2,1)}), bf16[32,16,128]{2,1,0:T(8,128)(2,1)S(1)}, u32[]{:S(2)}, u32[]{:S(2)}) %all-to-all-start) | async-done | bytes 131104 | tf_op jit(solution)/shard_map/all_to_all | solution.py:260
  25.3 1.2 %shard_map.104 = bf16[32,16,256]{2,1,0:T(8,128)(2,1)} custom-call(bf16[32,16,128]{2,1,0:T(8,128)(2,1)S(1)} %all-to-all-done.got_ref, bf16[512,256]{1,0:T(8,128)(2,1)S(1)} %get-tuple-element.19.narrow_ref), custom_call_target="tpu_custom_call" | custom-call | flops 268435456 | bytes 393216 | tf_op jit(solution)/shard_map/pallas_call | solution.py:244
  26.5 4.2 %all-to-all-start.1 = ((bf16[32,16,256]{2,1,0:T(8,128)(2,1)}), bf16[32,16,256]{2,1,0:T(8,128)(2,1)S(1)}, u32[]{:S(2)}, u32[]{:S(2)}) async-start(bf16[32,16,256]{2,1,0:T(8,128)(2,1)} %shard_map.104), calls=%async_computation.1 | async-start | bytes 524288 | tf_op jit(solution)/shard_map/all_to_all | solution.py:260
  30.7 0.7 shard_map.105
  31.4 8.9 %all-to-all-done.1.rows_ref = bf16[32,16,256]{2,1,0:T(8,128)(2,1)S(1)} async-done(((bf16[32,16,256]{2,1,0:T(8,128)(2,1)}), bf16[32,16,256]{2,1,0:T(8,128)(2,1)S(1)}, u32[]{:S(2)}, u32[]{:S(2)}) %all-to-all-start.1) | async-done | bytes 262176 | tf_op jit(solution)/shard_map/all_to_all | solution.py:260
  40.4 1.1 %shard_map.106 = bf16[32,16,384]{2,1,0:T(8,128)(2,1)S(1)} custom-call(bf16[32,16,256]{2,1,0:T(8,128)(2,1)S(1)} %all-to-all-done.1.rows_ref, bf16[256,512]{1,0:T(8,128)(2,1)S(1)} %get-tuple-element.20.counts_ref, bf16[512,256]{1,0:T(8,128)(2,1)S(1)} %get-tuple-element.21.counts_t_ref, f32[256,1]{1,0:T(8,128)S(1)} %get-tuple-element.22.clicks_ref, ...), custom_call_target="tpu_custom_call" | custom-call | flops 268435456 | bytes 918528 | tf_op jit(solution)/shard_map/pallas_call | solution.py:244
  41.5 15.9 %all_to_all.25.push_ref = bf16[32,16,384]{2,1,0:T(8,128)(2,1)S(1)} all-to-all(bf16[32,16,384]{2,1,0:T(8,128)(2,1)S(1)} %shard_map.106), channel_id=1, replica_groups=mesh['server'=32,'y'=8,'core'=2] {'server'}, dimensions={0} | all-to-all | bytes 786432 | tf_op jit(solution)/shard_map/all_to_all | solution.py:260
  57.4 0.4 shard_map.107
  57.9 24.5 %all_to_all.26.part_ref = bf16[16,72,128]{2,1,0:T(8,128)(2,1)S(1)} all-to-all(bf16[16,72,128]{2,1,0:T(8,128)(2,1)S(1)} %shard_map.107), channel_id=1, replica_groups=mesh['server'=32,'y'=8,'core'=2] {'y','core'}, dimensions={0} | all-to-all | bytes 589824 | tf_op jit(solution)/shard_map/all_to_all | solution.py:260
  82.4 0.7 shard_map.108
  83.1 3.4 %all-to-all-start.4 = ((bf16[8,72,128]{2,1,0:T(8,128)(2,1)}), bf16[8,72,128]{2,1,0:T(8,128)(2,1)S(1)}, u32[]{:S(2)}, u32[]{:S(2)}) async-start(bf16[8,72,128]{2,1,0:T(8,128)(2,1)} %shard_map.108), calls=%async_computation.4 | async-start | bytes 294912 | tf_op jit(solution)/shard_map/all_to_all | solution.py:260
  86.5 0.7 shard_map.110
  87.2 9.2 %all-to-all-done.4 = bf16[8,72,128]{2,1,0:T(8,128)(2,1)S(1)} async-done(((bf16[8,72,128]{2,1,0:T(8,128)(2,1)}), bf16[8,72,128]{2,1,0:T(8,128)(2,1)S(1)}, u32[]{:S(2)}, u32[]{:S(2)}) %all-to-all-start.4) | async-done | bytes 147488 | tf_op jit(solution)/shard_map/all_to_all | solution.py:260
  96.4 2.0 %all_gather.3.delta_ref = bf16[16,72,128]{2,1,0:T(8,128)(2,1)S(1)} all-gather(bf16[8,72,128]{2,1,0:T(8,128)(2,1)S(1)} %all-to-all-done.4), channel_id=1, replica_groups=mesh['server'=32,'y'=8,'core'=2] {'core'}, dimensions={0}, use_global_device_ids=true | all-gather | bytes 442368 | tf_op jit(solution)/shard_map/all_gather | solution.py:323
  98.4 0.9 shard_map.109
Async XLA Ops:
  2.3 13.9 %copy-start = (s32[32,16]{0,1:T(8,128)S(1)}, s32[32,16]{0,1:T(8,128)}, u32[]{:S(2)}) copy-start(s32[32,16]{0,1:T(8,128)} %param.12) | copy-start | bytes 6148
  2.3 13.9 %copy-start.3 = (s32[256,39]{0,1:T(8,128)S(1)}, s32[256,39]{0,1:T(8,128)}, u32[]{:S(2)}) copy-start(s32[256,39]{0,1:T(8,128)} %param.11) | copy-start | bytes 119812
  2.3 13.9 %copy-start.4 = (f32[32,256]{1,0:T(8,128)S(1)}, f32[32,256]{1,0:T(8,128)}, u32[]{:S(2)}) copy-start(f32[32,256]{1,0:T(8,128)} %acc_in.1) | copy-start | bytes 98308
  2.3 23.0 %all-to-all-start = ((bf16[32,16,128]{2,1,0:T(8,128)(2,1)}), bf16[32,16,128]{2,1,0:T(8,128)(2,1)S(1)}, u32[]{:S(2)}, u32[]{:S(2)}) async-start(bf16[32,16,128]{2,1,0:T(8,128)(2,1)} %shard_map.102), calls=%async_computation | async-start | bytes 262144 | tf_op jit(solution)/shard_map/all_to_all | solution.py:260
  16.2 0.7 copy-start.1
  16.2 0.7 copy-start.5
  16.2 0.7 copy-start.6
  16.9 1.0 %copy-start.2 = (f32[512,256]{1,0:T(8,128)S(1)}, f32[512,256]{1,0:T(8,128)}, u32[]{:S(2)}) copy-start(f32[512,256]{1,0:T(8,128)} %factors_in.1) | copy-start | bytes 1572868
  26.5 13.9 %all-to-all-start.1 = ((bf16[32,16,256]{2,1,0:T(8,128)(2,1)}), bf16[32,16,256]{2,1,0:T(8,128)(2,1)S(1)}, u32[]{:S(2)}, u32[]{:S(2)}) async-start(bf16[32,16,256]{2,1,0:T(8,128)(2,1)} %shard_map.104), calls=%async_computation.1 | async-start | bytes 524288 | tf_op jit(solution)/shard_map/all_to_all | solution.py:260
  83.1 13.3 %all-to-all-start.4 = ((bf16[8,72,128]{2,1,0:T(8,128)(2,1)}), bf16[8,72,128]{2,1,0:T(8,128)(2,1)S(1)}, u32[]{:S(2)}, u32[]{:S(2)}) async-start(bf16[8,72,128]{2,1,0:T(8,128)(2,1)} %shard_map.108), calls=%async_computation.4 | async-start | bytes 294912 | tf_op jit(solution)/shard_map/all_to_all | solution.py:260

commit v4 on v3

--- a/solution.py
+++ b/solution.py
@@ -127,7 +127,7 @@
     out_ref[...] = dot(hot, narrow_ref[...]).astype(bf16).reshape(OWNERS, CAP, K)
 
 
-def side_kernel(got_ref, req_t_ref, lin_ref, hot_t_ref):
+def side_kernel(got_ref, both_ref, req_t_ref, lin_ref, hot_t_ref):
     got = got_ref[...].reshape(SLOTS, 128)
     wanted = dot(own_lists(req_t_ref[...]).astype(bf16), ones((128, SLOTS), 0)).astype(jnp.int32)
     first = jnp.bitwise_and(iota((SLOTS, SLOTS), 0), -CAP)
@@ -135,8 +135,9 @@
     values = dot(pick.astype(f32).astype(bf16), got)
     here = iota((SLOTS, 128), 1) == jnp.bitwise_and(wanted[:, :128], 63) + 64
     lin_ref[...] = jnp.where(here, values, 0.0).astype(bf16)
-    asked_t = dot(ones((ROWS, 128), 1), got, 1, 1)
-    hot_t_ref[...] = (asked_t == iota((ROWS, SLOTS), 0).astype(f32)).astype(f32).astype(bf16)
+    asked_t = dot(ones((ROWS, 128), 1), both_ref[...].reshape(N_CORE * SLOTS, 128), 1, 1)
+    hot = asked_t == iota((ROWS, N_CORE * SLOTS), 0).astype(f32)
+    hot_t_ref[...] = hot.astype(f32).astype(bf16)
 
 
 def learn_kernel(rows_ref, counts_ref, counts_t_ref, clicks_ref, lin_ref, out_ref):
@@ -176,21 +177,24 @@
 
 
 def scatter_kernel(push_ref, hot_t_ref, out_ref):
-    pushed = push_ref[...].reshape(SLOTS, WIDE)
-    hot_t = hot_t_ref[...]
-    total = dot(hot_t, pushed[:, :K]).astype(bf16)
-    out_ref[:, :SHARE, :] = total[:, :128].reshape(N_WORKER, SHARE, 128)
-    out_ref[:, SHARE : 2 * SHARE, :] = total[:, 128:].reshape(N_WORKER, SHARE, 128)
-    linear = part_rows(jnp.sum(dot(pushed[:, K:], hot_t, 0, 1), axis=0, keepdims=True))
-    for w in range(N_WORKER):
-        lanes = w // 4 * 128
-        out_ref[w, 2 * SHARE :, :] = linear[:, lanes : lanes + 128]
+    core = lax.axis_index("core")
+    pushed = push_ref[...].reshape(N_CORE * SLOTS, WIDE)
+    shares = [
+        hot_t_ref[pl.ds(pl.multiple_of((y * N_CORE + core) * SHARE, SHARE), SHARE), :] for y in range(N_Y)
+    ]
+    total = dot(jnp.concatenate(shares, axis=0), pushed[:, :K]).astype(bf16)
+    out_ref[:, :SHARE, :] = total[:, :128].reshape(N_Y, SHARE, 128)
+    out_ref[:, SHARE : 2 * SHARE, :] = total[:, 128:].reshape(N_Y, SHARE, 128)
+    linear = part_rows(jnp.sum(dot(pushed[:, K:], hot_t_ref[...], 0, 1), axis=0, keepdims=True))
+    for y in range(N_Y):
+        lanes = y // 2 * 128
+        out_ref[y, 2 * SHARE :, :] = linear[:, lanes : lanes + 128]
 
 
 def add_parts(part_ref):
     total = part_ref[0].astype(f32)
-    for w in range(1, N_WORKER):
-        total = total + part_ref[w].astype(f32)
+    for y in range(1, N_Y):
+        total = total + part_ref[y].astype(f32)
     left, right = total[:SHARE], total[SHARE : 2 * SHARE]
     return left, right, jnp.sum(total[2 * SHARE :], axis=0, keepdims=True)
 
@@ -299,8 +303,14 @@
     )
     found = call(gather_kernel, shape((OWNERS, CAP, K), bf16), 1 << 28, got, narrow)
     rows = exchange(found, "server")
+    both = lax.all_gather(got, "core", axis=0, tiled=True)
     lin_terms, hot_t = call(
-        side_kernel, [shape((SLOTS, 128), bf16), shape((ROWS, SLOTS), bf16)], 1 << 28, got, req_t
+        side_kernel,
+        [shape((SLOTS, 128), bf16), shape((ROWS, N_CORE * SLOTS), bf16)],
+        1 << 28,
+        got,
+        both,
+        req_t,
     )
     push = call(
         learn_kernel,
@@ -313,8 +323,9 @@
         lin_terms,
     )
     pushed = exchange(push, "server")
-    dense = call(scatter_kernel, shape((N_WORKER, TALL, 128), bf16), 1 << 28, pushed, hot_t)
-    shared = exchange(dense, ("y", "core"))
+    pushed = lax.all_gather(pushed, "core", axis=0, tiled=True)
+    dense = call(scatter_kernel, shape((N_Y, TALL, 128), bf16), 1 << 28, pushed, hot_t)
+    shared = exchange(dense, "y")
     delta = call(update_kernel, shape((N_Y, TALL, 128), bf16), 1 << 20, shared, acc, acc_lin)
     deltas = exchange(delta, "y")
     new_acc, new_acc_lin = call(

time: 99.9 us -> 98.6 us (0.987)
  waiting for transfers between devices: 23.2 us -> 17.9 us
  blocking collectives: 42.5 us -> 46.2 us
    all_gather x0 -> x2, blocking collectives: none -> 10.6 us  [the longest x1 7.22 us: body(): pushed = lax.all_gather(pushed, 'core', axis=0, tiled=True)]
    all_to_all x2, blocking collectives: 40.4 us -> 30.8 us  [exchange(): return lax.all_to_all(x, axis, split_axis=0, concat_axis=0, tiled=True)]
    all_to_all x3, waiting for transfers between devices: 23.2 us -> 17.9 us  [exchange(): return lax.all_to_all(x, axis, split_axis=0, concat_axis=0, tiled=True)]
    all_gather x1, blocking collectives: 2.04 us -> 4.78 us  [body(): deltas = lax.all_gather(deltas, 'core', axis=0, tiled=True)]
where the time goes in v4:
time: 98.6 us; the launch traced here: 98 us
  blocking collectives  46.2 us (47%)
  starting transfers between devices  21.4 us (22%)
  waiting for transfers between devices  17.9 us (18%)
  Pallas kernels  9.97 us (10%)
  local copies, waits for them, and re-layouts  1.71 us (2%)
    all_to_all x2, blocking collectives, exchange(): return lax.all_to_all(x, axis, split_axis=0, concat_axis=0, tiled=True)  30.8 us
    all_to_all x3, starting transfers between devices, exchange(): return lax.all_to_all(x, axis, split_axis=0, concat_axis=0, tiled=True)  21.4 us
    all_to_all x3, waiting for transfers between devices, exchange(): return lax.all_to_all(x, axis, split_axis=0, concat_axis=0, tiled=True)  17.9 us
    pallas_call x9, Pallas kernels, call(): pl.pallas_call(kernel, out_shape=out, in_specs=[pl.BlockSpec(memory_space...  9.97 us
    all_gather x1, blocking collectives, body(): pushed = lax.all_gather(pushed, 'core', axis=0, tiled=True)  7.22 us
    all_gather x1, blocking collectives, body(): deltas = lax.all_gather(deltas, 'core', axis=0, tiled=True)  4.78 us
    all_gather x1, blocking collectives, body(): both = lax.all_gather(got, 'core', axis=0, tiled=True)  3.39 us
  transfers between devices with their start and end apart: 3, of which 3 were waited for; matrix products, arithmetic and copies ran while one was open for 0% of the time, Pallas kernels for 4%

profile of v4, /device:TPU:1, one launch (start us, length us, event | category | flops | bytes accessed | tf_op | source)
XLA Modules:
  0.0 98.0 jit_solution(8249538074032303054)
XLA Ops:
  0.6 1.6 %shard_map.102 = bf16[32,16,128]{2,1,0:T(8,128)(2,1)} custom-call(s32[16,32]{1,0:T(8,128)} %bitcast.8, f32[4,128]{1,0:T(4,128)} %bitcast.10), custom_call_target="tpu_custom_call" | custom-call | flops 1048576 | bytes 4096 | tf_op jit(solution)/shard_map/pallas_call | solution.py:248
  2.3 0.0 copy-start
  2.3 0.0 copy-start.3
  2.3 0.0 copy-start.4
  2.3 13.9 %all-to-all-start = ((bf16[32,16,128]{2,1,0:T(8,128)(2,1)}), bf16[32,16,128]{2,1,0:T(8,128)(2,1)S(1)}, u32[]{:S(2)}, u32[]{:S(2)}) async-start(bf16[32,16,128]{2,1,0:T(8,128)(2,1)} %shard_map.102), calls=%async_computation | async-start | bytes 262144 | tf_op jit(solution)/shard_map/all_to_all | solution.py:264
  16.2 0.0 copy-start.1
  16.2 0.0 copy-start.5
  16.2 0.0 copy-start.6
  16.2 0.0 copy-done
  16.2 0.0 copy-done.3
  16.2 0.0 copy-done.4
  16.2 0.6 copy-done.1
  16.9 0.0 copy-done.5
  16.9 1.0 %copy-done.2 = f32[512,256]{1,0:T(8,128)S(1)} copy-done((f32[512,256]{1,0:T(8,128)S(1)}, f32[512,256]{1,0:T(8,128)}, u32[]{:S(2)}) %copy-start.2) | copy-done | bytes 524312
  17.9 2.4 %shard_map.103 = (bf16[512,256]{1,0:T(8,128)(2,1)S(1)}, bf16[256,512]{1,0:T(8,128)(2,1)S(1)}, f32[256,1]{1,0:T(8,128)S(1)}, s32[16,32]{1,0:T(8,128)S(1)}, f32[51...) custom-call(s32[39,256]{1,0:T(8,128)S(1)} %bitcast.12, ...), custom_call_target="tpu_custom_call" | custom-call | flops 1073741824 | bytes 602240 | tf_op jit(solution)/shard_map/pallas_call | solution.py:248
  20.3 5.0 %all-to-all-done.got_ref = bf16[32,16,128]{2,1,0:T(8,128)(2,1)S(1)} async-done(((bf16[32,16,128]{2,1,0:T(8,128)(2,1)}), bf16[32,16,128]{2,1,0:T(8,128)(2,1)S(1)}, u32[]{:S(2)}, u32[]{:S(2)}) %all-to-all-start) | async-done | bytes 131104 | tf_op jit(solution)/shard_map/all_to_all | solution.py:264
  25.3 1.2 %shard_map.104 = bf16[32,16,256]{2,1,0:T(8,128)(2,1)} custom-call(bf16[32,16,128]{2,1,0:T(8,128)(2,1)S(1)} %all-to-all-done.got_ref, bf16[512,256]{1,0:T(8,128)(2,1)S(1)} %get-tuple-element.19.narrow_ref), custom_call_target="tpu_custom_call" | custom-call | flops 268435456 | bytes 393216 | tf_op jit(solution)/shard_map/pallas_call | solution.py:248
  26.5 4.2 %all-to-all-start.1 = ((bf16[32,16,256]{2,1,0:T(8,128)(2,1)}), bf16[32,16,256]{2,1,0:T(8,128)(2,1)S(1)}, u32[]{:S(2)}, u32[]{:S(2)}) async-start(bf16[32,16,256]{2,1,0:T(8,128)(2,1)} %shard_map.104), calls=%async_computation.1 | async-start | bytes 524288 | tf_op jit(solution)/shard_map/all_to_all | solution.py:264
  30.7 3.4 %all_gather.9.both_ref = bf16[64,16,128]{2,1,0:T(8,128)(2,1)S(1)} all-gather(bf16[32,16,128]{2,1,0:T(8,128)(2,1)S(1)} %all-to-all-done.got_ref), channel_id=1, replica_groups=mesh['server'=32,'y'=8,'core'=2] {'core'}, dimensions={0}, use_global_device_ids=true | all-gather | bytes 393216 | tf_op jit(solution)/shard_map/all_gather | solution.py:306
  34.1 0.8 shard_map.105
  35.0 5.4 %all-to-all-done.1.rows_ref = bf16[32,16,256]{2,1,0:T(8,128)(2,1)S(1)} async-done(((bf16[32,16,256]{2,1,0:T(8,128)(2,1)}), bf16[32,16,256]{2,1,0:T(8,128)(2,1)S(1)}, u32[]{:S(2)}, u32[]{:S(2)}) %all-to-all-start.1) | async-done | bytes 262176 | tf_op jit(solution)/shard_map/all_to_all | solution.py:264
  40.4 1.1 %shard_map.106 = bf16[32,16,384]{2,1,0:T(8,128)(2,1)S(1)} custom-call(bf16[32,16,256]{2,1,0:T(8,128)(2,1)S(1)} %all-to-all-done.1.rows_ref, bf16[256,512]{1,0:T(8,128)(2,1)S(1)} %get-tuple-element.20.counts_ref, bf16[512,256]{1,0:T(8,128)(2,1)S(1)} %get-tuple-element.21.counts_t_ref, f32[256,1]{1,0:T(8,128)S(1)} %get-tuple-element.22.clicks_ref, ...), custom_call_target="tpu_custom_call" | custom-call | flops 268435456 | bytes 918528 | tf_op jit(solution)/shard_map/pallas_call | solution.py:248
  41.5 15.9 %all_to_all.25 = bf16[32,16,384]{2,1,0:T(8,128)(2,1)S(1)} all-to-all(bf16[32,16,384]{2,1,0:T(8,128)(2,1)S(1)} %shard_map.106), channel_id=1, replica_groups=mesh['server'=32,'y'=8,'core'=2] {'server'}, dimensions={0} | all-to-all | bytes 786432 | tf_op jit(solution)/shard_map/all_to_all | solution.py:264
  57.4 7.2 %all_gather.10.push_ref = bf16[64,16,384]{2,1,0:T(8,128)(2,1)S(1)} all-gather(bf16[32,16,384]{2,1,0:T(8,128)(2,1)S(1)} %all_to_all.25), channel_id=1, replica_groups=mesh['server'=32,'y'=8,'core'=2] {'core'}, dimensions={0}, use_global_device_ids=true | all-gather | bytes 1179648 | tf_op jit(solution)/shard_map/all_gather | solution.py:326
  64.6 0.6 shard_map.107
  65.2 14.9 %all_to_all.26.part_ref = bf16[8,72,128]{2,1,0:T(8,128)(2,1)S(1)} all-to-all(bf16[8,72,128]{2,1,0:T(8,128)(2,1)S(1)} %shard_map.107), channel_id=1, replica_groups=mesh['server'=32,'y'=8,'core'=2] {'y'}, dimensions={0} | all-to-all | bytes 294912 | tf_op jit(solution)/shard_map/all_to_all | solution.py:264
  80.2 0.7 shard_map.108
  80.9 3.4 %all-to-all-start.4 = ((bf16[8,72,128]{2,1,0:T(8,128)(2,1)}), bf16[8,72,128]{2,1,0:T(8,128)(2,1)S(1)}, u32[]{:S(2)}, u32[]{:S(2)}) async-start(bf16[8,72,128]{2,1,0:T(8,128)(2,1)} %shard_map.108), calls=%async_computation.4 | async-start | bytes 294912 | tf_op jit(solution)/shard_map/all_to_all | solution.py:264
  84.3 0.6 shard_map.110
  84.9 7.5 %all-to-all-done.4 = bf16[8,72,128]{2,1,0:T(8,128)(2,1)S(1)} async-done(((bf16[8,72,128]{2,1,0:T(8,128)(2,1)}), bf16[8,72,128]{2,1,0:T(8,128)(2,1)S(1)}, u32[]{:S(2)}, u32[]{:S(2)}) %all-to-all-start.4) | async-done | bytes 147488 | tf_op jit(solution)/shard_map/all_to_all | solution.py:264
  92.4 4.8 %all_gather.11.delta_ref = bf16[16,72,128]{2,1,0:T(8,128)(2,1)S(1)} all-gather(bf16[8,72,128]{2,1,0:T(8,128)(2,1)S(1)} %all-to-all-done.4), channel_id=1, replica_groups=mesh['server'=32,'y'=8,'core'=2] {'core'}, dimensions={0}, use_global_device_ids=true | all-gather | bytes 442368 | tf_op jit(solution)/shard_map/all_gather | solution.py:334
  97.2 0.9 shard_map.109
  (2 shorter events, 0.0 us)
Async XLA Ops:
  2.3 13.9 %copy-start = (s32[32,16]{0,1:T(8,128)S(1)}, s32[32,16]{0,1:T(8,128)}, u32[]{:S(2)}) copy-start(s32[32,16]{0,1:T(8,128)} %param.12) | copy-start | bytes 6148
  2.3 13.9 %copy-start.3 = (s32[256,39]{0,1:T(8,128)S(1)}, s32[256,39]{0,1:T(8,128)}, u32[]{:S(2)}) copy-start(s32[256,39]{0,1:T(8,128)} %param.11) | copy-start | bytes 119812
  2.3 13.9 %copy-start.4 = (f32[32,256]{1,0:T(8,128)S(1)}, f32[32,256]{1,0:T(8,128)}, u32[]{:S(2)}) copy-start(f32[32,256]{1,0:T(8,128)} %acc_in.1) | copy-start | bytes 98308
  2.3 23.0 %all-to-all-start = ((bf16[32,16,128]{2,1,0:T(8,128)(2,1)}), bf16[32,16,128]{2,1,0:T(8,128)(2,1)S(1)}, u32[]{:S(2)}, u32[]{:S(2)}) async-start(bf16[32,16,128]{2,1,0:T(8,128)(2,1)} %shard_map.102), calls=%async_computation | async-start | bytes 262144 | tf_op jit(solution)/shard_map/all_to_all | solution.py:264
  16.2 0.7 copy-start.1
  16.2 0.7 copy-start.5
  16.2 0.7 copy-start.6
  16.9 1.0 %copy-start.2 = (f32[512,256]{1,0:T(8,128)S(1)}, f32[512,256]{1,0:T(8,128)}, u32[]{:S(2)}) copy-start(f32[512,256]{1,0:T(8,128)} %factors_in.1) | copy-start | bytes 1572868
  26.5 13.9 %all-to-all-start.1 = ((bf16[32,16,256]{2,1,0:T(8,128)(2,1)}), bf16[32,16,256]{2,1,0:T(8,128)(2,1)S(1)}, u32[]{:S(2)}, u32[]{:S(2)}) async-start(bf16[32,16,256]{2,1,0:T(8,128)(2,1)} %shard_map.104), calls=%async_computation.1 | async-start | bytes 524288 | tf_op jit(solution)/shard_map/all_to_all | solution.py:264
  80.9 11.5 %all-to-all-start.4 = ((bf16[8,72,128]{2,1,0:T(8,128)(2,1)}), bf16[8,72,128]{2,1,0:T(8,128)(2,1)S(1)}, u32[]{:S(2)}, u32[]{:S(2)}) async-start(bf16[8,72,128]{2,1,0:T(8,128)(2,1)} %shard_map.108), calls=%async_computation.4 | async-start | bytes 294912 | tf_op jit(solution)/shard_map/all_to_all | solution.py:264

commit v5 on v4

--- a/solution.py
+++ b/solution.py
@@ -14,7 +14,6 @@
 SLOTS = OWNERS * CAP
 ROWS = 512
 K = 256
-WIDE = K + 128
 SAMPLES = 256
 FIELDS = 39
 N_Y = 8
@@ -52,14 +51,15 @@
     return (iota(dims, axis) < 2 * CAP).astype(f32).astype(bf16)
 
 
-def ask_kernel(req_t_hbm, lin_hbm, out_ref, req_t_ref, lin_ref, sems):
+def ask_kernel(req_t_hbm, lin_hbm, factors_hbm, out_ref, factors_ref, req_t_ref, lin_ref, sems):
     copies = [
         pltpu.make_async_copy(req_t_hbm, req_t_ref, sems.at[0]),
         pltpu.make_async_copy(lin_hbm, lin_ref, sems.at[1]),
+        pltpu.make_async_copy(factors_hbm, factors_ref, sems.at[2]),
     ]
     for copy in copies:
         copy.start()
-    for copy in copies:
+    for copy in copies[:2]:
         copy.wait()
     lists = own_lists(req_t_ref[...])
     spread = (jnp.right_shift(iota((CAP, 4), 0), 1) == iota((CAP, 4), 1)).astype(f32).astype(bf16)
@@ -68,34 +68,50 @@
     lin = jnp.where(odd, lin, pltpu.roll(lin, 64, 1))
     lin = jnp.where(iota((CAP, 128), 1) >= 64, lin, 0.0)
     out_ref[...] = (lists.reshape(OWNERS, CAP, 128) + lin[None]).astype(bf16)
-
-
-def prep_kernel(
+    copies[2].wait()
+
+
+def of_share():
+    return jnp.bitwise_and(iota((SHARE, 128), 1), SHARE - 1) == iota((SHARE, 128), 0)
+
+
+def gather_kernel(got_ref, factors_ref, out_ref):
+    asked = dot(got_ref[...].reshape(SLOTS, 128), ones((128, ROWS), 0))
+    hot = (asked == iota((SLOTS, ROWS), 1).astype(f32)).astype(f32).astype(bf16)
+    out_ref[...] = dot(hot, factors_ref[...].astype(bf16)).astype(bf16).reshape(OWNERS, CAP, K)
+
+
+def side_kernel(
+    got_ref,
+    both_ref,
+    req_t_ref,
     fs_t_ref,
     clicks_ref,
-    req_t_in,
-    factors_in,
     acc_in,
     acc_lin_row_ref,
     linear_in,
+    lin_ref,
+    hot_t_ref,
     counts_t_ref,
     counts_ref,
     clicks_col_ref,
-    req_t_ref,
-    factors_ref,
-    narrow_ref,
     acc_ref,
     acc_lin_ref,
     linear_ref,
 ):
-    for here, there in (
-        (req_t_in, req_t_ref),
-        (factors_in, factors_ref),
-        (acc_in, acc_ref),
-        (linear_in, linear_ref),
-    ):
-        there[...] = here[...]
-    narrow_ref[...] = factors_in[...].astype(bf16)
+    acc_ref[...] = acc_in[...]
+    linear_ref[...] = linear_in[...]
+    got = got_ref[...].reshape(SLOTS, 128)
+    wanted = dot(own_lists(req_t_ref[...]).astype(bf16), ones((128, SLOTS), 0)).astype(jnp.int32)
+    first = jnp.bitwise_and(iota((SLOTS, SLOTS), 0), -CAP)
+    pick = iota((SLOTS, SLOTS), 1) == first + jnp.right_shift(wanted, 6)
+    values = dot(pick.astype(f32).astype(bf16), got)
+    here = iota((SLOTS, 128), 1) == jnp.bitwise_and(wanted[:, :128], 63) + 64
+    lin_ref[...] = jnp.where(here, values, 0.0).astype(bf16)
+
+    asked_t = dot(ones((ROWS, 128), 1), both_ref[...].reshape(N_CORE * SLOTS, 128), 1, 1)
+    hot = asked_t == iota((ROWS, N_CORE * SLOTS), 0).astype(f32)
+    hot_t_ref[...] = hot.astype(f32).astype(bf16)
     same_share = iota((SHARE, SHARE), 0) == iota((SHARE, SHARE), 1)
     acc_lin = jnp.sum(jnp.where(same_share, acc_lin_row_ref[...], 0.0), axis=1, keepdims=True)
     acc_lin_ref[...] = jnp.sum(jnp.where(of_share(), acc_lin, 0.0), axis=0, keepdims=True)
@@ -115,29 +131,6 @@
     same = iota((SAMPLES, SAMPLES), 0) == iota((SAMPLES, SAMPLES), 1)
     clicks = clicks_ref[...].astype(f32)
     clicks_col_ref[...] = jnp.sum(jnp.where(same, clicks, 0.0), axis=1, keepdims=True)
-
-
-def of_share():
-    return jnp.bitwise_and(iota((SHARE, 128), 1), SHARE - 1) == iota((SHARE, 128), 0)
-
-
-def gather_kernel(got_ref, narrow_ref, out_ref):
-    asked = dot(got_ref[...].reshape(SLOTS, 128), ones((128, ROWS), 0))
-    hot = (asked == iota((SLOTS, ROWS), 1).astype(f32)).astype(f32).astype(bf16)
-    out_ref[...] = dot(hot, narrow_ref[...]).astype(bf16).reshape(OWNERS, CAP, K)
-
-
-def side_kernel(got_ref, both_ref, req_t_ref, lin_ref, hot_t_ref):
-    got = got_ref[...].reshape(SLOTS, 128)
-    wanted = dot(own_lists(req_t_ref[...]).astype(bf16), ones((128, SLOTS), 0)).astype(jnp.int32)
-    first = jnp.bitwise_and(iota((SLOTS, SLOTS), 0), -CAP)
-    pick = iota((SLOTS, SLOTS), 1) == first + jnp.right_shift(wanted, 6)
-    values = dot(pick.astype(f32).astype(bf16), got)
-    here = iota((SLOTS, 128), 1) == jnp.bitwise_and(wanted[:, :128], 63) + 64
-    lin_ref[...] = jnp.where(here, values, 0.0).astype(bf16)
-    asked_t = dot(ones((ROWS, 128), 1), both_ref[...].reshape(N_CORE * SLOTS, 128), 1, 1)
-    hot = asked_t == iota((ROWS, N_CORE * SLOTS), 0).astype(f32)
-    hot_t_ref[...] = hot.astype(f32).astype(bf16)
 
 
 def learn_kernel(rows_ref, counts_ref, counts_t_ref, clicks_ref, lin_ref, out_ref):
@@ -158,12 +151,20 @@
     counts_t = counts_t_ref[...]
     error_sums = dot(counts_t, first) + dot(counts_t, second)
     grads = dot(counts_t, weighted) - error_sums * wide_rows
-    out_ref[:, :, :K] = grads.astype(bf16).reshape(OWNERS, CAP, K)
-    total = error_sums[:, :128]
-    lane = iota((SLOTS, 128), 1)
-    first = total.astype(bf16).astype(f32)
-    linear = jnp.where(lane == 0, first, jnp.where(lane == 1, total - first, 0.0))
-    out_ref[:, :, K:] = linear.astype(bf16).reshape(OWNERS, CAP, 128)
+    grads = grads.astype(bf16)
+    out_ref[:, :CAP, :] = grads[:, :128].reshape(OWNERS, CAP, 128)
+    out_ref[:, CAP : 2 * CAP, :] = grads[:, 128:].reshape(OWNERS, CAP, 128)
+    place = lax.rem(lax.axis_index("server"), 8)
+    sums_row = (dot(first[:, :128], counts, 0, 0) + dot(second[:, :128], counts, 0, 0))[:8]
+    high = sums_row.astype(bf16).astype(f32)
+    row = iota((8, SLOTS), 0)
+    sums_row = jnp.where(row == 0, high, jnp.where(row == 1, sums_row - high, 0.0))
+    mine = jnp.right_shift(iota((8, 128), 1), 4) == place
+    for owner in range(OWNERS):
+        lanes = owner // 8 * 128
+        turn = lax.rem(place + 8 - owner % 8, 8) * CAP
+        tile = pltpu.roll(sums_row[:, lanes : lanes + 128], turn, 1)
+        out_ref[owner, 2 * CAP :, :] = jnp.where(mine, tile, 0.0).astype(bf16)
 
 
 def part_rows(x):
@@ -178,14 +179,22 @@
 
 def scatter_kernel(push_ref, hot_t_ref, out_ref):
     core = lax.axis_index("core")
-    pushed = push_ref[...].reshape(N_CORE * SLOTS, WIDE)
+    left = push_ref[:, :CAP, :].reshape(N_CORE * SLOTS, 128)
+    right = push_ref[:, CAP : 2 * CAP, :].reshape(N_CORE * SLOTS, 128)
     shares = [
         hot_t_ref[pl.ds(pl.multiple_of((y * N_CORE + core) * SHARE, SHARE), SHARE), :] for y in range(N_Y)
     ]
-    total = dot(jnp.concatenate(shares, axis=0), pushed[:, :K]).astype(bf16)
+    total = dot(jnp.concatenate(shares, axis=0), jnp.concatenate([left, right], axis=1)).astype(bf16)
     out_ref[:, :SHARE, :] = total[:, :128].reshape(N_Y, SHARE, 128)
     out_ref[:, SHARE : 2 * SHARE, :] = total[:, 128:].reshape(N_Y, SHARE, 128)
-    linear = part_rows(jnp.sum(dot(pushed[:, K:], hot_t_ref[...], 0, 1), axis=0, keepdims=True))
+    chunks = []
+    for q in range(N_CORE * OWNERS // 8):
+        chunk = push_ref[8 * q, 2 * CAP :, :].astype(f32)
+        for i in range(1, 8):
+            chunk = chunk + push_ref[8 * q + i, 2 * CAP :, :].astype(f32)
+        chunks.append(chunk.astype(bf16))
+    linear = dot(jnp.concatenate(chunks, axis=1), hot_t_ref[...], 1, 1)
+    linear = part_rows(jnp.sum(linear, axis=0, keepdims=True))
     for y in range(N_Y):
         lanes = y // 2 * 128
         out_ref[y, 2 * SHARE :, :] = linear[:, lanes : lanes + 128]
@@ -220,7 +229,7 @@
         delta_ref[y, 2 * SHARE :, :] = linear
 
 
-def state_kernel(part_ref, acc_ref, acc_lin_ref, new_acc_ref, new_acc_lin_ref):
+def write_state(part_ref, acc_ref, acc_lin_ref, new_acc_ref, new_acc_lin_ref):
     left, right, linear = add_parts(part_ref)
     new_acc_ref[:, :128] = acc_ref[:, :128] + left * left
     new_acc_ref[:, 128:] = acc_ref[:, 128:] + right * right
@@ -230,7 +239,19 @@
     new_acc_lin_ref[...] = jnp.sum(jnp.where(same, column, 0.0), axis=0, keepdims=True)
 
 
-def apply_kernel(delta_ref, factors_ref, linear_ref, new_factors_ref, new_linear_ref):
+def apply_kernel(
+    delta_ref,
+    factors_ref,
+    linear_ref,
+    part_ref,
+    acc_ref,
+    acc_lin_ref,
+    new_factors_ref,
+    new_linear_ref,
+    new_acc_ref,
+    new_acc_lin_ref,
+):
+    write_state(part_ref, acc_ref, acc_lin_ref, new_acc_ref, new_acc_lin_ref)
     for q in range(4):
         lin = jnp.zeros((8, 128), f32)
         for w in range(4 * q, 4 * q + 4):
@@ -245,13 +266,15 @@
 
 def call(kernel, out, flops, *args, scratch=(), far=False):
     size = sum(a.size * a.dtype.itemsize for a in args)
+    if far:
+        args = [pltpu.with_memory_space_constraint(a, pltpu.HBM) for a in args]
     return pl.pallas_call(
         kernel,
         out_shape=out,
         in_specs=[pl.BlockSpec(memory_space=pltpu.HBM if far else pltpu.VMEM)] * len(args),
         out_specs=jax.tree.map(lambda _: pl.BlockSpec(memory_space=pltpu.VMEM), out),
         scratch_shapes=scratch,
-        compiler_params=pltpu.CompilerParams(vmem_limit_bytes=None if far else 24 * 1024 * 1024),
+        compiler_params=pltpu.CompilerParams(vmem_limit_bytes=24 * 1024 * 1024),
         cost_estimate=pl.CostEstimate(flops=flops, bytes_accessed=size, transcendentals=0),
     )(*args)
 
@@ -269,52 +292,46 @@
 
 def body(factors, linear, acc_factors, acc_linear, feature_slot, requests, clicks):
     dma = pltpu.SemaphoreType.DMA
-    ask = call(
+    req_t = requests.T
+    ask, wide = call(
         ask_kernel,
-        shape((OWNERS, CAP, 128), bf16),
+        [shape((OWNERS, CAP, 128), bf16), shape((ROWS, K), f32)],
         1 << 20,
-        requests.T,
+        req_t,
         linear.reshape(4, 128),
-        scratch=[pltpu.VMEM((CAP, OWNERS), jnp.int32), pltpu.VMEM((4, 128), f32), dma((2,))],
+        factors,
+        scratch=[pltpu.VMEM((CAP, OWNERS), jnp.int32), pltpu.VMEM((4, 128), f32), dma((3,))],
         far=True,
     )
     got = exchange(ask, "server")
-    counts_t, counts, clicks_col, req_t, wide, narrow, acc, acc_lin, lin_row = call(
-        prep_kernel,
+    found = call(gather_kernel, shape((OWNERS, CAP, K), bf16), 1 << 28, got, wide)
+    rows = exchange(found, "server")
+    both = lax.all_gather(got, "core", axis=0, tiled=True)
+    lin_terms, hot_t, counts_t, counts, clicks_col, acc, acc_lin, lin_row = call(
+        side_kernel,
         [
+            shape((SLOTS, 128), bf16),
+            shape((ROWS, N_CORE * SLOTS), bf16),
             shape((SLOTS, SAMPLES), bf16),
             shape((SAMPLES, SLOTS), bf16),
             shape((SAMPLES, 1), f32),
-            shape((CAP, OWNERS), jnp.int32),
-            shape((ROWS, K), f32),
-            shape((ROWS, K), bf16),
             shape((SHARE, K), f32),
             shape((1, 128), f32),
             shape((1, ROWS), f32),
         ],
         1 << 30,
+        got,
+        both,
+        req_t,
         feature_slot.T,
         clicks.reshape(1, SAMPLES),
-        requests.T,
-        factors,
         acc_factors,
         acc_linear.reshape(1, SHARE),
         linear.reshape(1, ROWS),
     )
-    found = call(gather_kernel, shape((OWNERS, CAP, K), bf16), 1 << 28, got, narrow)
-    rows = exchange(found, "server")
-    both = lax.all_gather(got, "core", axis=0, tiled=True)
-    lin_terms, hot_t = call(
-        side_kernel,
-        [shape((SLOTS, 128), bf16), shape((ROWS, N_CORE * SLOTS), bf16)],
-        1 << 28,
-        got,
-        both,
-        req_t,
-    )
     push = call(
         learn_kernel,
-        shape((OWNERS, CAP, WIDE), bf16),
+        shape((OWNERS, 2 * CAP + 8, 128), bf16),
         1 << 28,
         rows,
         counts,
@@ -324,16 +341,23 @@
     )
     pushed = exchange(push, "server")
     pushed = lax.all_gather(pushed, "core", axis=0, tiled=True)
-    dense = call(scatter_kernel, shape((N_Y, TALL, 128), bf16), 1 << 28, pushed, hot_t)
+    dense = call(
+        scatter_kernel, shape((N_Y, TALL, 128), bf16), 1 << 28, pushed, hot_t
+    )
     shared = exchange(dense, "y")
     delta = call(update_kernel, shape((N_Y, TALL, 128), bf16), 1 << 20, shared, acc, acc_lin)
     deltas = exchange(delta, "y")
-    new_acc, new_acc_lin = call(
-        state_kernel, [shape((SHARE, K), f32), shape((1, SHARE), f32)], 1 << 20, shared, acc, acc_lin
-    )
     deltas = lax.all_gather(deltas, "core", axis=0, tiled=True)
-    new_factors, new_linear = call(
-        apply_kernel, [shape((ROWS, K), f32), shape((1, ROWS), f32)], 1 << 20, deltas, wide, lin_row
+    new_factors, new_linear, new_acc, new_acc_lin = call(
+        apply_kernel,
+        [shape((ROWS, K), f32), shape((1, ROWS), f32), shape((SHARE, K), f32), shape((1, SHARE), f32)],
+        1 << 20,
+        deltas,
+        wide,
+        lin_row,
+        shared,
+        acc,
+        acc_lin,
     )
     return new_factors, new_linear.reshape(ROWS), new_acc, new_acc_lin.reshape(SHARE)
 

time: 98.6 us -> 96 us (0.974)
  blocking collectives: 46.2 us -> 80.3 us
  starting transfers between devices: 21.4 us -> 3.87 us
  waiting for transfers between devices: 17.9 us -> 1.96 us
  Pallas kernels: 9.97 us -> 7.98 us
  local copies, waits for them, and re-layouts: 1.71 us -> 0.69 us
    all_to_all x2 -> x4, blocking collectives: 30.8 us -> 66 us  [exchange(): return lax.all_to_all(x, axis, split_axis=0, concat_axis=0, tiled=True)]
    all_to_all x3 -> x1, starting transfers between devices: 21.4 us -> 3.87 us  [exchange(): return lax.all_to_all(x, axis, split_axis=0, concat_axis=0, tiled=True)]
    all_to_all x3 -> x1, waiting for transfers between devices: 17.9 us -> 1.96 us  [exchange(): return lax.all_to_all(x, axis, split_axis=0, concat_axis=0, tiled=True)]
    pallas_call x9 -> x7, Pallas kernels: 9.97 us -> 7.98 us  [call(): pl.pallas_call(kernel, out_shape=out, in_specs=[pl.BlockSpec(memory_space...]
    all_gather x1, blocking collectives: 7.22 us -> 5.7 us  [body(): pushed = lax.all_gather(pushed, 'core', axis=0, tiled=True)]
    unnamed x14 -> x12, local copies, waits for them, and re-layouts: 1.71 us -> 0.69 us
  transfers between devices with their start and end apart: 3 -> 1, of which waited for: 3 -> 1; matrix products, arithmetic and copies ran while one was open for 0% -> 0% of each run, Pallas kernels for 4% -> 3%
where the time goes in v5:
time: 96 us; the launch traced here: 95.5 us
  blocking collectives  80.3 us (84%)
  Pallas kernels  7.98 us (8%)
  starting transfers between devices  3.87 us (4%)
  waiting for transfers between devices  1.96 us (2%)
    all_to_all x4, blocking collectives, exchange(): return lax.all_to_all(x, axis, split_axis=0, concat_axis=0, tiled=True)  66 us
    pallas_call x7, Pallas kernels, call(): pl.pallas_call(kernel, out_shape=out, in_specs=[pl.BlockSpec(memory_space...  7.98 us
    all_gather x1, blocking collectives, body(): pushed = lax.all_gather(pushed, 'core', axis=0, tiled=True)  5.7 us
    all_gather x1, blocking collectives, body(): deltas = lax.all_gather(deltas, 'core', axis=0, tiled=True)  4.77 us
    all_to_all x1, starting transfers between devices, exchange(): return lax.all_to_all(x, axis, split_axis=0, concat_axis=0, tiled=True)  3.87 us
    all_gather x1, blocking collectives, body(): both = lax.all_gather(got, 'core', axis=0, tiled=True)  3.84 us
    all_to_all x1, waiting for transfers between devices, exchange(): return lax.all_to_all(x, axis, split_axis=0, concat_axis=0, tiled=True)  1.96 us
  transfers between devices with their start and end apart: 1, of which 1 were waited for; matrix products, arithmetic and copies ran while one was open for 0% of the time, Pallas kernels for 3%

profile of v5, /device:TPU:1, one launch (start us, length us, event | category | flops | bytes accessed | tf_op | source)
XLA Modules:
  0.0 95.5 jit_solution(15835313306718437529)
XLA Ops:
  0.6 1.1 %shard_map.102 = (bf16[32,16,128]{2,1,0:T(8,128)(2,1)S(1)}, f32[512,256]{1,0:T(8,128)S(1)}) custom-call(s32[16,32]{1,0:T(8,128)} %bitcast.8, f32[4,128]{1,0:T(4,128)} %bitcast.10, f32[512,256]{1,0:T(8,128)} %factors_hbm.1), custom_call_target="tpu_custom_call" | custom-call | flops 1048576 | bytes 528384 | tf_op jit(solution)/shard_map/pallas_call | solution.py:271
  1.7 22.7 %all_to_all.25.got_ref = bf16[32,16,128]{2,1,0:T(8,128)(2,1)S(1)} all-to-all(bf16[32,16,128]{2,1,0:T(8,128)(2,1)S(1)} %get-tuple-element.18), channel_id=1, replica_groups=mesh['server'=32,'y'=8,'core'=2] {'server'}, dimensions={0} | all-to-all | bytes 262144 | tf_op jit(solution)/shard_map/all_to_all | solution.py:287
  24.4 1.2 %shard_map.103 = bf16[32,16,256]{2,1,0:T(8,128)(2,1)} custom-call(bf16[32,16,128]{2,1,0:T(8,128)(2,1)S(1)} %all_to_all.25.got_ref, f32[512,256]{1,0:T(8,128)S(1)} %get-tuple-element.19.factors_ref), custom_call_target="tpu_custom_call" | custom-call | flops 268435456 | bytes 655360 | tf_op jit(solution)/shard_map/pallas_call | solution.py:271
  25.6 3.9 %all-to-all-start.1 = ((bf16[32,16,256]{2,1,0:T(8,128)(2,1)}), bf16[32,16,256]{2,1,0:T(8,128)(2,1)S(1)}, u32[]{:S(2)}, u32[]{:S(2)}) async-start(bf16[32,16,256]{2,1,0:T(8,128)(2,1)} %shard_map.103), calls=%async_computation.1 | async-start | bytes 524288 | tf_op jit(solution)/shard_map/all_to_all | solution.py:287
  29.5 0.0 copy-start
  29.5 0.0 copy-start.2
  29.5 0.0 copy-start.3
  29.5 3.8 %all_gather.9.both_ref = bf16[64,16,128]{2,1,0:T(8,128)(2,1)S(1)} all-gather(bf16[32,16,128]{2,1,0:T(8,128)(2,1)S(1)} %all_to_all.25.got_ref), channel_id=1, replica_groups=mesh['server'=32,'y'=8,'core'=2] {'core'}, dimensions={0}, use_global_device_ids=true | all-gather | bytes 393216 | tf_op jit(solution)/shard_map/all_gather | solution.py:309
  33.4 0.0 copy-start.1
  33.4 0.0 copy-start.4
  33.4 0.0 copy-start.5
  33.4 0.0 copy-done
  33.4 0.0 copy-done.2
  33.4 0.0 copy-done.3
  33.4 0.7 copy-done.1
  34.1 0.0 copy-done.4
  34.1 0.0 copy-done.5
  34.1 3.1 %shard_map.104 = (bf16[512,128]{1,0:T(8,128)(2,1)S(1)}, bf16[512,1024]{1,0:T(8,128)(2,1)S(1)}, bf16[512,256]{1,0:T(8,128)(2,1)S(1)}, bf16[256,512]{1,0:T(8,128)(...) custom-call(bf16[32,16,128]{2,1,0:T(8,128)(2,1)S(1)} %all_to_all.25.got_re, ...), custom_call_target="tpu_custom_call" | custom-call | flops 1073741824 | bytes 471168 | tf_op jit(solution)/shard_map/pallas_call | solution.py:271
  37.2 2.0 %all-to-all-done.1.rows_ref = bf16[32,16,256]{2,1,0:T(8,128)(2,1)S(1)} async-done(((bf16[32,16,256]{2,1,0:T(8,128)(2,1)}), bf16[32,16,256]{2,1,0:T(8,128)(2,1)S(1)}, u32[]{:S(2)}, u32[]{:S(2)}) %all-to-all-start.1) | async-done | bytes 262176 | tf_op jit(solution)/shard_map/all_to_all | solution.py:287
  39.2 1.1 %shard_map.105 = bf16[32,40,128]{2,1,0:T(8,128)(2,1)S(1)} custom-call(bf16[32,16,256]{2,1,0:T(8,128)(2,1)S(1)} %all-to-all-done.1.rows_ref, bf16[256,512]{1,0:T(8,128)(2,1)S(1)} %get-tuple-element.20.counts_ref, bf16[512,256]{1,0:T(8,128)(2,1)S(1)} %get-tuple-element.21.counts_t_ref, f32[256,1]{1,0:T(8,128)S(1)} %get-tuple-element.22.clicks_ref, ...), custom_call_target="tpu_custom_call" | custom-call | flops 268435456 | bytes 918528 | tf_op jit(solution)/shard_map/pallas_call | solution.py:271
  40.2 17.8 %all_to_all.26 = bf16[32,40,128]{2,1,0:T(8,128)(2,1)S(1)} all-to-all(bf16[32,40,128]{2,1,0:T(8,128)(2,1)S(1)} %shard_map.105), channel_id=1, replica_groups=mesh['server'=32,'y'=8,'core'=2] {'server'}, dimensions={0} | all-to-all | bytes 655360 | tf_op jit(solution)/shard_map/all_to_all | solution.py:287
  58.1 5.7 %all_gather.10.push_ref = bf16[64,40,128]{2,1,0:T(8,128)(2,1)S(1)} all-gather(bf16[32,40,128]{2,1,0:T(8,128)(2,1)S(1)} %all_to_all.26), channel_id=1, replica_groups=mesh['server'=32,'y'=8,'core'=2] {'core'}, dimensions={0}, use_global_device_ids=true | all-gather | bytes 983040 | tf_op jit(solution)/shard_map/all_gather | solution.py:343
  63.8 0.5 shard_map.106
  64.3 14.9 %all_to_all.27.part_ref = bf16[8,72,128]{2,1,0:T(8,128)(2,1)S(1)} all-to-all(bf16[8,72,128]{2,1,0:T(8,128)(2,1)S(1)} %shard_map.106), channel_id=1, replica_groups=mesh['server'=32,'y'=8,'core'=2] {'y'}, dimensions={0} | all-to-all | bytes 294912 | tf_op jit(solution)/shard_map/all_to_all | solution.py:287
  79.2 0.1 shard_map.107
  79.3 10.6 %all_to_all.28 = bf16[8,72,128]{2,1,0:T(8,128)(2,1)S(1)} all-to-all(bf16[8,72,128]{2,1,0:T(8,128)(2,1)S(1)} %shard_map.107), channel_id=1, replica_groups=mesh['server'=32,'y'=8,'core'=2] {'y'}, dimensions={0} | all-to-all | bytes 294912 | tf_op jit(solution)/shard_map/all_to_all | solution.py:287
  89.9 4.8 %all_gather.11.delta_ref = bf16[16,72,128]{2,1,0:T(8,128)(2,1)S(1)} all-gather(bf16[8,72,128]{2,1,0:T(8,128)(2,1)S(1)} %all_to_all.28), channel_id=1, replica_groups=mesh['server'=32,'y'=8,'core'=2] {'core'}, dimensions={0}, use_global_device_ids=true | all-gather | bytes 442368 | tf_op jit(solution)/shard_map/all_gather | solution.py:350
  94.7 0.9 shard_map.108
Async XLA Ops:
  25.6 13.5 %all-to-all-start.1 = ((bf16[32,16,256]{2,1,0:T(8,128)(2,1)}), bf16[32,16,256]{2,1,0:T(8,128)(2,1)S(1)}, u32[]{:S(2)}, u32[]{:S(2)}) async-start(bf16[32,16,256]{2,1,0:T(8,128)(2,1)} %shard_map.103), calls=%async_computation.1 | async-start | bytes 524288 | tf_op jit(solution)/shard_map/all_to_all | solution.py:287
  29.5 3.9 %copy-start = (s32[32,16]{0,1:T(8,128)S(1)}, s32[32,16]{0,1:T(8,128)}, u32[]{:S(2)}) copy-start(s32[32,16]{0,1:T(8,128)} %param.12) | copy-start | bytes 6148
  29.5 3.9 %copy-start.2 = (s32[256,39]{0,1:T(8,128)S(1)}, s32[256,39]{0,1:T(8,128)}, u32[]{:S(2)}) copy-start(s32[256,39]{0,1:T(8,128)} %param.11) | copy-start | bytes 119812
  29.5 3.9 %copy-start.3 = (f32[32,256]{1,0:T(8,128)S(1)}, f32[32,256]{1,0:T(8,128)}, u32[]{:S(2)}) copy-start(f32[32,256]{1,0:T(8,128)} %acc_in.1) | copy-start | bytes 98308
  33.4 0.7 copy-start.1
  33.4 0.7 copy-start.4
  33.4 0.7 copy-start.5

commit v6 on v5

--- a/solution.py
+++ b/solution.py
@@ -37,14 +37,21 @@
     return jnp.concatenate([high, low, pad], axis=0).astype(f32).astype(bf16)
 
 
-def own_lists(req_t):
-    owner = jnp.right_shift(iota((SLOTS, OWNERS), 0), 4)
-    mine = (owner == iota((SLOTS, OWNERS), 1)).astype(f32).astype(bf16)
+def own_lists(req_t, rows):
+    owner = jnp.right_shift(iota((OWNERS * rows, OWNERS), 0), 4 if rows == CAP else 3)
+    mine = (owner == iota((OWNERS * rows, OWNERS), 1)).astype(f32).astype(bf16)
     lists = dot(mine, split_requests(req_t), 1, 1)
-    lane = iota((SLOTS, 128), 1)
-    position = jnp.bitwise_and(iota((SLOTS, 128), 0), CAP - 1)
-    keep = (lane < 2 * CAP) & (jnp.bitwise_and(lane, CAP - 1) == position)
+    lane = iota((OWNERS * rows, 128), 1)
+    position = jnp.bitwise_and(iota((OWNERS * rows, 128), 0), rows - 1)
+    keep = (lane < 2 * CAP) & (jnp.bitwise_and(lane, rows - 1) == position)
     return jnp.where(keep, lists, 0.0)
+
+
+def one_slot_a_row(got):
+    got = got.astype(f32)
+    upper = jnp.bitwise_and(iota(got.shape, 2), 8) == 8
+    split = jnp.concatenate([jnp.where(upper, 0.0, got), jnp.where(upper, got, 0.0)], axis=1)
+    return split.astype(bf16).reshape(got.shape[0] * CAP, 128)
 
 
 def ones(dims, axis):
@@ -61,13 +68,13 @@
         copy.start()
     for copy in copies[:2]:
         copy.wait()
-    lists = own_lists(req_t_ref[...])
-    spread = (jnp.right_shift(iota((CAP, 4), 0), 1) == iota((CAP, 4), 1)).astype(f32).astype(bf16)
+    lists = own_lists(req_t_ref[...], 8)
+    spread = (jnp.right_shift(iota((8, 4), 0), 1) == iota((8, 4), 1)).astype(f32).astype(bf16)
     lin = dot(spread, lin_ref[...].astype(bf16))
-    odd = jnp.bitwise_and(iota((CAP, 128), 0), 1) == 1
+    odd = jnp.bitwise_and(iota((8, 128), 0), 1) == 1
     lin = jnp.where(odd, lin, pltpu.roll(lin, 64, 1))
-    lin = jnp.where(iota((CAP, 128), 1) >= 64, lin, 0.0)
-    out_ref[...] = (lists.reshape(OWNERS, CAP, 128) + lin[None]).astype(bf16)
+    lin = jnp.where(iota((8, 128), 1) >= 64, lin, 0.0)
+    out_ref[...] = (lists.reshape(OWNERS, 8, 128) + lin[None]).astype(bf16)
     copies[2].wait()
 
 
@@ -76,14 +83,13 @@
 
 
 def gather_kernel(got_ref, factors_ref, out_ref):
-    asked = dot(got_ref[...].reshape(SLOTS, 128), ones((128, ROWS), 0))
+    asked = dot(one_slot_a_row(got_ref[...]), ones((128, ROWS), 0))
     hot = (asked == iota((SLOTS, ROWS), 1).astype(f32)).astype(f32).astype(bf16)
     out_ref[...] = dot(hot, factors_ref[...].astype(bf16)).astype(bf16).reshape(OWNERS, CAP, K)
 
 
 def side_kernel(
     got_ref,
-    both_ref,
     req_t_ref,
     fs_t_ref,
     clicks_ref,
@@ -91,7 +97,6 @@
     acc_lin_row_ref,
     linear_in,
     lin_ref,
-    hot_t_ref,
     counts_t_ref,
     counts_ref,
     clicks_col_ref,
@@ -101,17 +106,14 @@
 ):
     acc_ref[...] = acc_in[...]
     linear_ref[...] = linear_in[...]
-    got = got_ref[...].reshape(SLOTS, 128)
-    wanted = dot(own_lists(req_t_ref[...]).astype(bf16), ones((128, SLOTS), 0)).astype(jnp.int32)
-    first = jnp.bitwise_and(iota((SLOTS, SLOTS), 0), -CAP)
-    pick = iota((SLOTS, SLOTS), 1) == first + jnp.right_shift(wanted, 6)
+    got = got_ref[...].astype(f32).reshape(8 * OWNERS, 128).astype(bf16)
+    lists = own_lists(req_t_ref[...], CAP).astype(bf16)
+    wanted = dot(lists, ones((128, 8 * OWNERS), 0)).astype(jnp.int32)
+    first = jnp.right_shift(iota((SLOTS, 8 * OWNERS), 0), 4) * 8
+    pick = iota((SLOTS, 8 * OWNERS), 1) == first + jnp.right_shift(wanted, 6)
     values = dot(pick.astype(f32).astype(bf16), got)
     here = iota((SLOTS, 128), 1) == jnp.bitwise_and(wanted[:, :128], 63) + 64
     lin_ref[...] = jnp.where(here, values, 0.0).astype(bf16)
-
-    asked_t = dot(ones((ROWS, 128), 1), both_ref[...].reshape(N_CORE * SLOTS, 128), 1, 1)
-    hot = asked_t == iota((ROWS, N_CORE * SLOTS), 0).astype(f32)
-    hot_t_ref[...] = hot.astype(f32).astype(bf16)
     same_share = iota((SHARE, SHARE), 0) == iota((SHARE, SHARE), 1)
     acc_lin = jnp.sum(jnp.where(same_share, acc_lin_row_ref[...], 0.0), axis=1, keepdims=True)
     acc_lin_ref[...] = jnp.sum(jnp.where(of_share(), acc_lin, 0.0), axis=0, keepdims=True)
@@ -133,7 +135,14 @@
     clicks_col_ref[...] = jnp.sum(jnp.where(same, clicks, 0.0), axis=1, keepdims=True)
 
 
-def learn_kernel(rows_ref, counts_ref, counts_t_ref, clicks_ref, lin_ref, out_ref):
+def asked_kernel(both_ref, hot_t_ref):
+    asked_t = dot(ones((ROWS, 128), 1), one_slot_a_row(both_ref[...]), 1, 1)
+    hot = asked_t == iota((ROWS, N_CORE * SLOTS), 0).astype(f32)
+    hot_t_ref[...] = hot.astype(f32).astype(bf16)
+
+
+def learn_kernel(rows_ref, counts_ref, counts_t_ref, clicks_ref, lin_ref, got_ref, out_ref, later_ref):
+    later_ref[...] = got_ref[...]
     rows = rows_ref[...].reshape(SLOTS, K)
     wide_rows = rows.astype(f32)
     counts = counts_ref[...]
@@ -295,7 +304,7 @@
     req_t = requests.T
     ask, wide = call(
         ask_kernel,
-        [shape((OWNERS, CAP, 128), bf16), shape((ROWS, K), f32)],
+        [shape((OWNERS, 8, 128), bf16), shape((ROWS, K), f32)],
         1 << 20,
         req_t,
         linear.reshape(4, 128),
@@ -306,12 +315,10 @@
     got = exchange(ask, "server")
     found = call(gather_kernel, shape((OWNERS, CAP, K), bf16), 1 << 28, got, wide)
     rows = exchange(found, "server")
-    both = lax.all_gather(got, "core", axis=0, tiled=True)
-    lin_terms, hot_t, counts_t, counts, clicks_col, acc, acc_lin, lin_row = call(
+    lin_terms, counts_t, counts, clicks_col, acc, acc_lin, lin_row = call(
         side_kernel,
         [
             shape((SLOTS, 128), bf16),
-            shape((ROWS, N_CORE * SLOTS), bf16),
             shape((SLOTS, SAMPLES), bf16),
             shape((SAMPLES, SLOTS), bf16),
             shape((SAMPLES, 1), f32),
@@ -321,7 +328,6 @@
         ],
         1 << 30,
         got,
-        both,
         req_t,
         feature_slot.T,
         clicks.reshape(1, SAMPLES),
@@ -329,17 +335,20 @@
         acc_linear.reshape(1, SHARE),
         linear.reshape(1, ROWS),
     )
-    push = call(
+    push, later = call(
         learn_kernel,
-        shape((OWNERS, 2 * CAP + 8, 128), bf16),
+        [shape((OWNERS, 2 * CAP + 8, 128), bf16), shape((OWNERS, 8, 128), bf16)],
         1 << 28,
         rows,
         counts,
         counts_t,
         clicks_col,
         lin_terms,
+        got,
     )
     pushed = exchange(push, "server")
+    both = lax.all_gather(later, "core", axis=0, tiled=True)
+    hot_t = call(asked_kernel, shape((ROWS, N_CORE * SLOTS), bf16), 1 << 30, both)
     pushed = lax.all_gather(pushed, "core", axis=0, tiled=True)
     dense = call(
         scatter_kernel, shape((N_Y, TALL, 128), bf16), 1 << 28, pushed, hot_t

time: 96 us -> 95.7 us (level)
  blocking collectives: 80.3 us -> 64.7 us
  waiting for transfers between devices: 1.96 us -> 11.2 us
  starting transfers between devices: 3.87 us -> 9.07 us
    all_to_all x4 -> x3, blocking collectives: 66 us -> 47.9 us  [exchange(): return lax.all_to_all(x, axis, split_axis=0, concat_axis=0, tiled=True)]
    all_to_all x1 -> x2, waiting for transfers between devices: 1.96 us -> 11.2 us  [exchange(): return lax.all_to_all(x, axis, split_axis=0, concat_axis=0, tiled=True)]
    all_to_all x1 -> x2, starting transfers between devices: 3.87 us -> 9.07 us  [exchange(): return lax.all_to_all(x, axis, split_axis=0, concat_axis=0, tiled=True)]
    all_gather x1, blocking collectives: 5.7 us -> 7.48 us  [body(): pushed = lax.all_gather(pushed, 'core', axis=0, tiled=True)]
    pallas_call x7 -> x8, Pallas kernels: 7.98 us -> 8.82 us  [call(): pl.pallas_call(kernel, out_shape=out, in_specs=[pl.BlockSpec(memory_space...]
  transfers between devices with their start and end apart: 1 -> 2, of which waited for: 1 -> 2; matrix products, arithmetic and copies ran while one was open for 0% -> 0% of each run, Pallas kernels for 3% -> 3%
where the time goes in v6:
time: 95.7 us; the launch traced here: 95.2 us
  blocking collectives  64.7 us (68%)
  waiting for transfers between devices  11.2 us (12%)
  starting transfers between devices  9.07 us (9%)
  Pallas kernels  8.82 us (9%)
    all_to_all x3, blocking collectives, exchange(): return lax.all_to_all(x, axis, split_axis=0, concat_axis=0, tiled=True)  47.9 us
    all_to_all x2, waiting for transfers between devices, exchange(): return lax.all_to_all(x, axis, split_axis=0, concat_axis=0, tiled=True)  11.2 us
    all_to_all x2, starting transfers between devices, exchange(): return lax.all_to_all(x, axis, split_axis=0, concat_axis=0, tiled=True)  9.07 us
    pallas_call x8, Pallas kernels, call(): pl.pallas_call(kernel, out_shape=out, in_specs=[pl.BlockSpec(memory_space...  8.82 us
    all_gather x1, blocking collectives, body(): pushed = lax.all_gather(pushed, 'core', axis=0, tiled=True)  7.48 us
    all_gather x1, blocking collectives, body(): deltas = lax.all_gather(deltas, 'core', axis=0, tiled=True)  4.77 us
    all_gather x1, blocking collectives, body(): both = lax.all_gather(later, 'core', axis=0, tiled=True)  4.59 us
  transfers between devices with their start and end apart: 2, of which 2 were waited for; matrix products, arithmetic and copies ran while one was open for 0% of the time, Pallas kernels for 3%

profile of v6, /device:TPU:1, one launch (start us, length us, event | category | flops | bytes accessed | tf_op | source)
XLA Modules:
  0.0 95.2 jit_solution(4275611340987642190)
XLA Ops:
  0.6 1.1 %shard_map.102 = (bf16[32,8,128]{2,1,0:T(8,128)(2,1)S(1)}, f32[512,256]{1,0:T(8,128)S(1)}) custom-call(s32[16,32]{1,0:T(8,128)} %bitcast.8, f32[4,128]{1,0:T(4,128)} %bitcast.10, f32[512,256]{1,0:T(8,128)} %factors_hbm.1), custom_call_target="tpu_custom_call" | custom-call | flops 1048576 | bytes 528384 | tf_op jit(solution)/shard_map/pallas_call | solution.py:280
  1.7 22.4 %all_to_all.25.got_ref = bf16[32,8,128]{2,1,0:T(8,128)(2,1)S(1)} all-to-all(bf16[32,8,128]{2,1,0:T(8,128)(2,1)S(1)} %get-tuple-element.19), channel_id=1, replica_groups=mesh['server'=32,'y'=8,'core'=2] {'server'}, dimensions={0} | all-to-all | bytes 131072 | tf_op jit(solution)/shard_map/all_to_all | solution.py:296
  24.1 1.2 %shard_map.103 = bf16[32,16,256]{2,1,0:T(8,128)(2,1)} custom-call(bf16[32,8,128]{2,1,0:T(8,128)(2,1)S(1)} %all_to_all.25.got_ref, f32[512,256]{1,0:T(8,128)S(1)} %get-tuple-element.20.factors_ref), custom_call_target="tpu_custom_call" | custom-call | flops 268435456 | bytes 589824 | tf_op jit(solution)/shard_map/pallas_call | solution.py:280
  25.3 0.0 copy-start
  25.3 0.0 copy-start.2
  25.3 0.0 copy-start.3
  25.3 4.0 %all-to-all-start.1 = ((bf16[32,16,256]{2,1,0:T(8,128)(2,1)}), bf16[32,16,256]{2,1,0:T(8,128)(2,1)S(1)}, u32[]{:S(2)}, u32[]{:S(2)}) async-start(bf16[32,16,256]{2,1,0:T(8,128)(2,1)} %shard_map.103), calls=%async_computation.1 | async-start | bytes 524288 | tf_op jit(solution)/shard_map/all_to_all | solution.py:296
  29.4 0.0 copy-start.1
  29.4 0.0 copy-start.4
  29.4 0.0 copy-start.5
  29.4 0.0 copy-done
  29.4 0.0 copy-done.2
  29.4 0.0 copy-done.3
  29.4 0.6 copy-done.1
  30.0 0.0 copy-done.4
  30.1 0.0 copy-done.5
  30.1 2.8 %shard_map.104 = (bf16[512,128]{1,0:T(8,128)(2,1)S(1)}, bf16[512,256]{1,0:T(8,128)(2,1)S(1)}, bf16[256,512]{1,0:T(8,128)(2,1)S(1)}, f32[256,1]{1,0:T(8,128)S(1)}...) custom-call(bf16[32,8,128]{2,1,0:T(8,128)(2,1)S(1)} %all_to_all.25.got_ref, ...), custom_call_target="tpu_custom_call" | custom-call | flops 1073741824 | bytes 143488 | tf_op jit(solution)/shard_map/pallas_call | solution.py:280
  32.8 6.2 %all-to-all-done.1.rows_ref = bf16[32,16,256]{2,1,0:T(8,128)(2,1)S(1)} async-done(((bf16[32,16,256]{2,1,0:T(8,128)(2,1)}), bf16[32,16,256]{2,1,0:T(8,128)(2,1)S(1)}, u32[]{:S(2)}, u32[]{:S(2)}) %all-to-all-start.1) | async-done | bytes 262176 | tf_op jit(solution)/shard_map/all_to_all | solution.py:296
  39.0 1.8 %shard_map.105 = (bf16[32,40,128]{2,1,0:T(8,128)(2,1)}, bf16[32,8,128]{2,1,0:T(8,128)(2,1)S(1)}) custom-call(bf16[32,16,256]{2,1,0:T(8,128)(2,1)S(1)} %all-to-all-done.1.rows_ref, bf16[256,512]{1,0:T(8,128)(2,1)S(1)} %get-tuple-element.21.counts_ref, bf16[512,256]{1,0:T(8,128)(2,1)S(1)} %get-tuple-element.22.counts_t_ref, ...), custom_call_target="tpu_custom_call" | custom-call | flops 268435456 | bytes 984064 | tf_op jit(solution)/shard_map/pallas_call | solution.py:280
  40.8 5.1 %all-to-all-start.2 = ((bf16[32,40,128]{2,1,0:T(8,128)(2,1)}), bf16[32,40,128]{2,1,0:T(8,128)(2,1)S(1)}, u32[]{:S(2)}, u32[]{:S(2)}) async-start(bf16[32,40,128]{2,1,0:T(8,128)(2,1)} %get-tuple-element.25), calls=%async_computation.2 | async-start | bytes 655360 | tf_op jit(solution)/shard_map/all_to_all | solution.py:296
  45.9 4.6 %all_gather.10.both_ref = bf16[64,8,128]{2,1,0:T(8,128)(2,1)S(1)} all-gather(bf16[32,8,128]{2,1,0:T(8,128)(2,1)S(1)} %get-tuple-element.26), channel_id=1, replica_groups=mesh['server'=32,'y'=8,'core'=2] {'core'}, dimensions={0}, use_global_device_ids=true | all-gather | bytes 196608 | tf_op jit(solution)/shard_map/all_gather | solution.py:350
  50.5 0.4 shard_map.106.hot_t_ref
  51.0 5.0 %all-to-all-done.2 = bf16[32,40,128]{2,1,0:T(8,128)(2,1)S(1)} async-done(((bf16[32,40,128]{2,1,0:T(8,128)(2,1)}), bf16[32,40,128]{2,1,0:T(8,128)(2,1)S(1)}, u32[]{:S(2)}, u32[]{:S(2)}) %all-to-all-start.2) | async-done | bytes 327712 | tf_op jit(solution)/shard_map/all_to_all | solution.py:296
  55.9 7.5 %all_gather.9.push_ref = bf16[64,40,128]{2,1,0:T(8,128)(2,1)S(1)} all-gather(bf16[32,40,128]{2,1,0:T(8,128)(2,1)S(1)} %all-to-all-done.2), channel_id=1, replica_groups=mesh['server'=32,'y'=8,'core'=2] {'core'}, dimensions={0}, use_global_device_ids=true | all-gather | bytes 983040 | tf_op jit(solution)/shard_map/all_gather | solution.py:352
  63.4 0.5 shard_map.107
  63.9 14.9 %all_to_all.26.part_ref = bf16[8,72,128]{2,1,0:T(8,128)(2,1)S(1)} all-to-all(bf16[8,72,128]{2,1,0:T(8,128)(2,1)S(1)} %shard_map.107), channel_id=1, replica_groups=mesh['server'=32,'y'=8,'core'=2] {'y'}, dimensions={0} | all-to-all | bytes 294912 | tf_op jit(solution)/shard_map/all_to_all | solution.py:296
  78.9 0.1 shard_map.108
  78.9 10.6 %all_to_all.27 = bf16[8,72,128]{2,1,0:T(8,128)(2,1)S(1)} all-to-all(bf16[8,72,128]{2,1,0:T(8,128)(2,1)S(1)} %shard_map.108), channel_id=1, replica_groups=mesh['server'=32,'y'=8,'core'=2] {'y'}, dimensions={0} | all-to-all | bytes 294912 | tf_op jit(solution)/shard_map/all_to_all | solution.py:296
  89.5 4.8 %all_gather.11.delta_ref = bf16[16,72,128]{2,1,0:T(8,128)(2,1)S(1)} all-gather(bf16[8,72,128]{2,1,0:T(8,128)(2,1)S(1)} %all_to_all.27), channel_id=1, replica_groups=mesh['server'=32,'y'=8,'core'=2] {'core'}, dimensions={0}, use_global_device_ids=true | all-gather | bytes 442368 | tf_op jit(solution)/shard_map/all_gather | solution.py:359
  94.3 0.9 shard_map.109
Async XLA Ops:
  25.3 4.1 %copy-start = (s32[32,16]{0,1:T(8,128)S(1)}, s32[32,16]{0,1:T(8,128)}, u32[]{:S(2)}) copy-start(s32[32,16]{0,1:T(8,128)} %param.12) | copy-start | bytes 6148
  25.3 4.1 %copy-start.2 = (s32[256,39]{0,1:T(8,128)S(1)}, s32[256,39]{0,1:T(8,128)}, u32[]{:S(2)}) copy-start(s32[256,39]{0,1:T(8,128)} %param.11) | copy-start | bytes 119812
  25.3 4.1 %copy-start.3 = (f32[32,256]{1,0:T(8,128)S(1)}, f32[32,256]{1,0:T(8,128)}, u32[]{:S(2)}) copy-start(f32[32,256]{1,0:T(8,128)} %acc_in.1) | copy-start | bytes 98308
  25.3 13.7 %all-to-all-start.1 = ((bf16[32,16,256]{2,1,0:T(8,128)(2,1)}), bf16[32,16,256]{2,1,0:T(8,128)(2,1)S(1)}, u32[]{:S(2)}, u32[]{:S(2)}) async-start(bf16[32,16,256]{2,1,0:T(8,128)(2,1)} %shard_map.103), calls=%async_computation.1 | async-start | bytes 524288 | tf_op jit(solution)/shard_map/all_to_all | solution.py:296
  29.4 0.7 copy-start.1
  29.4 0.7 copy-start.4
  29.4 0.7 copy-start.5
  40.8 15.1 %all-to-all-start.2 = ((bf16[32,40,128]{2,1,0:T(8,128)(2,1)}), bf16[32,40,128]{2,1,0:T(8,128)(2,1)S(1)}, u32[]{:S(2)}, u32[]{:S(2)}) async-start(bf16[32,40,128]{2,1,0:T(8,128)(2,1)} %get-tuple-element.25), calls=%async_computation.2 | async-start | bytes 655360 | tf_op jit(solution)/shard_map/all_to_all | solution.py:296

commit v7 on v6

--- a/solution.py
+++ b/solution.py
@@ -97,6 +97,7 @@
     acc_lin_row_ref,
     linear_in,
     lin_ref,
+    ids_ref,
     counts_t_ref,
     counts_ref,
     clicks_col_ref,
@@ -114,6 +115,14 @@
     values = dot(pick.astype(f32).astype(bf16), got)
     here = iota((SLOTS, 128), 1) == jnp.bitwise_and(wanted[:, :128], 63) + 64
     lin_ref[...] = jnp.where(here, values, 0.0).astype(bf16)
+    spread = jnp.right_shift(iota((OWNERS, SLOTS), 1), 4) == iota((OWNERS, SLOTS), 0)
+    lists = dot(split_requests(req_t_ref[...]), spread.astype(f32).astype(bf16))
+    place = iota((128, SLOTS), 0)
+    position = jnp.bitwise_and(iota((128, SLOTS), 1), CAP - 1)
+    high = jnp.sum(jnp.where(place == position, lists, 0.0), axis=0, keepdims=True)
+    low = jnp.sum(jnp.where(place == position + CAP, lists, 0.0), axis=0, keepdims=True)
+    row = iota((8, SLOTS), 0)
+    ids_ref[...] = jnp.where(row == 2, high, jnp.where(row == 3, low, 0.0))
     same_share = iota((SHARE, SHARE), 0) == iota((SHARE, SHARE), 1)
     acc_lin = jnp.sum(jnp.where(same_share, acc_lin_row_ref[...], 0.0), axis=1, keepdims=True)
     acc_lin_ref[...] = jnp.sum(jnp.where(of_share(), acc_lin, 0.0), axis=0, keepdims=True)
@@ -135,14 +144,7 @@
     clicks_col_ref[...] = jnp.sum(jnp.where(same, clicks, 0.0), axis=1, keepdims=True)
 
 
-def asked_kernel(both_ref, hot_t_ref):
-    asked_t = dot(ones((ROWS, 128), 1), one_slot_a_row(both_ref[...]), 1, 1)
-    hot = asked_t == iota((ROWS, N_CORE * SLOTS), 0).astype(f32)
-    hot_t_ref[...] = hot.astype(f32).astype(bf16)
-
-
-def learn_kernel(rows_ref, counts_ref, counts_t_ref, clicks_ref, lin_ref, got_ref, out_ref, later_ref):
-    later_ref[...] = got_ref[...]
+def learn_kernel(rows_ref, counts_ref, counts_t_ref, clicks_ref, lin_ref, ids_ref, out_ref):
     rows = rows_ref[...].reshape(SLOTS, K)
     wide_rows = rows.astype(f32)
     counts = counts_ref[...]
@@ -167,7 +169,7 @@
     sums_row = (dot(first[:, :128], counts, 0, 0) + dot(second[:, :128], counts, 0, 0))[:8]
     high = sums_row.astype(bf16).astype(f32)
     row = iota((8, SLOTS), 0)
-    sums_row = jnp.where(row == 0, high, jnp.where(row == 1, sums_row - high, 0.0))
+    sums_row = jnp.where(row == 0, high, jnp.where(row == 1, sums_row - high, ids_ref[...]))
     mine = jnp.right_shift(iota((8, 128), 1), 4) == place
     for owner in range(OWNERS):
         lanes = owner // 8 * 128
@@ -182,31 +184,36 @@
     rest = x - first
     second = rest.astype(bf16).astype(f32)
     third = rest - second
-    out = jnp.where(rows == 0, first, jnp.where(rows == 1, second, jnp.where(rows == 2, third, 0.0)))
-    return out.astype(bf16)
-
-
-def scatter_kernel(push_ref, hot_t_ref, out_ref):
+    return jnp.where(rows == 0, first, jnp.where(rows == 1, second, jnp.where(rows == 2, third, 0.0)))
+
+
+def scatter_kernel(push_ref, out_ref):
     core = lax.axis_index("core")
-    left = push_ref[:, :CAP, :].reshape(N_CORE * SLOTS, 128)
-    right = push_ref[:, CAP : 2 * CAP, :].reshape(N_CORE * SLOTS, 128)
-    shares = [
-        hot_t_ref[pl.ds(pl.multiple_of((y * N_CORE + core) * SHARE, SHARE), SHARE), :] for y in range(N_Y)
-    ]
-    total = dot(jnp.concatenate(shares, axis=0), jnp.concatenate([left, right], axis=1)).astype(bf16)
-    out_ref[:, :SHARE, :] = total[:, :128].reshape(N_Y, SHARE, 128)
-    out_ref[:, SHARE : 2 * SHARE, :] = total[:, 128:].reshape(N_Y, SHARE, 128)
     chunks = []
     for q in range(N_CORE * OWNERS // 8):
         chunk = push_ref[8 * q, 2 * CAP :, :].astype(f32)
         for i in range(1, 8):
             chunk = chunk + push_ref[8 * q + i, 2 * CAP :, :].astype(f32)
-        chunks.append(chunk.astype(bf16))
-    linear = dot(jnp.concatenate(chunks, axis=1), hot_t_ref[...], 1, 1)
+        chunks.append(chunk)
+    tails = jnp.concatenate(chunks, axis=1)
+    row = iota(tails.shape, 0)
+    asked = jnp.sum(jnp.where((row == 2) | (row == 3), tails, 0.0), axis=0, keepdims=True)
+    asked = asked.astype(jnp.int32)
+    ours = jnp.bitwise_and(jnp.right_shift(asked, 5), 1) == core
+    place = jnp.right_shift(asked, 6) * SHARE + jnp.bitwise_and(asked, SHARE - 1)
+    place = jnp.where(ours, place, -1)
+    hot = (iota((ROWS // N_CORE, N_CORE * SLOTS), 0) == place).astype(f32).astype(bf16)
+    left = push_ref[:, :CAP, :].reshape(N_CORE * SLOTS, 128)
+    right = push_ref[:, CAP : 2 * CAP, :].reshape(N_CORE * SLOTS, 128)
+    total = dot(hot, jnp.concatenate([left, right], axis=1)).astype(bf16)
+    out_ref[:, :SHARE, :] = total[:, :128].reshape(N_Y, SHARE, 128)
+    out_ref[:, SHARE : 2 * SHARE, :] = total[:, 128:].reshape(N_Y, SHARE, 128)
+    linear = dot(jnp.where(row < 2, tails, 0.0).astype(bf16), hot, 1, 1)
     linear = part_rows(jnp.sum(linear, axis=0, keepdims=True))
     for y in range(N_Y):
-        lanes = y // 2 * 128
-        out_ref[y, 2 * SHARE :, :] = linear[:, lanes : lanes + 128]
+        lanes = y // 4 * 128
+        turn = lax.rem(N_CORE * y + core + 4 - y % 4, 4) * SHARE
+        out_ref[y, 2 * SHARE :, :] = pltpu.roll(linear[:, lanes : lanes + 128], turn, 1).astype(bf16)
 
 
 def add_parts(part_ref):
@@ -231,7 +238,7 @@
 
     left = step(left, acc[:, :128]).astype(bf16)
     right = step(right, acc[:, 128:]).astype(bf16)
-    linear = part_rows(jnp.where(my_lanes(), step(linear, acc_lin_ref[...]), 0.0))
+    linear = part_rows(jnp.where(my_lanes(), step(linear, acc_lin_ref[...]), 0.0)).astype(bf16)
     for y in range(N_Y):
         delta_ref[y, :SHARE, :] = left
         delta_ref[y, SHARE : 2 * SHARE, :] = right
@@ -315,10 +322,11 @@
     got = exchange(ask, "server")
     found = call(gather_kernel, shape((OWNERS, CAP, K), bf16), 1 << 28, got, wide)
     rows = exchange(found, "server")
-    lin_terms, counts_t, counts, clicks_col, acc, acc_lin, lin_row = call(
+    lin_terms, ids, counts_t, counts, clicks_col, acc, acc_lin, lin_row = call(
         side_kernel,
         [
             shape((SLOTS, 128), bf16),
+            shape((8, SLOTS), f32),
             shape((SLOTS, SAMPLES), bf16),
             shape((SAMPLES, SLOTS), bf16),
             shape((SAMPLES, 1), f32),
@@ -335,24 +343,20 @@
         acc_linear.reshape(1, SHARE),
         linear.reshape(1, ROWS),
     )
-    push, later = call(
+    push = call(
         learn_kernel,
-        [shape((OWNERS, 2 * CAP + 8, 128), bf16), shape((OWNERS, 8, 128), bf16)],
+        shape((OWNERS, 2 * CAP + 8, 128), bf16),
         1 << 28,
         rows,
         counts,
         counts_t,
         clicks_col,
         lin_terms,
-        got,
+        ids,
     )
     pushed = exchange(push, "server")
-    both = lax.all_gather(later, "core", axis=0, tiled=True)
-    hot_t = call(asked_kernel, shape((ROWS, N_CORE * SLOTS), bf16), 1 << 30, both)
     pushed = lax.all_gather(pushed, "core", axis=0, tiled=True)
-    dense = call(
-        scatter_kernel, shape((N_Y, TALL, 128), bf16), 1 << 28, pushed, hot_t
-    )
+    dense = call(scatter_kernel, shape((N_Y, TALL, 128), bf16), 1 << 28, pushed)
     shared = exchange(dense, "y")
     delta = call(update_kernel, shape((N_Y, TALL, 128), bf16), 1 << 20, shared, acc, acc_lin)
     deltas = exchange(delta, "y")

time: 95.7 us -> 94.6 us (0.989)
  blocking collectives: 64.7 us -> 75 us
  starting transfers between devices: 9.07 us -> 4 us
  waiting for transfers between devices: 11.2 us -> 6.2 us
  Pallas kernels: 8.82 us -> 7.62 us
    all_to_all x3 -> x4, blocking collectives: 47.9 us -> 62.7 us  [exchange(): return lax.all_to_all(x, axis, split_axis=0, concat_axis=0, tiled=True)]
    all_to_all x2 -> x1, starting transfers between devices: 9.07 us -> 4 us  [exchange(): return lax.all_to_all(x, axis, split_axis=0, concat_axis=0, tiled=True)]
    all_to_all x2 -> x1, waiting for transfers between devices: 11.2 us -> 6.2 us  [exchange(): return lax.all_to_all(x, axis, split_axis=0, concat_axis=0, tiled=True)]
    all_gather x1 -> x0, blocking collectives: 4.59 us -> none  [body(): both = lax.all_gather(later, 'core', axis=0, tiled=True)]
    pallas_call x8 -> x7, Pallas kernels: 8.82 us -> 7.62 us  [call(): pl.pallas_call(kernel, out_shape=out, in_specs=[pl.BlockSpec(memory_space...]
  transfers between devices with their start and end apart: 2 -> 1, of which waited for: 2 -> 1; matrix products, arithmetic and copies ran while one was open for 0% -> 0% of each run, Pallas kernels for 3% -> 3%
where the time goes in v7:
time: 94.6 us; the launch traced here: 94.2 us
  blocking collectives  75 us (79%)
  Pallas kernels  7.62 us (8%)
  waiting for transfers between devices  6.2 us (7%)
  starting transfers between devices  4 us (4%)
    all_to_all x4, blocking collectives, exchange(): return lax.all_to_all(x, axis, split_axis=0, concat_axis=0, tiled=True)  62.7 us
    pallas_call x7, Pallas kernels, call(): pl.pallas_call(kernel, out_shape=out, in_specs=[pl.BlockSpec(memory_space...  7.62 us
    all_gather x1, blocking collectives, body(): pushed = lax.all_gather(pushed, 'core', axis=0, tiled=True)  7.48 us
    all_to_all x1, waiting for transfers between devices, exchange(): return lax.all_to_all(x, axis, split_axis=0, concat_axis=0, tiled=True)  6.2 us
    all_gather x1, blocking collectives, body(): deltas = lax.all_gather(deltas, 'core', axis=0, tiled=True)  4.77 us
    all_to_all x1, starting transfers between devices, exchange(): return lax.all_to_all(x, axis, split_axis=0, concat_axis=0, tiled=True)  4 us
  transfers between devices with their start and end apart: 1, of which 1 were waited for; matrix products, arithmetic and copies ran while one was open for 0% of the time, Pallas kernels for 3%

profile of v7, /device:TPU:1, one launch (start us, length us, event | category | flops | bytes accessed | tf_op | source)
XLA Modules:
  0.0 94.2 jit_solution(5646548199283509636)
XLA Ops:
  0.6 1.1 %shard_map.102 = (bf16[32,8,128]{2,1,0:T(8,128)(2,1)S(1)}, f32[512,256]{1,0:T(8,128)S(1)}) custom-call(s32[16,32]{1,0:T(8,128)} %bitcast.8, f32[4,128]{1,0:T(4,128)} %bitcast.10, f32[512,256]{1,0:T(8,128)} %factors_hbm.1), custom_call_target="tpu_custom_call" | custom-call | flops 1048576 | bytes 528384 | tf_op jit(solution)/shard_map/pallas_call | solution.py:287
  1.7 22.4 %all_to_all.25.got_ref = bf16[32,8,128]{2,1,0:T(8,128)(2,1)S(1)} all-to-all(bf16[32,8,128]{2,1,0:T(8,128)(2,1)S(1)} %get-tuple-element.18), channel_id=1, replica_groups=mesh['server'=32,'y'=8,'core'=2] {'server'}, dimensions={0} | all-to-all | bytes 131072 | tf_op jit(solution)/shard_map/all_to_all | solution.py:303
  24.1 1.2 %shard_map.103 = bf16[32,16,256]{2,1,0:T(8,128)(2,1)} custom-call(bf16[32,8,128]{2,1,0:T(8,128)(2,1)S(1)} %all_to_all.25.got_ref, f32[512,256]{1,0:T(8,128)S(1)} %get-tuple-element.19.factors_ref), custom_call_target="tpu_custom_call" | custom-call | flops 268435456 | bytes 589824 | tf_op jit(solution)/shard_map/pallas_call | solution.py:287
  25.3 0.0 copy-start
  25.3 0.0 copy-start.2
  25.3 0.0 copy-start.3
  25.3 4.0 %all-to-all-start.1 = ((bf16[32,16,256]{2,1,0:T(8,128)(2,1)}), bf16[32,16,256]{2,1,0:T(8,128)(2,1)S(1)}, u32[]{:S(2)}, u32[]{:S(2)}) async-start(bf16[32,16,256]{2,1,0:T(8,128)(2,1)} %shard_map.103), calls=%async_computation.1 | async-start | bytes 524288 | tf_op jit(solution)/shard_map/all_to_all | solution.py:303
  29.4 0.0 copy-start.1
  29.4 0.0 copy-start.4
  29.4 0.0 copy-start.5
  29.4 0.0 copy-done
  29.4 0.0 copy-done.2
  29.4 0.0 copy-done.3
  29.4 0.6 copy-done.1
  30.0 0.0 copy-done.4
  30.1 0.0 copy-done.5
  30.1 2.8 %shard_map.104 = (bf16[512,128]{1,0:T(8,128)(2,1)S(1)}, f32[8,512]{1,0:T(8,128)S(1)}, bf16[512,256]{1,0:T(8,128)(2,1)S(1)}, bf16[256,512]{1,0:T(8,128)(2,1)S(1)}...) custom-call(bf16[32,8,128]{2,1,0:T(8,128)(2,1)S(1)} %all_to_all.25.got_ref, ...), custom_call_target="tpu_custom_call" | custom-call | flops 1073741824 | bytes 143488 | tf_op jit(solution)/shard_map/pallas_call | solution.py:287
  32.8 6.2 %all-to-all-done.1.rows_ref = bf16[32,16,256]{2,1,0:T(8,128)(2,1)S(1)} async-done(((bf16[32,16,256]{2,1,0:T(8,128)(2,1)}), bf16[32,16,256]{2,1,0:T(8,128)(2,1)S(1)}, u32[]{:S(2)}, u32[]{:S(2)}) %all-to-all-start.1) | async-done | bytes 262176 | tf_op jit(solution)/shard_map/all_to_all | solution.py:303
  39.0 1.1 %shard_map.105 = bf16[32,40,128]{2,1,0:T(8,128)(2,1)S(1)} custom-call(bf16[32,16,256]{2,1,0:T(8,128)(2,1)S(1)} %all-to-all-done.1.rows_ref, bf16[256,512]{1,0:T(8,128)(2,1)S(1)} %get-tuple-element.20.counts_ref, bf16[512,256]{1,0:T(8,128)(2,1)S(1)} %get-tuple-element.21.counts_t_ref, f32[256,1]{1,0:T(8,128)S(1)} %get-tuple-element.22.clicks_ref, ...), custom_call_target="tpu_custom_call" | custom-call | flops 268435456 | bytes 934912 | tf_op jit(solution)/shard_map/pallas_call | solution.py:287
  40.1 14.9 %all_to_all.26 = bf16[32,40,128]{2,1,0:T(8,128)(2,1)S(1)} all-to-all(bf16[32,40,128]{2,1,0:T(8,128)(2,1)S(1)} %shard_map.105), channel_id=1, replica_groups=mesh['server'=32,'y'=8,'core'=2] {'server'}, dimensions={0} | all-to-all | bytes 655360 | tf_op jit(solution)/shard_map/all_to_all | solution.py:303
  55.0 7.5 %all_gather.6.push_ref = bf16[64,40,128]{2,1,0:T(8,128)(2,1)S(1)} all-gather(bf16[32,40,128]{2,1,0:T(8,128)(2,1)S(1)} %all_to_all.26), channel_id=1, replica_groups=mesh['server'=32,'y'=8,'core'=2] {'core'}, dimensions={0}, use_global_device_ids=true | all-gather | bytes 983040 | tf_op jit(solution)/shard_map/all_gather | solution.py:358
  62.5 0.5 shard_map.106
  63.0 14.9 %all_to_all.27.part_ref = bf16[8,72,128]{2,1,0:T(8,128)(2,1)S(1)} all-to-all(bf16[8,72,128]{2,1,0:T(8,128)(2,1)S(1)} %shard_map.106), channel_id=1, replica_groups=mesh['server'=32,'y'=8,'core'=2] {'y'}, dimensions={0} | all-to-all | bytes 294912 | tf_op jit(solution)/shard_map/all_to_all | solution.py:303
  77.9 0.1 shard_map.107
  77.9 10.6 %all_to_all.28 = bf16[8,72,128]{2,1,0:T(8,128)(2,1)S(1)} all-to-all(bf16[8,72,128]{2,1,0:T(8,128)(2,1)S(1)} %shard_map.107), channel_id=1, replica_groups=mesh['server'=32,'y'=8,'core'=2] {'y'}, dimensions={0} | all-to-all | bytes 294912 | tf_op jit(solution)/shard_map/all_to_all | solution.py:303
  88.5 4.8 %all_gather.7.delta_ref = bf16[16,72,128]{2,1,0:T(8,128)(2,1)S(1)} all-gather(bf16[8,72,128]{2,1,0:T(8,128)(2,1)S(1)} %all_to_all.28), channel_id=1, replica_groups=mesh['server'=32,'y'=8,'core'=2] {'core'}, dimensions={0}, use_global_device_ids=true | all-gather | bytes 442368 | tf_op jit(solution)/shard_map/all_gather | solution.py:363
  93.3 0.9 shard_map.108
Async XLA Ops:
  25.3 4.1 %copy-start = (s32[32,16]{0,1:T(8,128)S(1)}, s32[32,16]{0,1:T(8,128)}, u32[]{:S(2)}) copy-start(s32[32,16]{0,1:T(8,128)} %param.12) | copy-start | bytes 6148
  25.3 4.1 %copy-start.2 = (s32[256,39]{0,1:T(8,128)S(1)}, s32[256,39]{0,1:T(8,128)}, u32[]{:S(2)}) copy-start(s32[256,39]{0,1:T(8,128)} %param.11) | copy-start | bytes 119812
  25.3 4.1 %copy-start.3 = (f32[32,256]{1,0:T(8,128)S(1)}, f32[32,256]{1,0:T(8,128)}, u32[]{:S(2)}) copy-start(f32[32,256]{1,0:T(8,128)} %acc_in.1) | copy-start | bytes 98308
  25.3 13.7 %all-to-all-start.1 = ((bf16[32,16,256]{2,1,0:T(8,128)(2,1)}), bf16[32,16,256]{2,1,0:T(8,128)(2,1)S(1)}, u32[]{:S(2)}, u32[]{:S(2)}) async-start(bf16[32,16,256]{2,1,0:T(8,128)(2,1)} %shard_map.103), calls=%async_computation.1 | async-start | bytes 524288 | tf_op jit(solution)/shard_map/all_to_all | solution.py:303
  29.4 0.7 copy-start.1
  29.4 0.7 copy-start.4
  29.4 0.7 copy-start.5

commit v8 on v7

--- a/solution.py
+++ b/solution.py
@@ -47,11 +47,13 @@
     return jnp.where(keep, lists, 0.0)
 
 
-def one_slot_a_row(got):
+def asked_rows(got):
     got = got.astype(f32)
-    upper = jnp.bitwise_and(iota(got.shape, 2), 8) == 8
+    lane = iota(got.shape, 2)
+    upper = jnp.bitwise_and(lane, 8) == 8
+    got = jnp.where(lane < 2 * CAP, got, 0.0)
     split = jnp.concatenate([jnp.where(upper, 0.0, got), jnp.where(upper, got, 0.0)], axis=1)
-    return split.astype(bf16).reshape(got.shape[0] * CAP, 128)
+    return jnp.sum(split.reshape(SLOTS, 128), axis=1, keepdims=True)
 
 
 def ones(dims, axis):
@@ -83,7 +85,7 @@
 
 
 def gather_kernel(got_ref, factors_ref, out_ref):
-    asked = dot(one_slot_a_row(got_ref[...]), ones((128, ROWS), 0))
+    asked = asked_rows(got_ref[...])
     hot = (asked == iota((SLOTS, ROWS), 1).astype(f32)).astype(f32).astype(bf16)
     out_ref[...] = dot(hot, factors_ref[...].astype(bf16)).astype(bf16).reshape(OWNERS, CAP, K)
 
@@ -155,18 +157,22 @@
     terms = sums * sums - dot(counts, high) - dot(counts, low)
     terms = 0.5 * (terms[:, :128] + terms[:, 128:]) + dot(counts, lin_ref[...])
     logits = jnp.sum(terms, axis=1, keepdims=True)
-    errors = jnp.broadcast_to(jax.nn.sigmoid(logits) - clicks_ref[...], (SAMPLES, K))
-    weighted = (errors * sums).astype(bf16)
+    errors = jnp.broadcast_to(jax.nn.sigmoid(logits) - clicks_ref[...], (SAMPLES, 128))
     first = errors.astype(bf16)
     second = (errors - first.astype(f32)).astype(bf16)
+    weighted = (jnp.concatenate([errors, errors], axis=1) * sums).astype(bf16)
     counts_t = counts_t_ref[...]
-    error_sums = dot(counts_t, first) + dot(counts_t, second)
-    grads = dot(counts_t, weighted) - error_sums * wide_rows
-    grads = grads.astype(bf16)
-    out_ref[:, :CAP, :] = grads[:, :128].reshape(OWNERS, CAP, 128)
-    out_ref[:, CAP : 2 * CAP, :] = grads[:, 128:].reshape(OWNERS, CAP, 128)
+    error_sums = dot(counts_t, jnp.concatenate([first, second], axis=1))
+    error_sums = error_sums[:, :128] + error_sums[:, 128:]
+    gathered = dot(counts_t, weighted)
+    left = gathered[:, :128] - error_sums * wide_rows[:, :128]
+    right = gathered[:, 128:] - error_sums * wide_rows[:, 128:]
+    out_ref[:, :CAP, :] = left.astype(bf16).reshape(OWNERS, CAP, 128)
+    out_ref[:, CAP : 2 * CAP, :] = right.astype(bf16).reshape(OWNERS, CAP, 128)
     place = lax.rem(lax.axis_index("server"), 8)
-    sums_row = (dot(first[:, :128], counts, 0, 0) + dot(second[:, :128], counts, 0, 0))[:8]
+    pair = jnp.where(iota((SAMPLES, 128), 1) < 8, first.astype(f32), second.astype(f32)).astype(bf16)
+    sums_row = dot(pair, counts, 0, 0)
+    sums_row = sums_row[:8] + sums_row[8:16]
     high = sums_row.astype(bf16).astype(f32)
     row = iota((8, SLOTS), 0)
     sums_row = jnp.where(row == 0, high, jnp.where(row == 1, sums_row - high, ids_ref[...]))

time: 94.6 us -> 94.4 us (level)
  no operation moved by 1% of the time
where the time goes in v8:
time: 94.4 us; the launch traced here: 93.9 us
  blocking collectives  75 us (79%)
  Pallas kernels  7.36 us (8%)
  waiting for transfers between devices  6.2 us (7%)
  starting transfers between devices  4 us (4%)
    all_to_all x4, blocking collectives, exchange(): return lax.all_to_all(x, axis, split_axis=0, concat_axis=0, tiled=True)  62.8 us
    all_gather x1, blocking collectives, body(): pushed = lax.all_gather(pushed, 'core', axis=0, tiled=True)  7.48 us
    pallas_call x7, Pallas kernels, call(): pl.pallas_call(kernel, out_shape=out, in_specs=[pl.BlockSpec(memory_space...  7.36 us
    all_to_all x1, waiting for transfers between devices, exchange(): return lax.all_to_all(x, axis, split_axis=0, concat_axis=0, tiled=True)  6.2 us
    all_gather x1, blocking collectives, body(): deltas = lax.all_gather(deltas, 'core', axis=0, tiled=True)  4.77 us
    all_to_all x1, starting transfers between devices, exchange(): return lax.all_to_all(x, axis, split_axis=0, concat_axis=0, tiled=True)  4 us
  transfers between devices with their start and end apart: 1, of which 1 were waited for; matrix products, arithmetic and copies ran while one was open for 0% of the time, Pallas kernels for 3%

profile of v8, /device:TPU:1, one launch (start us, length us, event | category | flops | bytes accessed | tf_op | source)
XLA Modules:
  0.0 93.9 jit_solution(11882900130822018617)
XLA Ops:
  0.6 1.1 %shard_map.102 = (bf16[32,8,128]{2,1,0:T(8,128)(2,1)S(1)}, f32[512,256]{1,0:T(8,128)S(1)}) custom-call(s32[16,32]{1,0:T(8,128)} %bitcast.8, f32[4,128]{1,0:T(4,128)} %bitcast.10, f32[512,256]{1,0:T(8,128)} %factors_hbm.1), custom_call_target="tpu_custom_call" | custom-call | flops 1048576 | bytes 528384 | tf_op jit(solution)/shard_map/pallas_call | solution.py:293
  1.7 22.4 %all_to_all.25.got_ref = bf16[32,8,128]{2,1,0:T(8,128)(2,1)S(1)} all-to-all(bf16[32,8,128]{2,1,0:T(8,128)(2,1)S(1)} %get-tuple-element.18), channel_id=1, replica_groups=mesh['server'=32,'y'=8,'core'=2] {'server'}, dimensions={0} | all-to-all | bytes 131072 | tf_op jit(solution)/shard_map/all_to_all | solution.py:309
  24.1 1.1 %shard_map.103 = bf16[32,16,256]{2,1,0:T(8,128)(2,1)} custom-call(bf16[32,8,128]{2,1,0:T(8,128)(2,1)S(1)} %all_to_all.25.got_ref, f32[512,256]{1,0:T(8,128)S(1)} %get-tuple-element.19.factors_ref), custom_call_target="tpu_custom_call" | custom-call | flops 268435456 | bytes 589824 | tf_op jit(solution)/shard_map/pallas_call | solution.py:293
  25.2 0.0 copy-start
  25.2 0.0 copy-start.2
  25.2 0.0 copy-start.3
  25.2 4.0 %all-to-all-start.1 = ((bf16[32,16,256]{2,1,0:T(8,128)(2,1)}), bf16[32,16,256]{2,1,0:T(8,128)(2,1)S(1)}, u32[]{:S(2)}, u32[]{:S(2)}) async-start(bf16[32,16,256]{2,1,0:T(8,128)(2,1)} %shard_map.103), calls=%async_computation.1 | async-start | bytes 524288 | tf_op jit(solution)/shard_map/all_to_all | solution.py:309
  29.2 0.0 copy-start.1
  29.2 0.0 copy-start.4
  29.2 0.0 copy-start.5
  29.2 0.0 copy-done
  29.2 0.0 copy-done.2
  29.2 0.0 copy-done.3
  29.3 0.6 copy-done.1
  29.9 0.0 copy-done.4
  29.9 0.0 copy-done.5
  29.9 2.8 %shard_map.104 = (bf16[512,128]{1,0:T(8,128)(2,1)S(1)}, f32[8,512]{1,0:T(8,128)S(1)}, bf16[512,256]{1,0:T(8,128)(2,1)S(1)}, bf16[256,512]{1,0:T(8,128)(2,1)S(1)}...) custom-call(bf16[32,8,128]{2,1,0:T(8,128)(2,1)S(1)} %all_to_all.25.got_ref, ...), custom_call_target="tpu_custom_call" | custom-call | flops 1073741824 | bytes 143488 | tf_op jit(solution)/shard_map/pallas_call | solution.py:293
  32.7 6.2 %all-to-all-done.1.rows_ref = bf16[32,16,256]{2,1,0:T(8,128)(2,1)S(1)} async-done(((bf16[32,16,256]{2,1,0:T(8,128)(2,1)}), bf16[32,16,256]{2,1,0:T(8,128)(2,1)S(1)}, u32[]{:S(2)}, u32[]{:S(2)}) %all-to-all-start.1) | async-done | bytes 262176 | tf_op jit(solution)/shard_map/all_to_all | solution.py:309
  38.9 1.0 %shard_map.105 = bf16[32,40,128]{2,1,0:T(8,128)(2,1)S(1)} custom-call(bf16[32,16,256]{2,1,0:T(8,128)(2,1)S(1)} %all-to-all-done.1.rows_ref, bf16[256,512]{1,0:T(8,128)(2,1)S(1)} %get-tuple-element.20.counts_ref, bf16[512,256]{1,0:T(8,128)(2,1)S(1)} %get-tuple-element.21.counts_t_ref, f32[256,1]{1,0:T(8,128)S(1)} %get-tuple-element.22.clicks_ref, ...), custom_call_target="tpu_custom_call" | custom-call | flops 268435456 | bytes 934912 | tf_op jit(solution)/shard_map/pallas_call | solution.py:293
  39.9 14.9 %all_to_all.26 = bf16[32,40,128]{2,1,0:T(8,128)(2,1)S(1)} all-to-all(bf16[32,40,128]{2,1,0:T(8,128)(2,1)S(1)} %shard_map.105), channel_id=1, replica_groups=mesh['server'=32,'y'=8,'core'=2] {'server'}, dimensions={0} | all-to-all | bytes 655360 | tf_op jit(solution)/shard_map/all_to_all | solution.py:309
  54.8 7.5 %all_gather.6.push_ref = bf16[64,40,128]{2,1,0:T(8,128)(2,1)S(1)} all-gather(bf16[32,40,128]{2,1,0:T(8,128)(2,1)S(1)} %all_to_all.26), channel_id=1, replica_groups=mesh['server'=32,'y'=8,'core'=2] {'core'}, dimensions={0}, use_global_device_ids=true | all-gather | bytes 983040 | tf_op jit(solution)/shard_map/all_gather | solution.py:364
  62.2 0.5 shard_map.106
  62.7 14.9 %all_to_all.27.part_ref = bf16[8,72,128]{2,1,0:T(8,128)(2,1)S(1)} all-to-all(bf16[8,72,128]{2,1,0:T(8,128)(2,1)S(1)} %shard_map.106), channel_id=1, replica_groups=mesh['server'=32,'y'=8,'core'=2] {'y'}, dimensions={0} | all-to-all | bytes 294912 | tf_op jit(solution)/shard_map/all_to_all | solution.py:309
  77.6 0.1 shard_map.107
  77.7 10.6 %all_to_all.28 = bf16[8,72,128]{2,1,0:T(8,128)(2,1)S(1)} all-to-all(bf16[8,72,128]{2,1,0:T(8,128)(2,1)S(1)} %shard_map.107), channel_id=1, replica_groups=mesh['server'=32,'y'=8,'core'=2] {'y'}, dimensions={0} | all-to-all | bytes 294912 | tf_op jit(solution)/shard_map/all_to_all | solution.py:309
  88.3 4.8 %all_gather.7.delta_ref = bf16[16,72,128]{2,1,0:T(8,128)(2,1)S(1)} all-gather(bf16[8,72,128]{2,1,0:T(8,128)(2,1)S(1)} %all_to_all.28), channel_id=1, replica_groups=mesh['server'=32,'y'=8,'core'=2] {'core'}, dimensions={0}, use_global_device_ids=true | all-gather | bytes 442368 | tf_op jit(solution)/shard_map/all_gather | solution.py:369
  93.1 0.9 shard_map.108
Async XLA Ops:
  25.2 4.1 %copy-start = (s32[32,16]{0,1:T(8,128)S(1)}, s32[32,16]{0,1:T(8,128)}, u32[]{:S(2)}) copy-start(s32[32,16]{0,1:T(8,128)} %param.12) | copy-start | bytes 6148
  25.2 4.1 %copy-start.2 = (s32[256,39]{0,1:T(8,128)S(1)}, s32[256,39]{0,1:T(8,128)}, u32[]{:S(2)}) copy-start(s32[256,39]{0,1:T(8,128)} %param.11) | copy-start | bytes 119812
  25.2 4.1 %copy-start.3 = (f32[32,256]{1,0:T(8,128)S(1)}, f32[32,256]{1,0:T(8,128)}, u32[]{:S(2)}) copy-start(f32[32,256]{1,0:T(8,128)} %acc_in.1) | copy-start | bytes 98308
  25.2 13.7 %all-to-all-start.1 = ((bf16[32,16,256]{2,1,0:T(8,128)(2,1)}), bf16[32,16,256]{2,1,0:T(8,128)(2,1)S(1)}, u32[]{:S(2)}, u32[]{:S(2)}) async-start(bf16[32,16,256]{2,1,0:T(8,128)(2,1)} %shard_map.103), calls=%async_computation.1 | async-start | bytes 524288 | tf_op jit(solution)/shard_map/all_to_all | solution.py:309
  29.2 0.7 copy-start.1
  29.2 0.7 copy-start.4
  29.2 0.7 copy-start.5

commit v9 on v8

--- a/solution.py
+++ b/solution.py
@@ -116,7 +116,7 @@
     pick = iota((SLOTS, 8 * OWNERS), 1) == first + jnp.right_shift(wanted, 6)
     values = dot(pick.astype(f32).astype(bf16), got)
     here = iota((SLOTS, 128), 1) == jnp.bitwise_and(wanted[:, :128], 63) + 64
-    lin_ref[...] = jnp.where(here, values, 0.0).astype(bf16)
+    lin_terms = jnp.where(here, values, 0.0).astype(bf16)
     spread = jnp.right_shift(iota((OWNERS, SLOTS), 1), 4) == iota((OWNERS, SLOTS), 0)
     lists = dot(split_requests(req_t_ref[...]), spread.astype(f32).astype(bf16))
     place = iota((128, SLOTS), 0)
@@ -140,7 +140,9 @@
         return carry
 
     lax.fori_loop(0, SLOTS // chunk, one, 0)
-    counts_ref[...] = jnp.transpose(counts_t_ref[...].astype(f32)).astype(bf16)
+    counts = jnp.transpose(counts_t_ref[...].astype(f32)).astype(bf16)
+    counts_ref[...] = counts
+    lin_ref[...] = dot(counts, lin_terms)
     same = iota((SAMPLES, SAMPLES), 0) == iota((SAMPLES, SAMPLES), 1)
     clicks = clicks_ref[...].astype(f32)
     clicks_col_ref[...] = jnp.sum(jnp.where(same, clicks, 0.0), axis=1, keepdims=True)
@@ -152,10 +154,13 @@
     counts = counts_ref[...]
     sums = dot(counts, rows)
     square = wide_rows * wide_rows
+    square = square[:, :128] + square[:, 128:]
     high = square.astype(bf16)
-    low = (square - high.astype(f32)).astype(bf16)
-    terms = sums * sums - dot(counts, high) - dot(counts, low)
-    terms = 0.5 * (terms[:, :128] + terms[:, 128:]) + dot(counts, lin_ref[...])
+    rest = square - high.astype(f32)
+    middle = rest.astype(bf16)
+    low = (rest - middle.astype(f32)).astype(bf16)
+    terms = sums * sums - dot(counts, jnp.concatenate([high, middle], axis=1))
+    terms = 0.5 * (terms[:, :128] + terms[:, 128:] - dot(counts, low)) + lin_ref[...]
     logits = jnp.sum(terms, axis=1, keepdims=True)
     errors = jnp.broadcast_to(jax.nn.sigmoid(logits) - clicks_ref[...], (SAMPLES, 128))
     first = errors.astype(bf16)
@@ -331,7 +336,7 @@
     lin_terms, ids, counts_t, counts, clicks_col, acc, acc_lin, lin_row = call(
         side_kernel,
         [
-            shape((SLOTS, 128), bf16),
+            shape((SAMPLES, 128), f32),
             shape((8, SLOTS), f32),
             shape((SLOTS, SAMPLES), bf16),
             shape((SAMPLES, SLOTS), bf16),

time: 94.4 us -> 94.3 us (level)
  no operation moved by 1% of the time
where the time goes in v9:
time: 94.3 us; the launch traced here: 93.9 us
  blocking collectives  75 us (80%)
  Pallas kernels  7.39 us (8%)
  waiting for transfers between devices  6.11 us (6%)
  starting transfers between devices  4 us (4%)
    all_to_all x4, blocking collectives, exchange(): return lax.all_to_all(x, axis, split_axis=0, concat_axis=0, tiled=True)  62.8 us
    all_gather x1, blocking collectives, body(): pushed = lax.all_gather(pushed, 'core', axis=0, tiled=True)  7.49 us
    pallas_call x7, Pallas kernels, call(): pl.pallas_call(kernel, out_shape=out, in_specs=[pl.BlockSpec(memory_space...  7.39 us
    all_to_all x1, waiting for transfers between devices, exchange(): return lax.all_to_all(x, axis, split_axis=0, concat_axis=0, tiled=True)  6.11 us
    all_gather x1, blocking collectives, body(): deltas = lax.all_gather(deltas, 'core', axis=0, tiled=True)  4.76 us
    all_to_all x1, starting transfers between devices, exchange(): return lax.all_to_all(x, axis, split_axis=0, concat_axis=0, tiled=True)  4 us
  transfers between devices with their start and end apart: 1, of which 1 were waited for; matrix products, arithmetic and copies ran while one was open for 0% of the time, Pallas kernels for 3%

profile of v9, /device:TPU:1, one launch (start us, length us, event | category | flops | bytes accessed | tf_op | source)
XLA Modules:
  0.0 93.9 jit_solution(5992452380775164797)
XLA Ops:
  0.6 1.1 %shard_map.102 = (bf16[32,8,128]{2,1,0:T(8,128)(2,1)S(1)}, f32[512,256]{1,0:T(8,128)S(1)}) custom-call(s32[16,32]{1,0:T(8,128)} %bitcast.8, f32[4,128]{1,0:T(4,128)} %bitcast.10, f32[512,256]{1,0:T(8,128)} %factors_hbm.1), custom_call_target="tpu_custom_call" | custom-call | flops 1048576 | bytes 528384 | tf_op jit(solution)/shard_map/pallas_call | solution.py:298
  1.7 22.4 %all_to_all.25.got_ref = bf16[32,8,128]{2,1,0:T(8,128)(2,1)S(1)} all-to-all(bf16[32,8,128]{2,1,0:T(8,128)(2,1)S(1)} %get-tuple-element.18), channel_id=1, replica_groups=mesh['server'=32,'y'=8,'core'=2] {'server'}, dimensions={0} | all-to-all | bytes 131072 | tf_op jit(solution)/shard_map/all_to_all | solution.py:314
  24.1 1.1 %shard_map.103 = bf16[32,16,256]{2,1,0:T(8,128)(2,1)} custom-call(bf16[32,8,128]{2,1,0:T(8,128)(2,1)S(1)} %all_to_all.25.got_ref, f32[512,256]{1,0:T(8,128)S(1)} %get-tuple-element.19.factors_ref), custom_call_target="tpu_custom_call" | custom-call | flops 268435456 | bytes 589824 | tf_op jit(solution)/shard_map/pallas_call | solution.py:298
  25.2 0.0 copy-start
  25.2 0.0 copy-start.2
  25.2 0.0 copy-start.3
  25.2 4.0 %all-to-all-start.1 = ((bf16[32,16,256]{2,1,0:T(8,128)(2,1)}), bf16[32,16,256]{2,1,0:T(8,128)(2,1)S(1)}, u32[]{:S(2)}, u32[]{:S(2)}) async-start(bf16[32,16,256]{2,1,0:T(8,128)(2,1)} %shard_map.103), calls=%async_computation.1 | async-start | bytes 524288 | tf_op jit(solution)/shard_map/all_to_all | solution.py:314
  29.2 0.0 copy-start.1
  29.2 0.0 copy-start.4
  29.2 0.0 copy-start.5
  29.2 0.0 copy-done
  29.2 0.0 copy-done.2
  29.2 0.0 copy-done.3
  29.3 0.6 copy-done.1
  29.9 0.0 copy-done.4
  29.9 0.0 copy-done.5
  29.9 2.9 %shard_map.104 = (f32[256,128]{1,0:T(8,128)S(1)}, f32[8,512]{1,0:T(8,128)S(1)}, bf16[512,256]{1,0:T(8,128)(2,1)S(1)}, bf16[256,512]{1,0:T(8,128)(2,1)S(1)}, f32[...) custom-call(bf16[32,8,128]{2,1,0:T(8,128)(2,1)S(1)} %all_to_all.25.got_ref, ...), custom_call_target="tpu_custom_call" | custom-call | flops 1073741824 | bytes 143488 | tf_op jit(solution)/shard_map/pallas_call | solution.py:298
  32.8 6.1 %all-to-all-done.1.rows_ref = bf16[32,16,256]{2,1,0:T(8,128)(2,1)S(1)} async-done(((bf16[32,16,256]{2,1,0:T(8,128)(2,1)}), bf16[32,16,256]{2,1,0:T(8,128)(2,1)S(1)}, u32[]{:S(2)}, u32[]{:S(2)}) %all-to-all-start.1) | async-done | bytes 262176 | tf_op jit(solution)/shard_map/all_to_all | solution.py:314
  38.9 0.9 shard_map.105
  39.8 14.9 %all_to_all.26 = bf16[32,40,128]{2,1,0:T(8,128)(2,1)S(1)} all-to-all(bf16[32,40,128]{2,1,0:T(8,128)(2,1)S(1)} %shard_map.105), channel_id=1, replica_groups=mesh['server'=32,'y'=8,'core'=2] {'server'}, dimensions={0} | all-to-all | bytes 655360 | tf_op jit(solution)/shard_map/all_to_all | solution.py:314
  54.7 7.5 %all_gather.6.push_ref = bf16[64,40,128]{2,1,0:T(8,128)(2,1)S(1)} all-gather(bf16[32,40,128]{2,1,0:T(8,128)(2,1)S(1)} %all_to_all.26), channel_id=1, replica_groups=mesh['server'=32,'y'=8,'core'=2] {'core'}, dimensions={0}, use_global_device_ids=true | all-gather | bytes 983040 | tf_op jit(solution)/shard_map/all_gather | solution.py:369
  62.2 0.5 shard_map.106
  62.7 14.9 %all_to_all.27.part_ref = bf16[8,72,128]{2,1,0:T(8,128)(2,1)S(1)} all-to-all(bf16[8,72,128]{2,1,0:T(8,128)(2,1)S(1)} %shard_map.106), channel_id=1, replica_groups=mesh['server'=32,'y'=8,'core'=2] {'y'}, dimensions={0} | all-to-all | bytes 294912 | tf_op jit(solution)/shard_map/all_to_all | solution.py:314
  77.6 0.1 shard_map.107
  77.7 10.6 %all_to_all.28 = bf16[8,72,128]{2,1,0:T(8,128)(2,1)S(1)} all-to-all(bf16[8,72,128]{2,1,0:T(8,128)(2,1)S(1)} %shard_map.107), channel_id=1, replica_groups=mesh['server'=32,'y'=8,'core'=2] {'y'}, dimensions={0} | all-to-all | bytes 294912 | tf_op jit(solution)/shard_map/all_to_all | solution.py:314
  88.2 4.8 %all_gather.7.delta_ref = bf16[16,72,128]{2,1,0:T(8,128)(2,1)S(1)} all-gather(bf16[8,72,128]{2,1,0:T(8,128)(2,1)S(1)} %all_to_all.28), channel_id=1, replica_groups=mesh['server'=32,'y'=8,'core'=2] {'core'}, dimensions={0}, use_global_device_ids=true | all-gather | bytes 442368 | tf_op jit(solution)/shard_map/all_gather | solution.py:374
  93.0 0.9 shard_map.108
Async XLA Ops:
  25.2 4.1 %copy-start = (s32[32,16]{0,1:T(8,128)S(1)}, s32[32,16]{0,1:T(8,128)}, u32[]{:S(2)}) copy-start(s32[32,16]{0,1:T(8,128)} %param.12) | copy-start | bytes 6148
  25.2 4.1 %copy-start.2 = (s32[256,39]{0,1:T(8,128)S(1)}, s32[256,39]{0,1:T(8,128)}, u32[]{:S(2)}) copy-start(s32[256,39]{0,1:T(8,128)} %param.11) | copy-start | bytes 119812
  25.2 4.1 %copy-start.3 = (f32[32,256]{1,0:T(8,128)S(1)}, f32[32,256]{1,0:T(8,128)}, u32[]{:S(2)}) copy-start(f32[32,256]{1,0:T(8,128)} %acc_in.1) | copy-start | bytes 98308
  25.2 13.7 %all-to-all-start.1 = ((bf16[32,16,256]{2,1,0:T(8,128)(2,1)}), bf16[32,16,256]{2,1,0:T(8,128)(2,1)S(1)}, u32[]{:S(2)}, u32[]{:S(2)}) async-start(bf16[32,16,256]{2,1,0:T(8,128)(2,1)} %shard_map.103), calls=%async_computation.1 | async-start | bytes 524288 | tf_op jit(solution)/shard_map/all_to_all | solution.py:314
  29.2 0.7 copy-start.1
  29.2 0.7 copy-start.4
  29.2 0.7 copy-start.5

commit v10 on v9

--- a/solution.py
+++ b/solution.py
@@ -209,30 +209,22 @@
     tails = jnp.concatenate(chunks, axis=1)
     row = iota(tails.shape, 0)
     asked = jnp.sum(jnp.where((row == 2) | (row == 3), tails, 0.0), axis=0, keepdims=True)
-    asked = asked.astype(jnp.int32)
-    ours = jnp.bitwise_and(jnp.right_shift(asked, 5), 1) == core
-    place = jnp.right_shift(asked, 6) * SHARE + jnp.bitwise_and(asked, SHARE - 1)
-    place = jnp.where(ours, place, -1)
-    hot = (iota((ROWS // N_CORE, N_CORE * SLOTS), 0) == place).astype(f32).astype(bf16)
-    left = push_ref[:, :CAP, :].reshape(N_CORE * SLOTS, 128)
-    right = push_ref[:, CAP : 2 * CAP, :].reshape(N_CORE * SLOTS, 128)
-    total = dot(hot, jnp.concatenate([left, right], axis=1)).astype(bf16)
-    out_ref[:, :SHARE, :] = total[:, :128].reshape(N_Y, SHARE, 128)
-    out_ref[:, SHARE : 2 * SHARE, :] = total[:, 128:].reshape(N_Y, SHARE, 128)
+    hot = (iota((ROWS, N_CORE * SLOTS), 0) == asked.astype(jnp.int32)).astype(f32).astype(bf16)
+    half = push_ref[:, pl.ds(pl.multiple_of(core * CAP, CAP), CAP), :].reshape(N_CORE * SLOTS, 128)
+    out_ref[:, :SHARE, :] = dot(hot, half).astype(bf16).reshape(N_WORKER, SHARE, 128)
     linear = dot(jnp.where(row < 2, tails, 0.0).astype(bf16), hot, 1, 1)
-    linear = part_rows(jnp.sum(linear, axis=0, keepdims=True))
-    for y in range(N_Y):
-        lanes = y // 4 * 128
-        turn = lax.rem(N_CORE * y + core + 4 - y % 4, 4) * SHARE
-        out_ref[y, 2 * SHARE :, :] = pltpu.roll(linear[:, lanes : lanes + 128], turn, 1).astype(bf16)
+    linear = part_rows(jnp.sum(linear, axis=0, keepdims=True)).astype(bf16)
+    for w in range(N_WORKER):
+        lanes = w // 4 * 128
+        out_ref[w, SHARE:, :] = linear[:, lanes : lanes + 128]
 
 
 def add_parts(part_ref):
-    total = part_ref[0].astype(f32)
+    left, right = part_ref[0].astype(f32), part_ref[1].astype(f32)
     for y in range(1, N_Y):
-        total = total + part_ref[y].astype(f32)
-    left, right = total[:SHARE], total[SHARE : 2 * SHARE]
-    return left, right, jnp.sum(total[2 * SHARE :], axis=0, keepdims=True)
+        left = left + part_ref[N_CORE * y].astype(f32)
+        right = right + part_ref[N_CORE * y + 1].astype(f32)
+    return left[:SHARE], right[:SHARE], jnp.sum(left[SHARE:], axis=0, keepdims=True)
 
 
 def my_lanes():
@@ -250,10 +242,9 @@
     left = step(left, acc[:, :128]).astype(bf16)
     right = step(right, acc[:, 128:]).astype(bf16)
     linear = part_rows(jnp.where(my_lanes(), step(linear, acc_lin_ref[...]), 0.0)).astype(bf16)
-    for y in range(N_Y):
-        delta_ref[y, :SHARE, :] = left
-        delta_ref[y, SHARE : 2 * SHARE, :] = right
-        delta_ref[y, 2 * SHARE :, :] = linear
+    for w in range(N_WORKER):
+        delta_ref[w, :SHARE, :] = right if w % N_CORE else left
+        delta_ref[w, SHARE:, :] = linear
 
 
 def write_state(part_ref, acc_ref, acc_lin_ref, new_acc_ref, new_acc_lin_ref):
@@ -282,11 +273,12 @@
     for q in range(4):
         lin = jnp.zeros((8, 128), f32)
         for w in range(4 * q, 4 * q + 4):
-            block = delta_ref[w % N_CORE * N_Y + w // N_CORE].astype(f32)
+            block = delta_ref[w].astype(f32)
             here = pl.ds(w * SHARE, SHARE)
             new_factors_ref[here, :128] = factors_ref[here, :128] - block[:SHARE]
-            new_factors_ref[here, 128:] = factors_ref[here, 128:] - block[SHARE : 2 * SHARE]
-            lin = lin + block[2 * SHARE :]
+            other = delta_ref[N_WORKER + w, :SHARE, :].astype(f32)
+            new_factors_ref[here, 128:] = factors_ref[here, 128:] - other
+            lin = lin + block[SHARE:]
         lanes = pl.ds(q * 128, 128)
         new_linear_ref[:, lanes] = linear_ref[:, lanes] - jnp.sum(lin, axis=0, keepdims=True)
 
@@ -314,7 +306,7 @@
     return lax.all_to_all(x, axis, split_axis=0, concat_axis=0, tiled=True)
 
 
-TALL = 2 * SHARE + 8
+TALL = SHARE + 8
 
 
 def body(factors, linear, acc_factors, acc_linear, feature_slot, requests, clicks):
@@ -367,10 +359,10 @@
     )
     pushed = exchange(push, "server")
     pushed = lax.all_gather(pushed, "core", axis=0, tiled=True)
-    dense = call(scatter_kernel, shape((N_Y, TALL, 128), bf16), 1 << 28, pushed)
-    shared = exchange(dense, "y")
-    delta = call(update_kernel, shape((N_Y, TALL, 128), bf16), 1 << 20, shared, acc, acc_lin)
-    deltas = exchange(delta, "y")
+    dense = call(scatter_kernel, shape((N_WORKER, TALL, 128), bf16), 1 << 28, pushed)
+    shared = exchange(dense, ("y", "core"))
+    delta = call(update_kernel, shape((N_WORKER, TALL, 128), bf16), 1 << 20, shared, acc, acc_lin)
+    deltas = exchange(delta, ("y", "core"))
     deltas = lax.all_gather(deltas, "core", axis=0, tiled=True)
     new_factors, new_linear, new_acc, new_acc_lin = call(
         apply_kernel,

time: 94.3 us -> 95.5 us (1.013)
  blocking collectives: 75 us -> 76 us
    all_to_all x4, blocking collectives: 62.8 us -> 66.5 us  [exchange(): return lax.all_to_all(x, axis, split_axis=0, concat_axis=0, tiled=True)]
    all_gather x1, blocking collectives: 4.76 us -> 2.03 us  [body(): deltas = lax.all_gather(deltas, 'core', axis=0, tiled=True)]
where the time goes in v10:
time: 95.5 us; the launch traced here: 95.1 us
  blocking collectives  76 us (80%)
  Pallas kernels  7.6 us (8%)
  waiting for transfers between devices  6.11 us (6%)
  starting transfers between devices  4 us (4%)
    all_to_all x4, blocking collectives, exchange(): return lax.all_to_all(x, axis, split_axis=0, concat_axis=0, tiled=True)  66.5 us
    pallas_call x7, Pallas kernels, call(): pl.pallas_call(kernel, out_shape=out, in_specs=[pl.BlockSpec(memory_space...  7.6 us
    all_gather x1, blocking collectives, body(): pushed = lax.all_gather(pushed, 'core', axis=0, tiled=True)  7.49 us
    all_to_all x1, waiting for transfers between devices, exchange(): return lax.all_to_all(x, axis, split_axis=0, concat_axis=0, tiled=True)  6.11 us
    all_to_all x1, starting transfers between devices, exchange(): return lax.all_to_all(x, axis, split_axis=0, concat_axis=0, tiled=True)  4 us
    all_gather x1, blocking collectives, body(): deltas = lax.all_gather(deltas, 'core', axis=0, tiled=True)  2.03 us
  transfers between devices with their start and end apart: 1, of which 1 were waited for; matrix products, arithmetic and copies ran while one was open for 0% of the time, Pallas kernels for 3%

profile of v10, /device:TPU:1, one launch (start us, length us, event | category | flops | bytes accessed | tf_op | source)
XLA Modules:
  0.0 95.1 jit_solution(6878485472294136117)
XLA Ops:
  0.6 1.1 %shard_map.102 = (bf16[32,8,128]{2,1,0:T(8,128)(2,1)S(1)}, f32[512,256]{1,0:T(8,128)S(1)}) custom-call(s32[16,32]{1,0:T(8,128)} %bitcast.8, f32[4,128]{1,0:T(4,128)} %bitcast.10, f32[512,256]{1,0:T(8,128)} %factors_hbm.1), custom_call_target="tpu_custom_call" | custom-call | flops 1048576 | bytes 528384 | tf_op jit(solution)/shard_map/pallas_call | solution.py:290
  1.7 22.4 %all_to_all.25.got_ref = bf16[32,8,128]{2,1,0:T(8,128)(2,1)S(1)} all-to-all(bf16[32,8,128]{2,1,0:T(8,128)(2,1)S(1)} %get-tuple-element.18), channel_id=1, replica_groups=mesh['server'=32,'y'=8,'core'=2] {'server'}, dimensions={0} | all-to-all | bytes 131072 | tf_op jit(solution)/shard_map/all_to_all | solution.py:306
  24.1 1.1 %shard_map.103 = bf16[32,16,256]{2,1,0:T(8,128)(2,1)} custom-call(bf16[32,8,128]{2,1,0:T(8,128)(2,1)S(1)} %all_to_all.25.got_ref, f32[512,256]{1,0:T(8,128)S(1)} %get-tuple-element.19.factors_ref), custom_call_target="tpu_custom_call" | custom-call | flops 268435456 | bytes 589824 | tf_op jit(solution)/shard_map/pallas_call | solution.py:290
  25.2 0.0 copy-start
  25.2 0.0 copy-start.2
  25.2 0.0 copy-start.3
  25.2 4.0 %all-to-all-start.1 = ((bf16[32,16,256]{2,1,0:T(8,128)(2,1)}), bf16[32,16,256]{2,1,0:T(8,128)(2,1)S(1)}, u32[]{:S(2)}, u32[]{:S(2)}) async-start(bf16[32,16,256]{2,1,0:T(8,128)(2,1)} %shard_map.103), calls=%async_computation.1 | async-start | bytes 524288 | tf_op jit(solution)/shard_map/all_to_all | solution.py:306
  29.2 0.0 copy-start.1
  29.2 0.0 copy-start.4
  29.2 0.0 copy-start.5
  29.2 0.0 copy-done
  29.2 0.0 copy-done.2
  29.2 0.0 copy-done.3
  29.3 0.6 copy-done.1
  29.9 0.0 copy-done.4
  29.9 0.0 copy-done.5
  29.9 2.9 %shard_map.104 = (f32[256,128]{1,0:T(8,128)S(1)}, f32[8,512]{1,0:T(8,128)S(1)}, bf16[512,256]{1,0:T(8,128)(2,1)S(1)}, bf16[256,512]{1,0:T(8,128)(2,1)S(1)}, f32[...) custom-call(bf16[32,8,128]{2,1,0:T(8,128)(2,1)S(1)} %all_to_all.25.got_ref, ...), custom_call_target="tpu_custom_call" | custom-call | flops 1073741824 | bytes 143488 | tf_op jit(solution)/shard_map/pallas_call | solution.py:290
  32.8 6.1 %all-to-all-done.1.rows_ref = bf16[32,16,256]{2,1,0:T(8,128)(2,1)S(1)} async-done(((bf16[32,16,256]{2,1,0:T(8,128)(2,1)}), bf16[32,16,256]{2,1,0:T(8,128)(2,1)S(1)}, u32[]{:S(2)}, u32[]{:S(2)}) %all-to-all-start.1) | async-done | bytes 262176 | tf_op jit(solution)/shard_map/all_to_all | solution.py:306
  38.9 0.9 shard_map.105
  39.8 14.9 %all_to_all.26 = bf16[32,40,128]{2,1,0:T(8,128)(2,1)S(1)} all-to-all(bf16[32,40,128]{2,1,0:T(8,128)(2,1)S(1)} %shard_map.105), channel_id=1, replica_groups=mesh['server'=32,'y'=8,'core'=2] {'server'}, dimensions={0} | all-to-all | bytes 655360 | tf_op jit(solution)/shard_map/all_to_all | solution.py:306
  54.7 7.5 %all_gather.6.push_ref = bf16[64,40,128]{2,1,0:T(8,128)(2,1)S(1)} all-gather(bf16[32,40,128]{2,1,0:T(8,128)(2,1)S(1)} %all_to_all.26), channel_id=1, replica_groups=mesh['server'=32,'y'=8,'core'=2] {'core'}, dimensions={0}, use_global_device_ids=true | all-gather | bytes 983040 | tf_op jit(solution)/shard_map/all_gather | solution.py:361
  62.2 0.7 shard_map.106
  62.9 16.9 %all_to_all.27.part_ref = bf16[16,40,128]{2,1,0:T(8,128)(2,1)S(1)} all-to-all(bf16[16,40,128]{2,1,0:T(8,128)(2,1)S(1)} %shard_map.106), channel_id=1, replica_groups=mesh['server'=32,'y'=8,'core'=2] {'y','core'}, dimensions={0} | all-to-all | bytes 327680 | tf_op jit(solution)/shard_map/all_to_all | solution.py:306
  79.8 0.1 shard_map.107
  79.9 12.3 %all_to_all.28 = bf16[16,40,128]{2,1,0:T(8,128)(2,1)S(1)} all-to-all(bf16[16,40,128]{2,1,0:T(8,128)(2,1)S(1)} %shard_map.107), channel_id=1, replica_groups=mesh['server'=32,'y'=8,'core'=2] {'y','core'}, dimensions={0} | all-to-all | bytes 327680 | tf_op jit(solution)/shard_map/all_to_all | solution.py:306
  92.2 2.0 %all_gather.7.delta_ref = bf16[32,40,128]{2,1,0:T(8,128)(2,1)S(1)} all-gather(bf16[16,40,128]{2,1,0:T(8,128)(2,1)S(1)} %all_to_all.28), channel_id=1, replica_groups=mesh['server'=32,'y'=8,'core'=2] {'core'}, dimensions={0}, use_global_device_ids=true | all-gather | bytes 491520 | tf_op jit(solution)/shard_map/all_gather | solution.py:366
  94.2 0.9 shard_map.108
Async XLA Ops:
  25.2 4.1 %copy-start = (s32[32,16]{0,1:T(8,128)S(1)}, s32[32,16]{0,1:T(8,128)}, u32[]{:S(2)}) copy-start(s32[32,16]{0,1:T(8,128)} %param.12) | copy-start | bytes 6148
  25.2 4.1 %copy-start.2 = (s32[256,39]{0,1:T(8,128)S(1)}, s32[256,39]{0,1:T(8,128)}, u32[]{:S(2)}) copy-start(s32[256,39]{0,1:T(8,128)} %param.11) | copy-start | bytes 119812
  25.2 4.1 %copy-start.3 = (f32[32,256]{1,0:T(8,128)S(1)}, f32[32,256]{1,0:T(8,128)}, u32[]{:S(2)}) copy-start(f32[32,256]{1,0:T(8,128)} %acc_in.1) | copy-start | bytes 98308
  25.2 13.7 %all-to-all-start.1 = ((bf16[32,16,256]{2,1,0:T(8,128)(2,1)}), bf16[32,16,256]{2,1,0:T(8,128)(2,1)S(1)}, u32[]{:S(2)}, u32[]{:S(2)}) async-start(bf16[32,16,256]{2,1,0:T(8,128)(2,1)} %shard_map.103), calls=%async_computation.1 | async-start | bytes 524288 | tf_op jit(solution)/shard_map/all_to_all | solution.py:306
  29.2 0.7 copy-start.1
  29.2 0.7 copy-start.4
  29.2 0.7 copy-start.5

commit v11 on v9

--- a/solution.py
+++ b/solution.py
@@ -60,15 +60,14 @@
     return (iota(dims, axis) < 2 * CAP).astype(f32).astype(bf16)
 
 
-def ask_kernel(req_t_hbm, lin_hbm, factors_hbm, out_ref, factors_ref, req_t_ref, lin_ref, sems):
+def ask_kernel(req_t_hbm, lin_hbm, out_ref, req_t_ref, lin_ref, sems):
     copies = [
         pltpu.make_async_copy(req_t_hbm, req_t_ref, sems.at[0]),
         pltpu.make_async_copy(lin_hbm, lin_ref, sems.at[1]),
-        pltpu.make_async_copy(factors_hbm, factors_ref, sems.at[2]),
     ]
     for copy in copies:
         copy.start()
-    for copy in copies[:2]:
+    for copy in copies:
         copy.wait()
     lists = own_lists(req_t_ref[...], 8)
     spread = (jnp.right_shift(iota((8, 4), 0), 1) == iota((8, 4), 1)).astype(f32).astype(bf16)
@@ -77,29 +76,31 @@
     lin = jnp.where(odd, lin, pltpu.roll(lin, 64, 1))
     lin = jnp.where(iota((8, 128), 1) >= 64, lin, 0.0)
     out_ref[...] = (lists.reshape(OWNERS, 8, 128) + lin[None]).astype(bf16)
-    copies[2].wait()
 
 
 def of_share():
     return jnp.bitwise_and(iota((SHARE, 128), 1), SHARE - 1) == iota((SHARE, 128), 0)
 
 
-def gather_kernel(got_ref, factors_ref, out_ref):
+def gather_kernel(got_ref, narrow_ref, out_ref):
     asked = asked_rows(got_ref[...])
     hot = (asked == iota((SLOTS, ROWS), 1).astype(f32)).astype(f32).astype(bf16)
-    out_ref[...] = dot(hot, factors_ref[...].astype(bf16)).astype(bf16).reshape(OWNERS, CAP, K)
+    out_ref[...] = dot(hot, narrow_ref[...]).astype(bf16).reshape(OWNERS, CAP, K)
 
 
 def side_kernel(
-    got_ref,
     req_t_ref,
+    factors_in,
     fs_t_ref,
     clicks_ref,
     acc_in,
     acc_lin_row_ref,
     linear_in,
-    lin_ref,
+    pick_ref,
+    here_ref,
     ids_ref,
+    narrow_ref,
+    factors_ref,
     counts_t_ref,
     counts_ref,
     clicks_col_ref,
@@ -109,14 +110,15 @@
 ):
     acc_ref[...] = acc_in[...]
     linear_ref[...] = linear_in[...]
-    got = got_ref[...].astype(f32).reshape(8 * OWNERS, 128).astype(bf16)
+    narrow_ref[...] = factors_in[...].astype(bf16)
+    factors_ref[...] = factors_in[...]
     lists = own_lists(req_t_ref[...], CAP).astype(bf16)
     wanted = dot(lists, ones((128, 8 * OWNERS), 0)).astype(jnp.int32)
     first = jnp.right_shift(iota((SLOTS, 8 * OWNERS), 0), 4) * 8
     pick = iota((SLOTS, 8 * OWNERS), 1) == first + jnp.right_shift(wanted, 6)
-    values = dot(pick.astype(f32).astype(bf16), got)
+    pick_ref[...] = pick.astype(f32).astype(bf16)
     here = iota((SLOTS, 128), 1) == jnp.bitwise_and(wanted[:, :128], 63) + 64
-    lin_terms = jnp.where(here, values, 0.0).astype(bf16)
+    here_ref[...] = here.astype(f32)
     spread = jnp.right_shift(iota((OWNERS, SLOTS), 1), 4) == iota((OWNERS, SLOTS), 0)
     lists = dot(split_requests(req_t_ref[...]), spread.astype(f32).astype(bf16))
     place = iota((128, SLOTS), 0)
@@ -140,19 +142,21 @@
         return carry
 
     lax.fori_loop(0, SLOTS // chunk, one, 0)
-    counts = jnp.transpose(counts_t_ref[...].astype(f32)).astype(bf16)
-    counts_ref[...] = counts
-    lin_ref[...] = dot(counts, lin_terms)
+    counts_ref[...] = jnp.transpose(counts_t_ref[...].astype(f32)).astype(bf16)
     same = iota((SAMPLES, SAMPLES), 0) == iota((SAMPLES, SAMPLES), 1)
     clicks = clicks_ref[...].astype(f32)
     clicks_col_ref[...] = jnp.sum(jnp.where(same, clicks, 0.0), axis=1, keepdims=True)
 
 
-def learn_kernel(rows_ref, counts_ref, counts_t_ref, clicks_ref, lin_ref, ids_ref, out_ref):
+def learn_kernel(
+    rows_ref, counts_ref, counts_t_ref, clicks_ref, got_ref, pick_ref, here_ref, ids_ref, out_ref
+):
     rows = rows_ref[...].reshape(SLOTS, K)
     wide_rows = rows.astype(f32)
     counts = counts_ref[...]
     sums = dot(counts, rows)
+    got = got_ref[...].astype(f32).reshape(8 * OWNERS, 128).astype(bf16)
+    linear = dot(counts, (dot(pick_ref[...], got) * here_ref[...]).astype(bf16))
     square = wide_rows * wide_rows
     square = square[:, :128] + square[:, 128:]
     high = square.astype(bf16)
@@ -160,7 +164,7 @@
     middle = rest.astype(bf16)
     low = (rest - middle.astype(f32)).astype(bf16)
     terms = sums * sums - dot(counts, jnp.concatenate([high, middle], axis=1))
-    terms = 0.5 * (terms[:, :128] + terms[:, 128:] - dot(counts, low)) + lin_ref[...]
+    terms = 0.5 * (terms[:, :128] + terms[:, 128:] - dot(counts, low)) + linear
     logits = jnp.sum(terms, axis=1, keepdims=True)
     errors = jnp.broadcast_to(jax.nn.sigmoid(logits) - clicks_ref[...], (SAMPLES, 128))
     first = errors.astype(bf16)
@@ -320,24 +324,24 @@
 def body(factors, linear, acc_factors, acc_linear, feature_slot, requests, clicks):
     dma = pltpu.SemaphoreType.DMA
     req_t = requests.T
-    ask, wide = call(
+    ask = call(
         ask_kernel,
-        [shape((OWNERS, 8, 128), bf16), shape((ROWS, K), f32)],
+        shape((OWNERS, 8, 128), bf16),
         1 << 20,
         req_t,
         linear.reshape(4, 128),
-        factors,
-        scratch=[pltpu.VMEM((CAP, OWNERS), jnp.int32), pltpu.VMEM((4, 128), f32), dma((3,))],
+        scratch=[pltpu.VMEM((CAP, OWNERS), jnp.int32), pltpu.VMEM((4, 128), f32), dma((2,))],
         far=True,
     )
     got = exchange(ask, "server")
-    found = call(gather_kernel, shape((OWNERS, CAP, K), bf16), 1 << 28, got, wide)
-    rows = exchange(found, "server")
-    lin_terms, ids, counts_t, counts, clicks_col, acc, acc_lin, lin_row = call(
+    pick, here, ids, narrow, wide, counts_t, counts, clicks_col, acc, acc_lin, lin_row = call(
         side_kernel,
         [
-            shape((SAMPLES, 128), f32),
+            shape((SLOTS, 8 * OWNERS), bf16),
+            shape((SLOTS, 128), f32),
             shape((8, SLOTS), f32),
+            shape((ROWS, K), bf16),
+            shape((ROWS, K), f32),
             shape((SLOTS, SAMPLES), bf16),
             shape((SAMPLES, SLOTS), bf16),
             shape((SAMPLES, 1), f32),
@@ -346,14 +350,16 @@
             shape((1, ROWS), f32),
         ],
         1 << 30,
-        got,
         req_t,
+        factors,
         feature_slot.T,
         clicks.reshape(1, SAMPLES),
         acc_factors,
         acc_linear.reshape(1, SHARE),
         linear.reshape(1, ROWS),
     )
+    found = call(gather_kernel, shape((OWNERS, CAP, K), bf16), 1 << 28, got, narrow)
+    rows = exchange(found, "server")
     push = call(
         learn_kernel,
         shape((OWNERS, 2 * CAP + 8, 128), bf16),
@@ -362,7 +368,9 @@
         counts,
         counts_t,
         clicks_col,
-        lin_terms,
+        got,
+        pick,
+        here,
         ids,
     )
     pushed = exchange(push, "server")

time: 94.3 us -> 95.4 us (1.012)
  starting transfers between devices: 4 us -> 13.9 us
  blocking collectives: 75 us -> 67 us
  waiting for transfers between devices: 6.11 us -> 4.34 us
  local copies, waits for them, and re-layouts: 0.66 us -> 1.71 us
    all_to_all x1, starting transfers between devices: 4 us -> 13.9 us  [exchange(): return lax.all_to_all(x, axis, split_axis=0, concat_axis=0, tiled=True)]
    all_to_all x4, blocking collectives: 62.8 us -> 55.8 us  [exchange(): return lax.all_to_all(x, axis, split_axis=0, concat_axis=0, tiled=True)]
    all_to_all x1, waiting for transfers between devices: 6.11 us -> 4.34 us  [exchange(): return lax.all_to_all(x, axis, split_axis=0, concat_axis=0, tiled=True)]
    all_gather x1, blocking collectives: 7.49 us -> 6.38 us  [body(): pushed = lax.all_gather(pushed, 'core', axis=0, tiled=True)]
    unnamed x12 -> x14, local copies, waits for them, and re-layouts: 0.66 us -> 1.71 us
where the time goes in v11:
time: 95.4 us; the launch traced here: 94.9 us
  blocking collectives  67 us (70%)
  starting transfers between devices  13.9 us (15%)
  Pallas kernels  7.28 us (8%)
  waiting for transfers between devices  4.34 us (5%)
  local copies, waits for them, and re-layouts  1.71 us (2%)
    all_to_all x4, blocking collectives, exchange(): return lax.all_to_all(x, axis, split_axis=0, concat_axis=0, tiled=True)  55.8 us
    all_to_all x1, starting transfers between devices, exchange(): return lax.all_to_all(x, axis, split_axis=0, concat_axis=0, tiled=True)  13.9 us
    pallas_call x7, Pallas kernels, call(): pl.pallas_call(kernel, out_shape=out, in_specs=[pl.BlockSpec(memory_space...  7.28 us
    all_gather x1, blocking collectives, body(): pushed = lax.all_gather(pushed, 'core', axis=0, tiled=True)  6.38 us
    all_gather x1, blocking collectives, body(): deltas = lax.all_gather(deltas, 'core', axis=0, tiled=True)  4.76 us
    all_to_all x1, waiting for transfers between devices, exchange(): return lax.all_to_all(x, axis, split_axis=0, concat_axis=0, tiled=True)  4.34 us
  transfers between devices with their start and end apart: 1, of which 1 were waited for; matrix products, arithmetic and copies ran while one was open for 0% of the time, Pallas kernels for 3%

profile of v11, /device:TPU:1, one launch (start us, length us, event | category | flops | bytes accessed | tf_op | source)
XLA Modules:
  0.0 94.9 jit_solution(17127761385038497274)
XLA Ops:
  0.6 1.6 %shard_map.102 = bf16[32,8,128]{2,1,0:T(8,128)(2,1)} custom-call(s32[16,32]{1,0:T(8,128)} %bitcast.8, f32[4,128]{1,0:T(4,128)} %bitcast.10), custom_call_target="tpu_custom_call" | custom-call | flops 1048576 | bytes 4096 | tf_op jit(solution)/shard_map/pallas_call | solution.py:302
  2.2 0.0 copy-start
  2.2 0.0 copy-start.3
  2.2 0.0 copy-start.4
  2.2 13.9 %all-to-all-start = ((bf16[32,8,128]{2,1,0:T(8,128)(2,1)}), bf16[32,8,128]{2,1,0:T(8,128)(2,1)S(1)}, u32[]{:S(2)}, u32[]{:S(2)}) async-start(bf16[32,8,128]{2,1,0:T(8,128)(2,1)} %shard_map.102), calls=%async_computation | async-start | bytes 131072 | tf_op jit(solution)/shard_map/all_to_all | solution.py:318
  16.1 0.0 copy-start.1
  16.1 0.0 copy-start.5
  16.1 0.0 copy-start.6
  16.2 0.0 copy-done
  16.2 0.0 copy-done.3
  16.2 0.0 copy-done.4
  16.2 0.6 copy-done.1
  16.8 0.0 copy-done.5
  16.8 0.0 copy-done.6
  16.8 0.0 copy-start.2
  16.8 1.0 %copy-done.2 = f32[512,256]{1,0:T(8,128)S(1)} copy-done((f32[512,256]{1,0:T(8,128)S(1)}, f32[512,256]{1,0:T(8,128)}, u32[]{:S(2)}) %copy-start.2) | copy-done | bytes 524312
  17.9 2.8 %shard_map.103 = (bf16[512,256]{1,0:T(8,128)(2,1)S(1)}, f32[512,128]{1,0:T(8,128)S(1)}, f32[8,512]{1,0:T(8,128)S(1)}, bf16[512,256]{1,0:T(8,128)(2,1)S(1)}, f32[...) custom-call(s32[16,32]{1,0:T(8,128)S(1)} %bitcast.9, ...), custom_call_target="tpu_custom_call" | custom-call | flops 1073741824 | bytes 602240 | tf_op jit(solution)/shard_map/pallas_call | solution.py:302
  20.6 4.3 %all-to-all-done.got_ref = bf16[32,8,128]{2,1,0:T(8,128)(2,1)S(1)} async-done(((bf16[32,8,128]{2,1,0:T(8,128)(2,1)}), bf16[32,8,128]{2,1,0:T(8,128)(2,1)S(1)}, u32[]{:S(2)}, u32[]{:S(2)}) %all-to-all-start) | async-done | bytes 65568 | tf_op jit(solution)/shard_map/all_to_all | solution.py:318
  25.0 0.4 shard_map.104
  25.3 14.4 %all_to_all.25.rows_ref = bf16[32,16,256]{2,1,0:T(8,128)(2,1)S(1)} all-to-all(bf16[32,16,256]{2,1,0:T(8,128)(2,1)S(1)} %shard_map.104), channel_id=1, replica_groups=mesh['server'=32,'y'=8,'core'=2] {'server'}, dimensions={0} | all-to-all | bytes 524288 | tf_op jit(solution)/shard_map/all_to_all | solution.py:318
  39.7 1.1 %shard_map.105 = bf16[32,40,128]{2,1,0:T(8,128)(2,1)S(1)} custom-call(bf16[32,16,256]{2,1,0:T(8,128)(2,1)S(1)} %all_to_all.25.rows_ref, bf16[256,512]{1,0:T(8,128)(2,1)S(1)} %get-tuple-element.20.counts_ref, bf16[512,256]{1,0:T(8,128)(2,1)S(1)} %get-tuple-element.21.counts_t_ref, f32[256,1]{1,0:T(8,128)S(1)} %get-tuple-element.22.clicks_ref, ...), custom_call_target="tpu_custom_call" | custom-call | flops 268435456 | bytes 1393664 | tf_op jit(solution)/shard_map/pallas_call | solution.py:302
  40.8 15.9 %all_to_all.26 = bf16[32,40,128]{2,1,0:T(8,128)(2,1)S(1)} all-to-all(bf16[32,40,128]{2,1,0:T(8,128)(2,1)S(1)} %shard_map.105), channel_id=1, replica_groups=mesh['server'=32,'y'=8,'core'=2] {'server'}, dimensions={0} | all-to-all | bytes 655360 | tf_op jit(solution)/shard_map/all_to_all | solution.py:318
  56.8 6.4 %all_gather.6.push_ref = bf16[64,40,128]{2,1,0:T(8,128)(2,1)S(1)} all-gather(bf16[32,40,128]{2,1,0:T(8,128)(2,1)S(1)} %all_to_all.26), channel_id=1, replica_groups=mesh['server'=32,'y'=8,'core'=2] {'core'}, dimensions={0}, use_global_device_ids=true | all-gather | bytes 983040 | tf_op jit(solution)/shard_map/all_gather | solution.py:377
  63.2 0.5 shard_map.106
  63.7 14.9 %all_to_all.27.part_ref = bf16[8,72,128]{2,1,0:T(8,128)(2,1)S(1)} all-to-all(bf16[8,72,128]{2,1,0:T(8,128)(2,1)S(1)} %shard_map.106), channel_id=1, replica_groups=mesh['server'=32,'y'=8,'core'=2] {'y'}, dimensions={0} | all-to-all | bytes 294912 | tf_op jit(solution)/shard_map/all_to_all | solution.py:318
  78.6 0.1 shard_map.107
  78.6 10.6 %all_to_all.28 = bf16[8,72,128]{2,1,0:T(8,128)(2,1)S(1)} all-to-all(bf16[8,72,128]{2,1,0:T(8,128)(2,1)S(1)} %shard_map.107), channel_id=1, replica_groups=mesh['server'=32,'y'=8,'core'=2] {'y'}, dimensions={0} | all-to-all | bytes 294912 | tf_op jit(solution)/shard_map/all_to_all | solution.py:318
  89.2 4.8 %all_gather.7.delta_ref = bf16[16,72,128]{2,1,0:T(8,128)(2,1)S(1)} all-gather(bf16[8,72,128]{2,1,0:T(8,128)(2,1)S(1)} %all_to_all.28), channel_id=1, replica_groups=mesh['server'=32,'y'=8,'core'=2] {'core'}, dimensions={0}, use_global_device_ids=true | all-gather | bytes 442368 | tf_op jit(solution)/shard_map/all_gather | solution.py:382
  94.0 0.9 shard_map.108
Async XLA Ops:
  2.2 13.9 %copy-start = (s32[32,16]{0,1:T(8,128)S(1)}, s32[32,16]{0,1:T(8,128)}, u32[]{:S(2)}) copy-start(s32[32,16]{0,1:T(8,128)} %param.12) | copy-start | bytes 6148
  2.2 13.9 %copy-start.3 = (s32[256,39]{0,1:T(8,128)S(1)}, s32[256,39]{0,1:T(8,128)}, u32[]{:S(2)}) copy-start(s32[256,39]{0,1:T(8,128)} %param.11) | copy-start | bytes 119812
  2.2 13.9 %copy-start.4 = (f32[32,256]{1,0:T(8,128)S(1)}, f32[32,256]{1,0:T(8,128)}, u32[]{:S(2)}) copy-start(f32[32,256]{1,0:T(8,128)} %acc_in.1) | copy-start | bytes 98308
  2.2 22.7 %all-to-all-start = ((bf16[32,8,128]{2,1,0:T(8,128)(2,1)}), bf16[32,8,128]{2,1,0:T(8,128)(2,1)S(1)}, u32[]{:S(2)}, u32[]{:S(2)}) async-start(bf16[32,8,128]{2,1,0:T(8,128)(2,1)} %shard_map.102), calls=%async_computation | async-start | bytes 131072 | tf_op jit(solution)/shard_map/all_to_all | solution.py:318
  16.1 0.7 copy-start.1
  16.1 0.7 copy-start.5
  16.1 0.7 copy-start.6
  16.8 1.0 %copy-start.2 = (f32[512,256]{1,0:T(8,128)S(1)}, f32[512,256]{1,0:T(8,128)}, u32[]{:S(2)}) copy-start(f32[512,256]{1,0:T(8,128)} %factors_in.1) | copy-start | bytes 1572868

commit v12 on v9

--- a/solution.py
+++ b/solution.py
@@ -66,7 +66,7 @@
         pltpu.make_async_copy(lin_hbm, lin_ref, sems.at[1]),
         pltpu.make_async_copy(factors_hbm, factors_ref, sems.at[2]),
     ]
-    for copy in copies:
+    for copy in copies[::-1]:
         copy.start()
     for copy in copies[:2]:
         copy.wait()

time: 94.3 us -> 94.4 us (level)
  no operation moved by 1% of the time
where the time goes in v12:
time: 94.4 us; the launch traced here: 93.9 us
  blocking collectives  75 us (79%)
  Pallas kernels  7.41 us (8%)
  waiting for transfers between devices  6.11 us (6%)
  starting transfers between devices  4 us (4%)
    all_to_all x4, blocking collectives, exchange(): return lax.all_to_all(x, axis, split_axis=0, concat_axis=0, tiled=True)  62.8 us
    all_gather x1, blocking collectives, body(): pushed = lax.all_gather(pushed, 'core', axis=0, tiled=True)  7.49 us
    pallas_call x7, Pallas kernels, call(): pl.pallas_call(kernel, out_shape=out, in_specs=[pl.BlockSpec(memory_space...  7.41 us
    all_to_all x1, waiting for transfers between devices, exchange(): return lax.all_to_all(x, axis, split_axis=0, concat_axis=0, tiled=True)  6.11 us
    all_gather x1, blocking collectives, body(): deltas = lax.all_gather(deltas, 'core', axis=0, tiled=True)  4.76 us
    all_to_all x1, starting transfers between devices, exchange(): return lax.all_to_all(x, axis, split_axis=0, concat_axis=0, tiled=True)  4 us
  transfers between devices with their start and end apart: 1, of which 1 were waited for; matrix products, arithmetic and copies ran while one was open for 0% of the time, Pallas kernels for 3%

profile of v12, /device:TPU:1, one launch (start us, length us, event | category | flops | bytes accessed | tf_op | source)
XLA Modules:
  0.0 93.9 jit_solution(10541096153609761395)
XLA Ops:
  0.6 1.1 %shard_map.102 = (bf16[32,8,128]{2,1,0:T(8,128)(2,1)S(1)}, f32[512,256]{1,0:T(8,128)S(1)}) custom-call(s32[16,32]{1,0:T(8,128)} %bitcast.8, f32[4,128]{1,0:T(4,128)} %bitcast.10, f32[512,256]{1,0:T(8,128)} %factors_hbm.1), custom_call_target="tpu_custom_call" | custom-call | flops 1048576 | bytes 528384 | tf_op jit(solution)/shard_map/pallas_call | solution.py:298
  1.8 22.4 %all_to_all.25.got_ref = bf16[32,8,128]{2,1,0:T(8,128)(2,1)S(1)} all-to-all(bf16[32,8,128]{2,1,0:T(8,128)(2,1)S(1)} %get-tuple-element.18), channel_id=1, replica_groups=mesh['server'=32,'y'=8,'core'=2] {'server'}, dimensions={0} | all-to-all | bytes 131072 | tf_op jit(solution)/shard_map/all_to_all | solution.py:314
  24.1 1.1 %shard_map.103 = bf16[32,16,256]{2,1,0:T(8,128)(2,1)} custom-call(bf16[32,8,128]{2,1,0:T(8,128)(2,1)S(1)} %all_to_all.25.got_ref, f32[512,256]{1,0:T(8,128)S(1)} %get-tuple-element.19.factors_ref), custom_call_target="tpu_custom_call" | custom-call | flops 268435456 | bytes 589824 | tf_op jit(solution)/shard_map/pallas_call | solution.py:298
  25.2 0.0 copy-start
  25.2 0.0 copy-start.2
  25.2 0.0 copy-start.3
  25.2 4.0 %all-to-all-start.1 = ((bf16[32,16,256]{2,1,0:T(8,128)(2,1)}), bf16[32,16,256]{2,1,0:T(8,128)(2,1)S(1)}, u32[]{:S(2)}, u32[]{:S(2)}) async-start(bf16[32,16,256]{2,1,0:T(8,128)(2,1)} %shard_map.103), calls=%async_computation.1 | async-start | bytes 524288 | tf_op jit(solution)/shard_map/all_to_all | solution.py:314
  29.2 0.0 copy-start.1
  29.2 0.0 copy-start.4
  29.2 0.0 copy-start.5
  29.2 0.0 copy-done
  29.3 0.0 copy-done.2
  29.3 0.0 copy-done.3
  29.3 0.6 copy-done.1
  29.9 0.0 copy-done.4
  29.9 0.0 copy-done.5
  29.9 2.9 %shard_map.104 = (f32[256,128]{1,0:T(8,128)S(1)}, f32[8,512]{1,0:T(8,128)S(1)}, bf16[512,256]{1,0:T(8,128)(2,1)S(1)}, bf16[256,512]{1,0:T(8,128)(2,1)S(1)}, f32[...) custom-call(bf16[32,8,128]{2,1,0:T(8,128)(2,1)S(1)} %all_to_all.25.got_ref, ...), custom_call_target="tpu_custom_call" | custom-call | flops 1073741824 | bytes 143488 | tf_op jit(solution)/shard_map/pallas_call | solution.py:298
  32.8 6.1 %all-to-all-done.1.rows_ref = bf16[32,16,256]{2,1,0:T(8,128)(2,1)S(1)} async-done(((bf16[32,16,256]{2,1,0:T(8,128)(2,1)}), bf16[32,16,256]{2,1,0:T(8,128)(2,1)S(1)}, u32[]{:S(2)}, u32[]{:S(2)}) %all-to-all-start.1) | async-done | bytes 262176 | tf_op jit(solution)/shard_map/all_to_all | solution.py:314
  38.9 0.9 shard_map.105
  39.8 14.9 %all_to_all.26 = bf16[32,40,128]{2,1,0:T(8,128)(2,1)S(1)} all-to-all(bf16[32,40,128]{2,1,0:T(8,128)(2,1)S(1)} %shard_map.105), channel_id=1, replica_groups=mesh['server'=32,'y'=8,'core'=2] {'server'}, dimensions={0} | all-to-all | bytes 655360 | tf_op jit(solution)/shard_map/all_to_all | solution.py:314
  54.7 7.5 %all_gather.6.push_ref = bf16[64,40,128]{2,1,0:T(8,128)(2,1)S(1)} all-gather(bf16[32,40,128]{2,1,0:T(8,128)(2,1)S(1)} %all_to_all.26), channel_id=1, replica_groups=mesh['server'=32,'y'=8,'core'=2] {'core'}, dimensions={0}, use_global_device_ids=true | all-gather | bytes 983040 | tf_op jit(solution)/shard_map/all_gather | solution.py:369
  62.2 0.5 shard_map.106
  62.7 14.9 %all_to_all.27.part_ref = bf16[8,72,128]{2,1,0:T(8,128)(2,1)S(1)} all-to-all(bf16[8,72,128]{2,1,0:T(8,128)(2,1)S(1)} %shard_map.106), channel_id=1, replica_groups=mesh['server'=32,'y'=8,'core'=2] {'y'}, dimensions={0} | all-to-all | bytes 294912 | tf_op jit(solution)/shard_map/all_to_all | solution.py:314
  77.6 0.1 shard_map.107
  77.7 10.6 %all_to_all.28 = bf16[8,72,128]{2,1,0:T(8,128)(2,1)S(1)} all-to-all(bf16[8,72,128]{2,1,0:T(8,128)(2,1)S(1)} %shard_map.107), channel_id=1, replica_groups=mesh['server'=32,'y'=8,'core'=2] {'y'}, dimensions={0} | all-to-all | bytes 294912 | tf_op jit(solution)/shard_map/all_to_all | solution.py:314
  88.3 4.8 %all_gather.7.delta_ref = bf16[16,72,128]{2,1,0:T(8,128)(2,1)S(1)} all-gather(bf16[8,72,128]{2,1,0:T(8,128)(2,1)S(1)} %all_to_all.28), channel_id=1, replica_groups=mesh['server'=32,'y'=8,'core'=2] {'core'}, dimensions={0}, use_global_device_ids=true | all-gather | bytes 442368 | tf_op jit(solution)/shard_map/all_gather | solution.py:374
  93.0 0.9 shard_map.108
Async XLA Ops:
  25.2 4.1 %copy-start = (s32[32,16]{0,1:T(8,128)S(1)}, s32[32,16]{0,1:T(8,128)}, u32[]{:S(2)}) copy-start(s32[32,16]{0,1:T(8,128)} %param.12) | copy-start | bytes 6148
  25.2 4.1 %copy-start.2 = (s32[256,39]{0,1:T(8,128)S(1)}, s32[256,39]{0,1:T(8,128)}, u32[]{:S(2)}) copy-start(s32[256,39]{0,1:T(8,128)} %param.11) | copy-start | bytes 119812
  25.2 4.1 %copy-start.3 = (f32[32,256]{1,0:T(8,128)S(1)}, f32[32,256]{1,0:T(8,128)}, u32[]{:S(2)}) copy-start(f32[32,256]{1,0:T(8,128)} %acc_in.1) | copy-start | bytes 98308
  25.2 13.7 %all-to-all-start.1 = ((bf16[32,16,256]{2,1,0:T(8,128)(2,1)}), bf16[32,16,256]{2,1,0:T(8,128)(2,1)S(1)}, u32[]{:S(2)}, u32[]{:S(2)}) async-start(bf16[32,16,256]{2,1,0:T(8,128)(2,1)} %shard_map.103), calls=%async_computation.1 | async-start | bytes 524288 | tf_op jit(solution)/shard_map/all_to_all | solution.py:314
  29.2 0.7 copy-start.1
  29.2 0.7 copy-start.4
  29.2 0.7 copy-start.5

commit v13 on v9

--- a/solution.py
+++ b/solution.py
@@ -202,10 +202,10 @@
     core = lax.axis_index("core")
     chunks = []
     for q in range(N_CORE * OWNERS // 8):
-        chunk = push_ref[8 * q, 2 * CAP :, :].astype(f32)
+        chunk = push_ref[8 * q, 2 * CAP :, :]
         for i in range(1, 8):
-            chunk = chunk + push_ref[8 * q + i, 2 * CAP :, :].astype(f32)
-        chunks.append(chunk)
+            chunk = chunk + push_ref[8 * q + i, 2 * CAP :, :]
+        chunks.append(chunk.astype(f32))
     tails = jnp.concatenate(chunks, axis=1)
     row = iota(tails.shape, 0)
     asked = jnp.sum(jnp.where((row == 2) | (row == 3), tails, 0.0), axis=0, keepdims=True)

time: 94.3 us -> 94.3 us (level)
  no operation moved by 1% of the time
where the time goes in v13:
time: 94.3 us; the launch traced here: 93.9 us
  blocking collectives  75 us (80%)
  Pallas kernels  7.39 us (8%)
  waiting for transfers between devices  6.11 us (6%)
  starting transfers between devices  4 us (4%)
    all_to_all x4, blocking collectives, exchange(): return lax.all_to_all(x, axis, split_axis=0, concat_axis=0, tiled=True)  62.8 us
    all_gather x1, blocking collectives, body(): pushed = lax.all_gather(pushed, 'core', axis=0, tiled=True)  7.49 us
    pallas_call x7, Pallas kernels, call(): pl.pallas_call(kernel, out_shape=out, in_specs=[pl.BlockSpec(memory_space...  7.39 us
    all_to_all x1, waiting for transfers between devices, exchange(): return lax.all_to_all(x, axis, split_axis=0, concat_axis=0, tiled=True)  6.11 us
    all_gather x1, blocking collectives, body(): deltas = lax.all_gather(deltas, 'core', axis=0, tiled=True)  4.76 us
    all_to_all x1, starting transfers between devices, exchange(): return lax.all_to_all(x, axis, split_axis=0, concat_axis=0, tiled=True)  4 us
  transfers between devices with their start and end apart: 1, of which 1 were waited for; matrix products, arithmetic and copies ran while one was open for 0% of the time, Pallas kernels for 3%

profile of v13, /device:TPU:1, one launch (start us, length us, event | category | flops | bytes accessed | tf_op | source)
XLA Modules:
  0.0 93.9 jit_solution(1422555925354841841)
XLA Ops:
  0.6 1.1 %shard_map.102 = (bf16[32,8,128]{2,1,0:T(8,128)(2,1)S(1)}, f32[512,256]{1,0:T(8,128)S(1)}) custom-call(s32[16,32]{1,0:T(8,128)} %bitcast.8, f32[4,128]{1,0:T(4,128)} %bitcast.10, f32[512,256]{1,0:T(8,128)} %factors_hbm.1), custom_call_target="tpu_custom_call" | custom-call | flops 1048576 | bytes 528384 | tf_op jit(solution)/shard_map/pallas_call | solution.py:298
  1.7 22.4 %all_to_all.25.got_ref = bf16[32,8,128]{2,1,0:T(8,128)(2,1)S(1)} all-to-all(bf16[32,8,128]{2,1,0:T(8,128)(2,1)S(1)} %get-tuple-element.18), channel_id=1, replica_groups=mesh['server'=32,'y'=8,'core'=2] {'server'}, dimensions={0} | all-to-all | bytes 131072 | tf_op jit(solution)/shard_map/all_to_all | solution.py:314
  24.1 1.1 %shard_map.103 = bf16[32,16,256]{2,1,0:T(8,128)(2,1)} custom-call(bf16[32,8,128]{2,1,0:T(8,128)(2,1)S(1)} %all_to_all.25.got_ref, f32[512,256]{1,0:T(8,128)S(1)} %get-tuple-element.19.factors_ref), custom_call_target="tpu_custom_call" | custom-call | flops 268435456 | bytes 589824 | tf_op jit(solution)/shard_map/pallas_call | solution.py:298
  25.2 0.0 copy-start
  25.2 0.0 copy-start.2
  25.2 0.0 copy-start.3
  25.2 4.0 %all-to-all-start.1 = ((bf16[32,16,256]{2,1,0:T(8,128)(2,1)}), bf16[32,16,256]{2,1,0:T(8,128)(2,1)S(1)}, u32[]{:S(2)}, u32[]{:S(2)}) async-start(bf16[32,16,256]{2,1,0:T(8,128)(2,1)} %shard_map.103), calls=%async_computation.1 | async-start | bytes 524288 | tf_op jit(solution)/shard_map/all_to_all | solution.py:314
  29.2 0.0 copy-start.1
  29.2 0.0 copy-start.4
  29.2 0.0 copy-start.5
  29.2 0.0 copy-done
  29.2 0.0 copy-done.2
  29.2 0.0 copy-done.3
  29.3 0.6 copy-done.1
  29.9 0.0 copy-done.4
  29.9 0.0 copy-done.5
  29.9 2.9 %shard_map.104 = (f32[256,128]{1,0:T(8,128)S(1)}, f32[8,512]{1,0:T(8,128)S(1)}, bf16[512,256]{1,0:T(8,128)(2,1)S(1)}, bf16[256,512]{1,0:T(8,128)(2,1)S(1)}, f32[...) custom-call(bf16[32,8,128]{2,1,0:T(8,128)(2,1)S(1)} %all_to_all.25.got_ref, ...), custom_call_target="tpu_custom_call" | custom-call | flops 1073741824 | bytes 143488 | tf_op jit(solution)/shard_map/pallas_call | solution.py:298
  32.8 6.1 %all-to-all-done.1.rows_ref = bf16[32,16,256]{2,1,0:T(8,128)(2,1)S(1)} async-done(((bf16[32,16,256]{2,1,0:T(8,128)(2,1)}), bf16[32,16,256]{2,1,0:T(8,128)(2,1)S(1)}, u32[]{:S(2)}, u32[]{:S(2)}) %all-to-all-start.1) | async-done | bytes 262176 | tf_op jit(solution)/shard_map/all_to_all | solution.py:314
  38.9 0.9 shard_map.105
  39.8 14.9 %all_to_all.26 = bf16[32,40,128]{2,1,0:T(8,128)(2,1)S(1)} all-to-all(bf16[32,40,128]{2,1,0:T(8,128)(2,1)S(1)} %shard_map.105), channel_id=1, replica_groups=mesh['server'=32,'y'=8,'core'=2] {'server'}, dimensions={0} | all-to-all | bytes 655360 | tf_op jit(solution)/shard_map/all_to_all | solution.py:314
  54.7 7.5 %all_gather.6.push_ref = bf16[64,40,128]{2,1,0:T(8,128)(2,1)S(1)} all-gather(bf16[32,40,128]{2,1,0:T(8,128)(2,1)S(1)} %all_to_all.26), channel_id=1, replica_groups=mesh['server'=32,'y'=8,'core'=2] {'core'}, dimensions={0}, use_global_device_ids=true | all-gather | bytes 983040 | tf_op jit(solution)/shard_map/all_gather | solution.py:369
  62.2 0.5 shard_map.106
  62.7 14.9 %all_to_all.27.part_ref = bf16[8,72,128]{2,1,0:T(8,128)(2,1)S(1)} all-to-all(bf16[8,72,128]{2,1,0:T(8,128)(2,1)S(1)} %shard_map.106), channel_id=1, replica_groups=mesh['server'=32,'y'=8,'core'=2] {'y'}, dimensions={0} | all-to-all | bytes 294912 | tf_op jit(solution)/shard_map/all_to_all | solution.py:314
  77.6 0.1 shard_map.107
  77.7 10.6 %all_to_all.28 = bf16[8,72,128]{2,1,0:T(8,128)(2,1)S(1)} all-to-all(bf16[8,72,128]{2,1,0:T(8,128)(2,1)S(1)} %shard_map.107), channel_id=1, replica_groups=mesh['server'=32,'y'=8,'core'=2] {'y'}, dimensions={0} | all-to-all | bytes 294912 | tf_op jit(solution)/shard_map/all_to_all | solution.py:314
  88.2 4.8 %all_gather.7.delta_ref = bf16[16,72,128]{2,1,0:T(8,128)(2,1)S(1)} all-gather(bf16[8,72,128]{2,1,0:T(8,128)(2,1)S(1)} %all_to_all.28), channel_id=1, replica_groups=mesh['server'=32,'y'=8,'core'=2] {'core'}, dimensions={0}, use_global_device_ids=true | all-gather | bytes 442368 | tf_op jit(solution)/shard_map/all_gather | solution.py:374
  93.0 0.9 shard_map.108
Async XLA Ops:
  25.2 4.1 %copy-start = (s32[32,16]{0,1:T(8,128)S(1)}, s32[32,16]{0,1:T(8,128)}, u32[]{:S(2)}) copy-start(s32[32,16]{0,1:T(8,128)} %param.12) | copy-start | bytes 6148
  25.2 4.1 %copy-start.2 = (s32[256,39]{0,1:T(8,128)S(1)}, s32[256,39]{0,1:T(8,128)}, u32[]{:S(2)}) copy-start(s32[256,39]{0,1:T(8,128)} %param.11) | copy-start | bytes 119812
  25.2 4.1 %copy-start.3 = (f32[32,256]{1,0:T(8,128)S(1)}, f32[32,256]{1,0:T(8,128)}, u32[]{:S(2)}) copy-start(f32[32,256]{1,0:T(8,128)} %acc_in.1) | copy-start | bytes 98308
  25.2 13.7 %all-to-all-start.1 = ((bf16[32,16,256]{2,1,0:T(8,128)(2,1)}), bf16[32,16,256]{2,1,0:T(8,128)(2,1)S(1)}, u32[]{:S(2)}, u32[]{:S(2)}) async-start(bf16[32,16,256]{2,1,0:T(8,128)(2,1)} %shard_map.103), calls=%async_computation.1 | async-start | bytes 524288 | tf_op jit(solution)/shard_map/all_to_all | solution.py:314
  29.2 0.7 copy-start.1
  29.2 0.7 copy-start.4
  29.2 0.7 copy-start.5
